TPU v7x, 32 devices: a whole 2x2x4 slice. The times are simulated.
32 devices in a mesh: groups: 2 (over y), side: 8 (over z, x), tp: 2 (over core).
Axes of the slice: x: 2, y: 2, z: 4, core: 2. Of those that a mesh axis runs over, the one named last changes fastest.
Arguments:
- residual: bfloat16 [2, 32, 3072], P(None, ('groups', 'side'), 'tp'), parts along dimension 1, may hold values from -5 to 5
- queries: bfloat16 [2, 32, 3072], P(None, ('groups', 'side'), 'tp'), parts along dimension 1, may hold values from -24 to 24
- key_cache: bfloat16 [128, 16, 512], P(('groups', 'side'), None, 'tp'), parts along dimension 0, may hold values from -6 to 6
- value_cache: bfloat16 [128, 16, 512], P(('groups', 'side'), None, 'tp'), parts along dimension 0, may hold values from -6 to 6
- page_table: int32 [2, 32, 2], P(None, ('groups', 'side')), parts along dimension 1, may hold values from 0 to 7, as said below
- lengths: int32 [2, 32], P(None, ('groups', 'side')), parts along dimension 1, may hold values from 2 to 32, as said below
- routes: int32 [2, 32, 2], P(None, ('groups', 'side')), parts along dimension 1, may hold values from 0 to 3, all different within a row; in each aligned block of 2 rows (0 to 1, 2 to 3, ..., all dimensions but the last counted through in order) at most 2 rows name the same one
- gate_fixed: int32 [2, 32], P(None, ('groups', 'side')), parts along dimension 1, may hold values from 6554 to 58981
- norm_gain: bfloat16 [3072], replicated, may hold values from 0.099609375 to 1.8984375
- w_gate: bfloat16 [3072, 65536], P(None, ('side', 'tp')), may hold values from -0.109375 to 0.109375
- w_up: bfloat16 [3072, 65536], P(None, ('side', 'tp')), may hold values from -0.109375 to 0.109375
- w_down: bfloat16 [65536, 3072], P('side', 'tp'), may hold values from -0.046875 to 0.046875
Outputs:
- layer_out: bfloat16 [2, 32, 3072], P(None, ('groups', 'side'), 'tp'), parts along dimension 1
There are 2 independent parts, one for each index of `groups`. A program takes and returns all parts, laid end to end along the dimension named above; an argument that names none is the same for every part. Nothing has to cross between parts.
Inputs may be any that keep to these rules, and one draw needn't show every extreme that they name: `page_table`: on each index of side, the 2 x 2 x 2 entries of its requests are a permutation of its 8 pages. `lengths`: positions of a request's cache, its current token included; some request holds 32. `routes`: each token names two different experts; among the 2 tokens of one micro-batch on one index of side, no expert is named more than 2 times.
All inputs are finite; a program needn't handle non-finite values.
Results may differ from a plain program's by a relative error of at most 0.0075.
Values may be sent and summed in bfloat16 or wider, within the bound.
No kernel may reach another device: no remote copies, remote signals or barrier semaphores. Data moves between devices by JAX's collectives and lax.ppermute only.
A program may use at most 192 MiB of HBM per device.

v0:
```python
import math

import jax
import jax.numpy as jnp
from jax import lax
from jax.sharding import PartitionSpec as P

HEAD_DIM = 128
EXPERTS = 4
CAP = 2


EPS = 1e-05
GATE_ONE = 65536.0


def attend(query_rows, key_cache, value_cache, page_rows, length_row):
    tok_count = query_rows.shape[0]
    kv_width = key_cache.shape[2]
    kv_local = kv_width // HEAD_DIM
    per_group = query_rows.shape[1] // kv_width
    inv_root = 1.0 / math.sqrt(HEAD_DIM)
    key_rows = key_cache[page_rows].reshape(tok_count, -1, kv_local, HEAD_DIM)
    value_rows = value_cache[page_rows].reshape(tok_count, -1, kv_local, HEAD_DIM)
    query_heads = query_rows.reshape(tok_count, kv_local, per_group, HEAD_DIM)
    scores = (
        jnp.einsum("tkgd,tlkd->tkgl", query_heads, key_rows, preferred_element_type=jnp.float32)
        * inv_root
    )
    positions = jnp.arange(key_rows.shape[1], dtype=jnp.int32)
    is_live = (positions[None, :] < length_row[:, None])[:, None, None, :]
    scores = jnp.where(is_live, scores, -1e30)
    row_max = jnp.max(scores, axis=-1, keepdims=True)
    unnorm = jnp.where(is_live, jnp.exp(scores - row_max), 0.0)
    denom_sum = jnp.sum(unnorm, axis=-1, keepdims=True)
    blended = (
        jnp.einsum(
            "tkgl,tlkd->tkgd",
            unnorm.astype(jnp.bfloat16),
            value_rows,
            preferred_element_type=jnp.float32,
        )
        / denom_sum
    )
    return blended.reshape(tok_count, -1)


def per_device(
    residual,
    queries,
    key_cache,
    value_cache,
    page_table,
    lengths,
    routes,
    gate_fixed,
    norm_gain,
    w_gate,
    w_up,
    w_down,
):
    micro_count, tok_dev, half_width = residual.shape
    tp_size = lax.axis_size("tp")
    full_width = half_width * tp_size
    side_size = lax.axis_size("side")
    expert_span = side_size // EXPERTS
    results = []
    for micro_idx in range(micro_count):
        attended = attend(
            queries[micro_idx], key_cache, value_cache, page_table[micro_idx], lengths[micro_idx]
        )
        carried = (residual[micro_idx].astype(jnp.float32) + attended).astype(jnp.bfloat16)
        joined = lax.all_gather(carried, "tp", axis=1, tiled=True)
        whole_rows = joined.astype(jnp.float32)
        inv_rms = lax.rsqrt(jnp.mean(whole_rows * whole_rows, axis=-1, keepdims=True) + EPS)
        normed = (whole_rows * inv_rms * norm_gain.astype(jnp.float32)).astype(jnp.bfloat16)
        row_width = normed.shape[1]
        expert_ids = routes[micro_idx]
        per_token = expert_ids.shape[1]
        flat_ids = expert_ids.reshape(-1)
        member = (flat_ids[:, None] == jnp.arange(EXPERTS, dtype=jnp.int32)[None, :]).astype(
            jnp.int32
        )
        slot_idx = jnp.sum((jnp.cumsum(member, axis=0) - 1) * member, axis=1)
        slot_pos = flat_ids * CAP + slot_idx
        one_hot = (slot_pos[:, None] == jnp.arange(EXPERTS * CAP, dtype=jnp.int32)[None, :]).astype(
            jnp.bfloat16
        )
        doubled = jnp.repeat(normed, per_token, axis=0)
        packed = jnp.einsum(
            "rs,rw->sw", one_hot, doubled, preferred_element_type=jnp.float32
        ).astype(jnp.bfloat16)
        outgoing = jnp.broadcast_to(
            packed.reshape(EXPERTS, 1, CAP, row_width), (EXPERTS, expert_span, CAP, row_width)
        )
        outgoing = outgoing.reshape(side_size, CAP, row_width)
        incoming = lax.all_to_all(outgoing, "side", split_axis=0, concat_axis=0, tiled=True)
        rows_in = incoming
        rows_in = rows_in.reshape(side_size * CAP, full_width)
        gate_proj = jnp.dot(rows_in, w_gate, preferred_element_type=jnp.float32)
        up_proj = jnp.dot(rows_in, w_up, preferred_element_type=jnp.float32)
        hidden = (jax.nn.silu(gate_proj) * up_proj).astype(jnp.bfloat16)
        paired = lax.all_gather(hidden, "tp", axis=1, tiled=True)
        partial_value = jnp.dot(paired, w_down, preferred_element_type=jnp.float32)
        returned = lax.all_to_all(
            partial_value.reshape(side_size, CAP, half_width),
            "side",
            split_axis=0,
            concat_axis=0,
            tiled=True,
        )
        experts_out = jnp.sum(returned.reshape(EXPERTS, expert_span, CAP, half_width), axis=1)
        experts_out = experts_out.reshape(EXPERTS * CAP, half_width)
        chosen = experts_out[slot_pos].reshape(tok_dev, per_token, half_width)
        first_gate = gate_fixed[micro_idx].astype(jnp.float32) / GATE_ONE
        second = (GATE_ONE - gate_fixed[micro_idx].astype(jnp.float32)) / GATE_ONE
        moe_sum = first_gate[:, None] * chosen[:, 0] + second[:, None] * chosen[:, 1]
        results.append((carried.astype(jnp.float32) + moe_sum).astype(jnp.bfloat16))
    return jnp.stack(results)


def solution(mesh):
    in_specs = (
        P(None, ("groups", "side"), "tp"),
        P(None, ("groups", "side"), "tp"),
        P(("groups", "side"), None, "tp"),
        P(("groups", "side"), None, "tp"),
        P(None, ("groups", "side"), None),
        P(None, ("groups", "side")),
        P(None, ("groups", "side"), None),
        P(None, ("groups", "side")),
        P(),
        P(None, ("side", "tp")),
        P(None, ("side", "tp")),
        P("side", "tp"),
    )
    out_specs = P(None, ("groups", "side"), "tp")
    return jax.shard_map(
        per_device, mesh=mesh, in_specs=in_specs, out_specs=out_specs, check_vma=False
    )
```

profile of v0, /device:TPU:0, one launch (start us, length us, event | category | flops | bytes accessed | tf_op | source)
XLA Modules:
  0.0 119.2 jit_solution(9831163285338712139)
XLA Ops:
  0.0 0.7 compare_select_fusion.1
  1.4 1.4 %gather_fusion = bf16[4,16,256]{2,1,0:T(8,128)(2,1)S(1)} fusion(bf16[8,16,256]{2,1,0:T(8,128)(2,1)} %param.14, s32[1024]{0:T(1024)S(1)} %pad_clamp_fusion.3), kind=kCustom, calls=%fused_computation | custom fusion | bytes 65552 | tf_op jit(solution)/shard_map/gather | solution.py:23
  3.4 1.4 %gather_fusion.3 = bf16[4,16,256]{2,1,0:T(8,128)(2,1)S(1)} fusion(bf16[8,16,256]{2,1,0:T(8,128)(2,1)} %param.14, s32[1024]{0:T(1024)S(1)} %pad_clamp_fusion.1), kind=kCustom, calls=%fused_computation.3 | custom fusion | bytes 65552 | tf_op jit(solution)/shard_map/gather | solution.py:23
  4.9 0.7 fusion.50
  5.6 0.8 slice_bitcast_fusion.1
  7.6 0.7 fusion.26
  8.3 1.9 %all_gather.12 = bf16[2,3072]{1,0:T(2,128)(2,1)S(1)} all-gather(bf16[2,1536]{1,0:T(2,128)(2,1)S(1)} %get-tuple-element.13), channel_id=1, replica_groups=mesh['groups'=2,'side'=8,'tp'=2] {'tp'}, dimensions={1}, use_global_device_ids=true | all-gather | bytes 18432 | tf_op jit(solution)/shard_map/all_gather | solution.py:73
  11.1 1.8 %all_gather.14 = bf16[2,3072]{1,0:T(2,128)(2,1)S(1)} all-gather(bf16[2,1536]{1,0:T(2,128)(2,1)S(1)} %get-tuple-element.14), channel_id=1, replica_groups=mesh['groups'=2,'side'=8,'tp'=2] {'tp'}, dimensions={1}, use_global_device_ids=true | all-gather | bytes 18432 | tf_op jit(solution)/shard_map/all_gather | solution.py:73
  13.2 0.7 broadcast_multiply_fusion.1
  15.3 7.1 %all-to-all-start = ((bf16[8,2,3072]{2,1,0:T(2,128)(2,1)}), bf16[8,2,3072]{2,1,0:T(2,128)(2,1)S(1)}, u32[]{:S(2)}, u32[]{:S(2)}) async-start(bf16[8,2,3072]{2,1,0:T(2,128)(2,1)} %bitcast.5), calls=%async_computation | async-start | bytes 196608 | tf_op jit(solution)/shard_map/all_to_all | solution.py:97
  23.4 0.8 multiply_bitcast_fusion.3
  24.1 5.4 %all-to-all-done = bf16[8,2,3072]{2,1,0:T(2,128)(2,1)S(1)} async-done(((bf16[8,2,3072]{2,1,0:T(2,128)(2,1)}), bf16[8,2,3072]{2,1,0:T(2,128)(2,1)S(1)}, u32[]{:S(2)}, u32[]{:S(2)}) %all-to-all-start) | async-done | bytes 98336 | tf_op jit(solution)/shard_map/all_to_all | solution.py:97
  30.2 3.4 %all-to-all-start.2 = ((bf16[8,2,3072]{2,1,0:T(2,128)(2,1)}), bf16[8,2,3072]{2,1,0:T(2,128)(2,1)S(1)}, u32[]{:S(2)}, u32[]{:S(2)}) async-start(bf16[8,2,3072]{2,1,0:T(2,128)(2,1)} %bitcast.17), calls=%async_computation.2 | async-start | bytes 196608 | tf_op jit(solution)/shard_map/all_to_all | solution.py:97
  33.6 9.9 %fusion.53 = f32[16,4096]{1,0:T(8,128)S(1)} fusion(bf16[16,3072]{1,0:T(8,128)(2,1)S(1)} %reshape.423, bf16[3072,4096]{1,0:T(8,128)(2,1)} %param.21), kind=kOutput, calls=%fused_computation.112 | convolution fusion | flops 402653184 | bytes 25526272 | tf_op jit(solution)/shard_map/dot_general | solution.py:100
  43.5 10.0 %fusion.2 = bf16[16,4096]{1,0:T(8,128)(2,1)S(1)} fusion(bf16[16,3072]{1,0:T(8,128)(2,1)S(1)} %reshape.423, bf16[3072,4096]{1,0:T(8,128)(2,1)} %param.22, f32[16,4096]{1,0:T(8,128)S(1)} %fusion.53), kind=kOutput, calls=%fused_computation.10 | convolution fusion | flops 403046400 | bytes 25657344 | tf_op jit(solution)/shard_map/dot_general | solution.py:101
  53.5 2.0 %all_gather.13 = bf16[16,8192]{1,0:T(8,128)(2,1)S(1)} all-gather(bf16[16,4096]{1,0:T(8,128)(2,1)S(1)} %fusion.2), channel_id=1, replica_groups=mesh['groups'=2,'side'=8,'tp'=2] {'tp'}, dimensions={1}, use_global_device_ids=true | all-gather | bytes 393216 | tf_op jit(solution)/shard_map/all_gather | solution.py:103
  55.5 9.9 %fusion.54 = f32[16,1536]{1,0:T(8,128)S(1)} fusion(bf16[16,8192]{1,0:T(8,128)(2,1)S(1)} %all_gather.13, bf16[8192,1536]{1,0:T(8,128)(2,1)} %param.23), kind=kOutput, calls=%fused_computation.113 | convolution fusion | flops 402653184 | bytes 25526272 | tf_op jit(solution)/shard_map/dot_general | solution.py:104
  66.1 5.9 %all-to-all-start.1 = ((f32[8,2,1536]{2,1,0:T(2,128)}), f32[8,2,1536]{2,1,0:T(2,128)S(1)}, u32[]{:S(2)}, u32[]{:S(2)}) async-start(f32[8,2,1536]{2,1,0:T(2,128)} %reshape.424), calls=%async_computation.1 | async-start | bytes 196608 | tf_op jit(solution)/shard_map/all_to_all | solution.py:105
  72.1 9.9 %fusion.55 = f32[16,4096]{1,0:T(8,128)S(1)} fusion(bf16[16,3072]{1,0:T(8,128)(2,1)S(1)} %reshape.434, bf16[3072,4096]{1,0:T(8,128)(2,1)} %param.21), kind=kOutput, calls=%fused_computation.114 | convolution fusion | flops 402653184 | bytes 25526272 | tf_op jit(solution)/shard_map/dot_general | solution.py:100
  82.0 10.0 %fusion.3 = bf16[16,4096]{1,0:T(8,128)(2,1)S(1)} fusion(bf16[16,3072]{1,0:T(8,128)(2,1)S(1)} %reshape.434, bf16[3072,4096]{1,0:T(8,128)(2,1)} %param.22, f32[16,4096]{1,0:T(8,128)S(1)} %fusion.55), kind=kOutput, calls=%fused_computation.11 | convolution fusion | flops 403046400 | bytes 25657344 | tf_op jit(solution)/shard_map/dot_general | solution.py:101
  92.0 2.0 %all_gather.15 = bf16[16,8192]{1,0:T(8,128)(2,1)S(1)} all-gather(bf16[16,4096]{1,0:T(8,128)(2,1)S(1)} %fusion.3), channel_id=1, replica_groups=mesh['groups'=2,'side'=8,'tp'=2] {'tp'}, dimensions={1}, use_global_device_ids=true | all-gather | bytes 393216 | tf_op jit(solution)/shard_map/all_gather | solution.py:103
  94.0 9.9 %fusion.56 = f32[16,1536]{1,0:T(8,128)S(1)} fusion(bf16[16,8192]{1,0:T(8,128)(2,1)S(1)} %all_gather.15, bf16[8192,1536]{1,0:T(8,128)(2,1)} %param.23), kind=kOutput, calls=%fused_computation.115 | convolution fusion | flops 402653184 | bytes 25526272 | tf_op jit(solution)/shard_map/dot_general | solution.py:104
  104.6 6.0 %all-to-all-start.3 = ((f32[8,2,1536]{2,1,0:T(2,128)}), f32[8,2,1536]{2,1,0:T(2,128)S(1)}, u32[]{:S(2)}, u32[]{:S(2)}) async-start(f32[8,2,1536]{2,1,0:T(2,128)} %reshape.435), calls=%async_computation.3 | async-start | bytes 196608 | tf_op jit(solution)/shard_map/all_to_all | solution.py:105
  111.3 6.4 %all-to-all-done.3 = f32[8,2,1536]{2,1,0:T(2,128)S(1)} async-done(((f32[8,2,1536]{2,1,0:T(2,128)}), f32[8,2,1536]{2,1,0:T(2,128)S(1)}, u32[]{:S(2)}, u32[]{:S(2)}) %all-to-all-start.3) | async-done | bytes 98336 | tf_op jit(solution)/shard_map/all_to_all | solution.py:105
  (81 shorter events, 10.2 us)
Async XLA Ops:
  0.0 0.8 copy-start
  15.3 14.2 %all-to-all-start = ((bf16[8,2,3072]{2,1,0:T(2,128)(2,1)}), bf16[8,2,3072]{2,1,0:T(2,128)(2,1)S(1)}, u32[]{:S(2)}, u32[]{:S(2)}) async-start(bf16[8,2,3072]{2,1,0:T(2,128)(2,1)} %bitcast.5), calls=%async_computation | async-start | bytes 196608 | tf_op jit(solution)/shard_map/all_to_all | solution.py:97
  30.2 35.9 %all-to-all-start.2 = ((bf16[8,2,3072]{2,1,0:T(2,128)(2,1)}), bf16[8,2,3072]{2,1,0:T(2,128)(2,1)S(1)}, u32[]{:S(2)}, u32[]{:S(2)}) async-start(bf16[8,2,3072]{2,1,0:T(2,128)(2,1)} %bitcast.17), calls=%async_computation.2 | async-start | bytes 196608 | tf_op jit(solution)/shard_map/all_to_all | solution.py:97
  66.1 38.5 %all-to-all-start.1 = ((f32[8,2,1536]{2,1,0:T(2,128)}), f32[8,2,1536]{2,1,0:T(2,128)S(1)}, u32[]{:S(2)}, u32[]{:S(2)}) async-start(f32[8,2,1536]{2,1,0:T(2,128)} %reshape.424), calls=%async_computation.1 | async-start | bytes 196608 | tf_op jit(solution)/shard_map/all_to_all | solution.py:105
  82.0 37.2 %copy-start.1 = (bf16[8,16,256]{2,1,0:T(8,128)(2,1)S(1)}, bf16[8,16,256]{2,1,0:T(8,128)(2,1)}, u32[]{:S(2)}) copy-start(bf16[8,16,256]{2,1,0:T(8,128)(2,1)} %param.15) | copy-start | bytes 196612
  92.0 26.4 %copy-start.2 = (bf16[2,2,1536]{2,1,0:T(2,128)(2,1)S(1)}, bf16[2,2,1536]{2,1,0:T(2,128)(2,1)}, u32[]{:S(2)}) copy-start(bf16[2,2,1536]{2,1,0:T(2,128)(2,1)} %param.12) | copy-start | bytes 36868
  104.6 13.1 %all-to-all-start.3 = ((f32[8,2,1536]{2,1,0:T(2,128)}), f32[8,2,1536]{2,1,0:T(2,128)S(1)}, u32[]{:S(2)}, u32[]{:S(2)}) async-start(f32[8,2,1536]{2,1,0:T(2,128)} %reshape.435), calls=%async_computation.3 | async-start | bytes 196608 | tf_op jit(solution)/shard_map/all_to_all | solution.py:105
  118.6 0.6 copy-start.3
where the time goes:
time: 120 us; the launch traced here: 119 us
  matrix products  60.8 us (51%)
  starting transfers between devices  22.4 us (19%)
  waiting for transfers between devices  11.8 us (10%)
  local copies, waits for them, and re-layouts  10.9 us (9%)
  blocking collectives  7.73 us (6%)
  other arithmetic  5.28 us (4%)
    dot_general x2, matrix products, per_device(): up_proj = jnp.dot(rows_in, w_up, preferred_element_type=jnp.float32)  20 us
    dot_general x2, matrix products, per_device(): gate_proj = jnp.dot(rows_in, w_gate, preferred_element_type=jnp.float32)  19.8 us
    dot_general x2, matrix products, per_device(): partial_value = jnp.dot(paired, w_down, preferred_element_type=jnp.float32)  19.8 us
    all_to_all x2, starting transfers between devices, per_device(): lax.all_to_all(partial_value.reshape(side_size, CAP, half_width), 'side',...  11.9 us
    all_to_all x2, starting transfers between devices, per_device(): lax.all_to_all(outgoing, 'side', split_axis=0, concat_axis=0, tiled=True)  10.5 us
    all_to_all x2, waiting for transfers between devices, per_device(): lax.all_to_all(partial_value.reshape(side_size, CAP, half_width), 'side',...  6.41 us
    all_to_all x2, waiting for transfers between devices, per_device(): lax.all_to_all(outgoing, 'side', split_axis=0, concat_axis=0, tiled=True)  5.39 us
    all_gather x2, blocking collectives, per_device(): paired = lax.all_gather(hidden, 'tp', axis=1, tiled=True)  3.99 us
  transfers between devices with their start and end apart: 4, of which 2 were waited for; matrix products, arithmetic and copies ran while one was open for 53% of the time, Pallas kernels for 0%

commit v1 on v0

v1 whole, which is shorter than its diff:
```python
import functools
import math

import jax
import jax.numpy as jnp
from jax import lax
from jax.experimental import pallas as pl
from jax.experimental.pallas import tpu as pltpu
from jax.sharding import PartitionSpec as P

HEAD_DIM = 128
EXPERTS = 4
EPS = 1e-05
GATE_ONE = 65536.0
LANES = 128
SMALL = 2 << 20


def by_row(shape, scalars):
    token = lax.broadcasted_iota(jnp.int32, shape, 0) % len(scalars)
    out = jnp.full(shape, scalars[0])
    for idx in range(1, len(scalars)):
        out = jnp.where(token == idx, scalars[idx], out)
    return out


def flat(ref):
    return jnp.concatenate([ref[idx].astype(jnp.float32) for idx in range(ref.shape[0])], axis=0)


def attend_kernel(where_ref, pages_ref, len_ref, routes_ref, gate_ref, res_ref, q_ref, k_ref, v_ref, _w0_ref, _w1_ref, out_ref):
    micro, dev, half = res_ref.shape
    tok = micro * dev
    pages, page, kv_width = k_ref.shape
    kv_local = kv_width // HEAD_DIM
    group = half // kv_width
    inv_root = 1.0 / math.sqrt(HEAD_DIM)
    keys = k_ref[...].reshape(pages * page, kv_width)
    values = v_ref[...].reshape(pages * page, kv_width)
    shape = (group * tok, pages * page)
    slot = lax.broadcasted_iota(jnp.int32, shape, 1)
    slot_page, offset = slot // page, slot % page
    position = jnp.full(shape, 1 << 20, jnp.int32)
    for nth in range(pages_ref.shape[2]):
        owner = by_row(shape, [pages_ref[t // dev, t % dev, nth] for t in range(tok)])
        position = jnp.where(slot_page == owner, offset + nth * page, position)
    live = position < by_row(shape, [len_ref[t // dev, t % dev] for t in range(tok)])
    queries = flat(q_ref)
    residual = flat(res_ref)
    for head in range(kv_local):
        cols = slice(head * HEAD_DIM, (head + 1) * HEAD_DIM)
        first = head * group
        rows = jnp.concatenate(
            [
                queries[:, (first + g) * HEAD_DIM : (first + g + 1) * HEAD_DIM]
                for g in range(group)
            ],
            axis=0,
        ).astype(jnp.bfloat16)
        scores = lax.dot_general(
            rows, keys[:, cols], (((1,), (1,)), ((), ())), preferred_element_type=jnp.float32
        )
        scores = jnp.where(live, scores * inv_root, -1e30)
        row_max = jnp.max(scores, axis=-1, keepdims=True)
        unnorm = jnp.where(live, jnp.exp(scores - row_max), 0.0)
        denom = jnp.sum(unnorm, axis=-1, keepdims=True)
        blended = (
            jnp.dot(
                unnorm.astype(jnp.bfloat16), values[:, cols], preferred_element_type=jnp.float32
            )
            / denom
        )
        for g in range(group):
            at = slice((first + g) * HEAD_DIM, (first + g + 1) * HEAD_DIM)
            carried = residual[:, at] + blended[g * tok : (g + 1) * tok]
            out_ref[:, at] = carried.astype(jnp.bfloat16)
    lane = lax.broadcasted_iota(jnp.int32, (tok, LANES), 1)
    expert = lane % EXPERTS
    fixed = by_row((tok, LANES), [gate_ref[t // dev, t % dev] for t in range(tok)])
    one = by_row((tok, LANES), [routes_ref[t // dev, t % dev, 0] for t in range(tok)])
    two = by_row((tok, LANES), [routes_ref[t // dev, t % dev, 1] for t in range(tok)])
    fixed = fixed.astype(jnp.float32)
    weight = jnp.where(expert == one, fixed / GATE_ONE, 0.0) + jnp.where(
        expert == two, (GATE_ONE - fixed) / GATE_ONE, 0.0
    )
    high = weight.astype(jnp.bfloat16).astype(jnp.float32)
    mid = (weight - high).astype(jnp.bfloat16).astype(jnp.float32)
    low = weight - high - mid
    term = lane // EXPERTS
    packed = jnp.where(
        term == 0, high, jnp.where(term == 1, mid, jnp.where(term == 2, low, 0.0))
    )
    out_ref[:, half:] = packed.astype(jnp.bfloat16)


def join_kernel(one_ref, two_ref, out_ref):
    out_ref[...] = jnp.concatenate([one_ref[...], two_ref[...]], axis=0)


def fetch(w_ref, buf_ref, sem, start):
    chunks, depth, _ = buf_ref.shape
    copies = []
    for idx in range(chunks):
        copies.append(
            pltpu.make_async_copy(
                w_ref.at[pl.ds(pl.multiple_of(start + idx * depth, depth), depth), :],
                buf_ref.at[idx],
                sem.at[idx],
            )
        )
        copies[-1].start()
    return copies


def hidden_kernel(
    where_ref, own_ref, other_ref, gain_ref, wg_ref, wu_ref, out_ref, x_ref, gate_ref, buf_ref, sem
):
    chunks, depth, _ = buf_ref.shape
    half = own_ref.shape[1] - LANES
    copies = fetch(wu_ref, buf_ref, sem, 0)
    is_first = where_ref[0] == 0
    own = own_ref[:, :half].astype(jnp.float32)
    other = other_ref[:, :half].astype(jnp.float32)
    square = jnp.sum(own * own, axis=-1, keepdims=True)
    square = square + jnp.sum(other * other, axis=-1, keepdims=True)
    inv_rms = lax.rsqrt(square / (2 * half) + EPS)
    left = jnp.where(is_first, own, other)
    right = jnp.where(is_first, other, own)
    gain = gain_ref[...].astype(jnp.float32).reshape(1, -1)
    x_ref[:, :half] = (left * inv_rms * gain[:, :half]).astype(jnp.bfloat16)
    x_ref[:, half:] = (right * inv_rms * gain[:, half:]).astype(jnp.bfloat16)
    gate = jnp.dot(x_ref[...], wg_ref[...], preferred_element_type=jnp.float32)
    gate_ref[...] = gate / (1.0 + jnp.exp(-gate))
    up = None
    for idx, copy in enumerate(copies):
        copy.wait()
        part = jnp.dot(
            x_ref[:, idx * depth : (idx + 1) * depth],
            buf_ref[idx],
            preferred_element_type=jnp.float32,
        )
        up = part if up is None else up + part
    out_ref[...] = (gate_ref[...] * up).astype(jnp.bfloat16)


def down_own_kernel(where_ref, hid_ref, w_ref, out_ref, buf_ref, sem):
    chunks, depth, _ = buf_ref.shape
    copies = fetch(w_ref, buf_ref, sem, where_ref[0] * chunks * depth)
    for idx, copy in enumerate(copies):
        copy.wait()
        part = jnp.dot(
            hid_ref[:, idx * depth : (idx + 1) * depth],
            buf_ref[idx],
            preferred_element_type=jnp.float32,
        )
        out_ref[...] = part if idx == 0 else out_ref[...] + part


def down_other_kernel(where_ref, hid_ref, part_ref, extra_ref, w_ref, out_ref, buf_ref, sem):
    chunks, depth, _ = buf_ref.shape
    copies = fetch(w_ref, buf_ref, sem, (1 - where_ref[0]) * chunks * depth)
    total = part_ref[...]
    for idx, copy in enumerate(copies):
        copy.wait()
        total = total + jnp.dot(
            hid_ref[:, idx * depth : (idx + 1) * depth],
            buf_ref[idx],
            preferred_element_type=jnp.float32,
        )
    extra = extra_ref[...].astype(jnp.float32)
    lane = lax.broadcasted_iota(jnp.int32, extra.shape, 1)
    mine = (lane % EXPERTS == where_ref[1]) & (lane < 3 * EXPERTS)
    weight = jnp.sum(jnp.where(mine, extra, 0.0), axis=-1, keepdims=True)
    out_ref[...] = (total * weight).astype(jnp.bfloat16)


SMEM = pl.BlockSpec(memory_space=pltpu.SMEM)
VMEM = pl.BlockSpec(memory_space=pltpu.VMEM)
ANY = pl.BlockSpec(memory_space=pl.ANY)


def call(kernel, out_shape, in_specs, args, scratch=(), limit=SMALL):
    return pl.pallas_call(
        kernel,
        out_shape=out_shape,
        in_specs=in_specs,
        out_specs=jax.tree.map(lambda _: VMEM, out_shape),
        scratch_shapes=scratch,
        compiler_params=pltpu.CompilerParams(vmem_limit_bytes=limit),
    )(*args)


def in_vmem(array):
    return pltpu.with_memory_space_constraint(array, pltpu.VMEM)


def in_hbm(array):
    return pltpu.with_memory_space_constraint(array, pltpu.HBM)


def swap(array, axis, mask):
    size = lax.axis_size(axis)
    return lax.ppermute(array, axis, [(i, i ^ mask) for i in range(size)])


def per_device(
    residual,
    queries,
    key_cache,
    value_cache,
    page_table,
    lengths,
    routes,
    gate_fixed,
    norm_gain,
    w_gate,
    w_up,
    w_down,
):
    micro_count, tok_dev, half = residual.shape
    side_size = lax.axis_size("side")
    tok = micro_count * tok_dev
    rows = tok * side_size
    span = side_size // EXPERTS
    small = SMALL + 64 * rows * half
    width = w_gate.shape[1]
    where = jnp.stack([lax.axis_index("tp"), lax.axis_index("side") // span]).astype(jnp.int32)
    local = call(
        attend_kernel,
        jax.ShapeDtypeStruct((tok, half + LANES), jnp.bfloat16),
        [SMEM] * 5 + [VMEM] * 4 + [ANY] * 2,
        (
            where,
            page_table,
            lengths,
            routes,
            gate_fixed,
            residual,
            queries,
            key_cache,
            value_cache,
            in_hbm(w_gate),
            in_hbm(w_up),
        ),
    )
    gathered = local
    masks = [1 << bit for bit in range(side_size.bit_length() - 1)]
    for mask in masks:
        shape = (2 * gathered.shape[0], gathered.shape[1])
        gathered = call(
            join_kernel,
            jax.ShapeDtypeStruct(shape, gathered.dtype),
            [VMEM] * 2,
            (gathered, swap(gathered, "side", mask)),
            limit=small,
        )
    other = swap(gathered, "tp", 1)
    up_chunks = 6
    hidden = call(
        hidden_kernel,
        jax.ShapeDtypeStruct((rows, width), jnp.bfloat16),
        [SMEM] + [VMEM] * 4 + [ANY],
        (where, gathered, other, norm_gain, in_vmem(w_gate), in_hbm(w_up)),
        (
            pltpu.VMEM((rows, 2 * half), jnp.bfloat16),
            pltpu.VMEM((rows, width), jnp.float32),
            pltpu.VMEM((up_chunks, 2 * half // up_chunks, width), jnp.bfloat16),
            pltpu.SemaphoreType.DMA((up_chunks,)),
        ),
        small + w_up.size * w_up.dtype.itemsize,
    )
    hidden_other = swap(hidden, "tp", 1)
    chunks = max(1, width // 1024)
    stream = (
        pltpu.VMEM((chunks, width // chunks, half), jnp.bfloat16),
        pltpu.SemaphoreType.DMA((chunks,)),
    )
    part = call(
        down_own_kernel,
        jax.ShapeDtypeStruct((rows, half), jnp.float32),
        [SMEM, VMEM, ANY],
        (where, hidden, in_hbm(w_down)),
        stream,
        small + w_down.size * w_down.dtype.itemsize // 2,
    )
    sent = call(
        down_other_kernel,
        jax.ShapeDtypeStruct((rows, half), jnp.bfloat16),
        [SMEM] + [VMEM] * 3 + [ANY],
        (where, hidden_other, part, gathered[:, half:], in_hbm(w_down)),
        stream,
        small + w_down.size * w_down.dtype.itemsize // 2,
    )
    for mask in reversed(masks):
        count = sent.shape[0] // 2
        received = swap(sent[count:], "side", mask)
        sent = sent[:count].astype(jnp.float32) + received.astype(jnp.float32)
        if mask > 1:
            sent = sent.astype(jnp.bfloat16)
    carried = local[:, :half].astype(jnp.float32)
    return (carried + sent).astype(jnp.bfloat16).reshape(residual.shape)


def solution(mesh):
    in_specs = (
        P(None, ("groups", "side"), "tp"),
        P(None, ("groups", "side"), "tp"),
        P(("groups", "side"), None, "tp"),
        P(("groups", "side"), None, "tp"),
        P(None, ("groups", "side"), None),
        P(None, ("groups", "side")),
        P(None, ("groups", "side"), None),
        P(None, ("groups", "side")),
        P(),
        P(None, ("side", "tp")),
        P(None, ("side", "tp")),
        P("side", "tp"),
    )
    out_specs = P(None, ("groups", "side"), "tp")
    return jax.shard_map(
        per_device, mesh=mesh, in_specs=in_specs, out_specs=out_specs, check_vma=False
    )
```

time: 120 us -> 62.6 us (0.52)
  matrix products: 60.8 us -> 0 us
  Pallas kernels: 0 us -> 27.1 us
  blocking collectives: 7.73 us -> 0 us
  starting transfers between devices: 22.4 us -> 15.3 us
  other arithmetic: 5.28 us -> 0.11 us
  local copies, waits for them, and re-layouts: 10.9 us -> 6.45 us
  waiting for transfers between devices: 11.8 us -> 13.1 us
    dot_general x12 -> x0, matrix products: 60.8 us -> none  [the longest x2 20 us: per_device(): up_proj = jnp.dot(rows_in, w_up, preferred_element_type=jnp.float32)]
    pallas_call x0 -> x7, Pallas kernels: none -> 27.1 us  [call(): pl.pallas_call(kernel, out_shape=out_shape, in_specs=in_specs, out_specs=...]
    all_to_all x4 -> x0, starting transfers between devices: 22.4 us -> none  [the longest x2 11.9 us: per_device(): lax.all_to_all(partial_value.reshape(side_size, CAP, half_width), 'side',...]
    ppermute x0 -> x8, starting transfers between devices: none -> 15.3 us  [swap(): return lax.ppermute(array, axis, [(i, i ^ mask) for i in range(size)])]
    ppermute x0 -> x8, waiting for transfers between devices: none -> 13.1 us  [swap(): return lax.ppermute(array, axis, [(i, i ^ mask) for i in range(size)])]
    all_to_all x4 -> x0, waiting for transfers between devices: 11.8 us -> none  [the longest x2 6.41 us: per_device(): lax.all_to_all(partial_value.reshape(side_size, CAP, half_width), 'side',...]
    all_gather x4 -> x0, blocking collectives: 7.73 us -> none  [the longest x2 3.99 us: per_device(): paired = lax.all_gather(hidden, 'tp', axis=1, tiled=True)]
    unnamed x8 -> x20, local copies, waits for them, and re-layouts: 0.62 us -> 5.82 us
  transfers between devices with their start and end apart: 4 -> 8, of which waited for: 2 -> 7; matrix products, arithmetic and copies ran while one was open for 53% -> 0% of each run, Pallas kernels for 0% -> 9%
where the time goes in v1:
time: 62.6 us; the launch traced here: 62.2 us
  Pallas kernels  27.1 us (43%)
  starting transfers between devices  15.3 us (24%)
  waiting for transfers between devices  13.1 us (21%)
  local copies, waits for them, and re-layouts  6.45 us (10%)
    pallas_call x7, Pallas kernels, call(): pl.pallas_call(kernel, out_shape=out_shape, in_specs=in_specs, out_specs=...  27.1 us
    ppermute x8, starting transfers between devices, swap(): return lax.ppermute(array, axis, [(i, i ^ mask) for i in range(size)])  15.3 us
    ppermute x8, waiting for transfers between devices, swap(): return lax.ppermute(array, axis, [(i, i ^ mask) for i in range(size)])  13.1 us
    unnamed x20, local copies, waits for them, and re-layouts  5.82 us
  transfers between devices with their start and end apart: 8, of which 7 were waited for; matrix products, arithmetic and copies ran while one was open for 0% of the time, Pallas kernels for 9%

profile of v1, /device:TPU:0, one launch (start us, length us, event | category | flops | bytes accessed | tf_op | source)
XLA Modules:
  0.0 62.2 jit_solution(10688537343243142462)
XLA Ops:
  0.1 0.8 %copy-done.1 = bf16[8,16,256]{2,1,0:T(8,128)(2,1)S(1)} copy-done((bf16[8,16,256]{2,1,0:T(8,128)(2,1)S(1)}, bf16[8,16,256]{2,1,0:T(8,128)(2,1)}, u32[]{:S(2)}) %copy-start.1) | copy-done | bytes 65560
  0.9 0.8 %copy-done.2 = bf16[8,16,256]{2,1,0:T(8,128)(2,1)S(1)} copy-done((bf16[8,16,256]{2,1,0:T(8,128)(2,1)S(1)}, bf16[8,16,256]{2,1,0:T(8,128)(2,1)}, u32[]{:S(2)}) %copy-start.2) | copy-done | bytes 65560
  1.8 0.7 %copy-done.3 = bf16[2,2,1536]{2,1,0:T(2,128)(2,1)S(1)} copy-done((bf16[2,2,1536]{2,1,0:T(2,128)(2,1)S(1)}, bf16[2,2,1536]{2,1,0:T(2,128)(2,1)}, u32[]{:S(2)}) %copy-start.3) | copy-done | bytes 12312
  2.5 0.7 %copy-done.4 = bf16[2,2,1536]{2,1,0:T(2,128)(2,1)S(1)} copy-done((bf16[2,2,1536]{2,1,0:T(2,128)(2,1)S(1)}, bf16[2,2,1536]{2,1,0:T(2,128)(2,1)}, u32[]{:S(2)}) %copy-start.4) | copy-done | bytes 12312
  3.2 0.7 %copy-done.6 = s32[2,2,2]{2,1,0:T(2,128)S(1)} copy-done((s32[2,2,2]{2,1,0:T(2,128)S(1)}, s32[2,2,2]{2,1,0:T(2,128)}, u32[]{:S(2)}) %copy-start.6) | copy-done | bytes 56
  3.9 0.7 %copy-done.7 = s32[2,2,2]{2,1,0:T(2,128)S(1)} copy-done((s32[2,2,2]{2,1,0:T(2,128)S(1)}, s32[2,2,2]{2,1,0:T(2,128)}, u32[]{:S(2)}) %copy-start.7) | copy-done | bytes 56
  4.5 0.7 %copy-done.8 = s32[2,2]{1,0:T(2,128)S(1)} copy-done((s32[2,2]{1,0:T(2,128)S(1)}, s32[2,2]{1,0:T(2,128)}, u32[]{:S(2)}) %copy-start.8) | copy-done | bytes 40
  5.9 1.2 %shard_map.118.one_ref = bf16[4,1664]{1,0:T(4,128)(2,1)S(1)} custom-call(s32[2]{0:T(128)S(1)} %pad_add_fusion.where_ref, s32[2,2,2]{2,1,0:T(2,128)S(1)} %copy-done.6, s32[2,2]{1,0:T(2,128)S(1)} %copy-done.8, s32[2,2,2]{2,1,0:T(2,128)S(1)} %copy-done.7, s32[2,2]{1,0:T(2,128)S(1)} %copy-done.9, bf16[2,2,1536]{2,1,0:T(2,128)(2,1)S(1)} %copy-done.3, ...), custom_call_target="tpu_custom_call" | custom-call | tf_op jit(solution)/shard_map/pallas_call | solution.py:183
  7.1 3.0 %collective-permute-start = (bf16[4,1664]{1,0:T(4,128)(2,1)S(1)}, bf16[4,1664]{1,0:T(4,128)(2,1)S(1)}, u32[]{:S(2)}, u32[]{:S(2)}) collective-permute-start(bf16[4,1664]{1,0:T(4,128)(2,1)S(1)} %shard_map.118.one_ref), channel_id=1, source_target_pairs={{0,2},{2,0},{4,6},{6,4},{8,10},{10,8},{12,14},{14,12},{1,3},{3,1},... | collective-permute-start | bytes 39944 | tf_op jit(solution)/shard_map/ppermute | solution.py:203
  10.1 1.7 %collective-permute-done.two_ref = bf16[4,1664]{1,0:T(4,128)(2,1)S(1)} collective-permute-done((bf16[4,1664]{1,0:T(4,128)(2,1)S(1)}, bf16[4,1664]{1,0:T(4,128)(2,1)S(1)}, u32[]{:S(2)}, u32[]{:S(2)}) %collective-permute-start) | collective-permute-done | bytes 13344 | tf_op jit(solution)/shard_map/ppermute | solution.py:203
  11.8 2.2 %collective-permute-start.1 = (bf16[8,1664]{1,0:T(8,128)(2,1)S(1)}, bf16[8,1664]{1,0:T(8,128)(2,1)S(1)}, u32[]{:S(2)}, u32[]{:S(2)}) collective-permute-start(bf16[8,1664]{1,0:T(8,128)(2,1)S(1)} %shard_map.119.one_ref), channel_id=1, source_target_pairs={{0,4},{2,6},{4,0},{6,2},{8,12},{10,14},{12,8},{14,10},{1,5},{3,7},... | collective-permute-start | bytes 79880 | tf_op jit(solution)/shard_map/ppermute | solution.py:203
  14.0 1.8 %collective-permute-done.1.two_ref = bf16[8,1664]{1,0:T(8,128)(2,1)S(1)} collective-permute-done((bf16[8,1664]{1,0:T(8,128)(2,1)S(1)}, bf16[8,1664]{1,0:T(8,128)(2,1)S(1)}, u32[]{:S(2)}, u32[]{:S(2)}) %collective-permute-start.1) | collective-permute-done | bytes 26656 | tf_op jit(solution)/shard_map/ppermute | solution.py:203
  15.8 3.1 %collective-permute-start.2 = (bf16[16,1664]{1,0:T(8,128)(2,1)S(1)}, bf16[16,1664]{1,0:T(8,128)(2,1)S(1)}, u32[]{:S(2)}, u32[]{:S(2)}) collective-permute-start(bf16[16,1664]{1,0:T(8,128)(2,1)S(1)} %shard_map.120.one_ref), channel_id=1, source_target_pairs={{0,8},{2,10},{4,12},{6,14},{8,0},{10,2},{12,4},{14,6},{1,9},{3,11}... | collective-permute-start | bytes 159752 | tf_op jit(solution)/shard_map/ppermute | solution.py:203
  18.9 2.1 %collective-permute-done.2.two_ref = bf16[16,1664]{1,0:T(8,128)(2,1)S(1)} collective-permute-done((bf16[16,1664]{1,0:T(8,128)(2,1)S(1)}, bf16[16,1664]{1,0:T(8,128)(2,1)S(1)}, u32[]{:S(2)}, u32[]{:S(2)}) %collective-permute-start.2) | collective-permute-done | bytes 53280 | tf_op jit(solution)/shard_map/ppermute | solution.py:203
  21.1 1.3 %collective-permute-done.3.other_ref = bf16[32,1664]{1,0:T(8,128)(2,1)S(1)} collective-permute-done((bf16[32,1664]{1,0:T(8,128)(2,1)S(1)}, bf16[32,1664]{1,0:T(8,128)(2,1)S(1)}, u32[]{:S(2)}, u32[]{:S(2)}) %collective-permute-start.3) | collective-permute-done | bytes 106528 | tf_op jit(solution)/shard_map/ppermute | solution.py:203
  22.4 14.1 %shard_map.122.hid_ref = bf16[32,4096]{1,0:T(8,128)(2,1)S(1)} custom-call(s32[2]{0:T(128)S(1)} %pad_add_fusion.where_ref, bf16[32,1664]{1,0:T(8,128)(2,1)S(1)} %shard_map.121.own_ref, bf16[32,1664]{1,0:T(8,128)(2,1)S(1)} %collective-permute-done.3.other_ref, bf16[3072]{0:T(1024)(128)(2,1)S(1)} %copy-done.5, bf16[3072,4096]{1,0:T(8,128)(2,1)S(1)} %copy-done, ...), custom_call_target="tpu_custom_call" | custom-call | tf_op jit(solution)/shard_map/pallas_call | solution.py:183
  36.8 5.9 %shard_map.123.part_ref = f32[32,1536]{1,0:T(8,128)S(1)} custom-call(s32[2]{0:T(128)S(1)} %pad_add_fusion.where_ref, bf16[32,4096]{1,0:T(8,128)(2,1)S(1)} %shard_map.122.hid_ref, bf16[8192,1536]{1,0:T(8,128)(2,1)} %w_ref.3), custom_call_target="tpu_custom_call" | custom-call | tf_op jit(solution)/shard_map/pallas_call | solution.py:183
  42.6 5.9 %shard_map.124 = bf16[32,1536]{1,0:T(8,128)(2,1)S(1)} custom-call(s32[2]{0:T(128)S(1)} %pad_add_fusion.where_ref, bf16[32,4096]{1,0:T(8,128)(2,1)S(1)} %collective-permute-done.4.hid_ref, f32[32,1536]{1,0:T(8,128)S(1)} %shard_map.123.part_ref, bf16[32,128]{1,0:T(8,128)(2,1)S(1)} %slice.33.extra_ref, bf16[8192,1536]{1,0:T(8,128)(2,1)} %w_ref.3), custom_call_target="tpu_custom_call" | custom-call | tf_op jit(solution)/shard_map/pallas_call | solution.py:183
  48.6 3.0 %collective-permute-start.5 = (bf16[16,1536]{1,0:T(8,128)(2,1)S(1)}, bf16[16,1536]{1,0:T(8,128)(2,1)S(1)}, u32[]{:S(2)}, u32[]{:S(2)}) collective-permute-start(bf16[16,1536]{1,0:T(8,128)(2,1)S(1)} %slice.35), channel_id=1, source_target_pairs={{0,8},{2,10},{4,12},{6,14},{8,0},{10,2},{12,4},{14,6},{1,9},{3,11}... | collective-permute-start | bytes 147464 | tf_op jit(solution)/shard_map/ppermute | solution.py:203
  51.6 2.3 %collective-permute-done.5 = bf16[16,1536]{1,0:T(8,128)(2,1)S(1)} collective-permute-done((bf16[16,1536]{1,0:T(8,128)(2,1)S(1)}, bf16[16,1536]{1,0:T(8,128)(2,1)S(1)}, u32[]{:S(2)}, u32[]{:S(2)}) %collective-permute-start.5) | collective-permute-done | bytes 49184 | tf_op jit(solution)/shard_map/ppermute | solution.py:203
  53.9 2.0 %collective-permute-start.6 = (bf16[8,1536]{1,0:T(8,128)(2,1)S(1)}, bf16[8,1536]{1,0:T(8,128)(2,1)S(1)}, u32[]{:S(2)}, u32[]{:S(2)}) collective-permute-start(bf16[8,1536]{1,0:T(8,128)(2,1)S(1)} %slice.37), channel_id=1, source_target_pairs={{0,4},{2,6},{4,0},{6,2},{8,12},{10,14},{12,8},{14,10},{1,5},{3,7},... | collective-permute-start | bytes 73736 | tf_op jit(solution)/shard_map/ppermute | solution.py:203
  55.9 1.8 %collective-permute-done.6 = bf16[8,1536]{1,0:T(8,128)(2,1)S(1)} collective-permute-done((bf16[8,1536]{1,0:T(8,128)(2,1)S(1)}, bf16[8,1536]{1,0:T(8,128)(2,1)S(1)}, u32[]{:S(2)}, u32[]{:S(2)}) %collective-permute-start.6) | collective-permute-done | bytes 24608 | tf_op jit(solution)/shard_map/ppermute | solution.py:203
  57.8 1.6 %collective-permute-start.7 = (bf16[4,1536]{1,0:T(4,128)(2,1)S(1)}, bf16[4,1536]{1,0:T(4,128)(2,1)S(1)}, u32[]{:S(2)}, u32[]{:S(2)}) collective-permute-start(bf16[4,1536]{1,0:T(4,128)(2,1)S(1)} %slice.39), channel_id=1, source_target_pairs={{0,2},{2,0},{4,6},{6,4},{8,10},{10,8},{12,14},{14,12},{1,3},{3,1},... | collective-permute-start | bytes 36872 | tf_op jit(solution)/shard_map/ppermute | solution.py:203
  59.5 2.1 %collective-permute-done.7 = bf16[4,1536]{1,0:T(4,128)(2,1)S(1)} collective-permute-done((bf16[4,1536]{1,0:T(4,128)(2,1)S(1)}, bf16[4,1536]{1,0:T(4,128)(2,1)S(1)}, u32[]{:S(2)}, u32[]{:S(2)}) %collective-permute-start.7) | collective-permute-done | bytes 12320 | tf_op jit(solution)/shard_map/ppermute | solution.py:203
  (28 shorter events, 1.8 us)
Async XLA Ops:
  0.1 0.8 %copy-start.1 = (bf16[8,16,256]{2,1,0:T(8,128)(2,1)S(1)}, bf16[8,16,256]{2,1,0:T(8,128)(2,1)}, u32[]{:S(2)}) copy-start(bf16[8,16,256]{2,1,0:T(8,128)(2,1)} %k_ref.1) | copy-start | bytes 196612
  0.9 0.8 %copy-start.2 = (bf16[8,16,256]{2,1,0:T(8,128)(2,1)S(1)}, bf16[8,16,256]{2,1,0:T(8,128)(2,1)}, u32[]{:S(2)}) copy-start(bf16[8,16,256]{2,1,0:T(8,128)(2,1)} %v_ref.1) | copy-start | bytes 196612
  1.8 0.7 %copy-start.3 = (bf16[2,2,1536]{2,1,0:T(2,128)(2,1)S(1)}, bf16[2,2,1536]{2,1,0:T(2,128)(2,1)}, u32[]{:S(2)}) copy-start(bf16[2,2,1536]{2,1,0:T(2,128)(2,1)} %res_ref.1) | copy-start | bytes 36868
  2.5 0.7 %copy-start.4 = (bf16[2,2,1536]{2,1,0:T(2,128)(2,1)S(1)}, bf16[2,2,1536]{2,1,0:T(2,128)(2,1)}, u32[]{:S(2)}) copy-start(bf16[2,2,1536]{2,1,0:T(2,128)(2,1)} %q_ref.1) | copy-start | bytes 36868
  3.2 0.7 %copy-start.6 = (s32[2,2,2]{2,1,0:T(2,128)S(1)}, s32[2,2,2]{2,1,0:T(2,128)}, u32[]{:S(2)}) copy-start(s32[2,2,2]{2,1,0:T(2,128)} %pages_ref.1) | copy-start | bytes 100
  3.9 0.7 %copy-start.7 = (s32[2,2,2]{2,1,0:T(2,128)S(1)}, s32[2,2,2]{2,1,0:T(2,128)}, u32[]{:S(2)}) copy-start(s32[2,2,2]{2,1,0:T(2,128)} %routes_ref.1) | copy-start | bytes 100
  4.5 0.7 %copy-start.8 = (s32[2,2]{1,0:T(2,128)S(1)}, s32[2,2]{1,0:T(2,128)}, u32[]{:S(2)}) copy-start(s32[2,2]{1,0:T(2,128)} %len_ref.1) | copy-start | bytes 52
  5.2 0.7 %copy-start.9 = (s32[2,2]{1,0:T(2,128)S(1)}, s32[2,2]{1,0:T(2,128)}, u32[]{:S(2)}) copy-start(s32[2,2]{1,0:T(2,128)} %gate_ref.1) | copy-start | bytes 52
  5.9 16.5 %copy-start = (bf16[3072,4096]{1,0:T(8,128)(2,1)S(1)}, bf16[3072,4096]{1,0:T(8,128)(2,1)}, u32[]{:S(2)}) copy-start(bf16[3072,4096]{1,0:T(8,128)(2,1)} %wg_ref.1) | copy-start | bytes 75497472
  5.9 16.5 %copy-start.5 = (bf16[3072]{0:T(1024)(128)(2,1)S(1)}, bf16[3072]{0:T(1024)(128)(2,1)}, u32[]{:S(2)}) copy-start(bf16[3072]{0:T(1024)(128)(2,1)} %gain_ref.1) | copy-start | bytes 18436
  7.1 4.7 %collective-permute-start = (bf16[4,1664]{1,0:T(4,128)(2,1)S(1)}, bf16[4,1664]{1,0:T(4,128)(2,1)S(1)}, u32[]{:S(2)}, u32[]{:S(2)}) collective-permute-start(bf16[4,1664]{1,0:T(4,128)(2,1)S(1)} %shard_map.118.one_ref), channel_id=1, source_target_pairs={{0,2},{2,0},{4,6},{6,4},{8,10},{10,8},{12,14},{14,12},{1,3},{3,1},... | collective-permute-start | bytes 39944 | tf_op jit(solution)/shard_map/ppermute | solution.py:203
  11.8 4.0 %collective-permute-start.1 = (bf16[8,1664]{1,0:T(8,128)(2,1)S(1)}, bf16[8,1664]{1,0:T(8,128)(2,1)S(1)}, u32[]{:S(2)}, u32[]{:S(2)}) collective-permute-start(bf16[8,1664]{1,0:T(8,128)(2,1)S(1)} %shard_map.119.one_ref), channel_id=1, source_target_pairs={{0,4},{2,6},{4,0},{6,2},{8,12},{10,14},{12,8},{14,10},{1,5},{3,7},... | collective-permute-start | bytes 79880 | tf_op jit(solution)/shard_map/ppermute | solution.py:203
  15.8 5.2 %collective-permute-start.2 = (bf16[16,1664]{1,0:T(8,128)(2,1)S(1)}, bf16[16,1664]{1,0:T(8,128)(2,1)S(1)}, u32[]{:S(2)}, u32[]{:S(2)}) collective-permute-start(bf16[16,1664]{1,0:T(8,128)(2,1)S(1)} %shard_map.120.one_ref), channel_id=1, source_target_pairs={{0,8},{2,10},{4,12},{6,14},{8,0},{10,2},{12,4},{14,6},{1,9},{3,11}... | collective-permute-start | bytes 159752 | tf_op jit(solution)/shard_map/ppermute | solution.py:203
  21.0 1.4 %collective-permute-start.3 = (bf16[32,1664]{1,0:T(8,128)(2,1)S(1)}, bf16[32,1664]{1,0:T(8,128)(2,1)S(1)}, u32[]{:S(2)}, u32[]{:S(2)}) collective-permute-start(bf16[32,1664]{1,0:T(8,128)(2,1)S(1)} %shard_map.121.own_ref), channel_id=1, source_target_pairs={{0,1},{1,0},{2,3},{3,2},{4,5},{5,4},{6,7},{7,6},{8,9},{9,8},{10,11... | collective-permute-start | bytes 319496 | tf_op jit(solution)/shard_map/ppermute | solution.py:203
  36.5 6.1 %collective-permute-start.4 = (bf16[32,4096]{1,0:T(8,128)(2,1)S(1)}, bf16[32,4096]{1,0:T(8,128)(2,1)S(1)}, u32[]{:S(2)}, u32[]{:S(2)}) collective-permute-start(bf16[32,4096]{1,0:T(8,128)(2,1)S(1)} %shard_map.122.hid_ref), channel_id=1, source_target_pairs={{0,1},{1,0},{2,3},{3,2},{4,5},{5,4},{6,7},{7,6},{8,9},{9,8},{10,11... | collective-permute-start | bytes 786440 | tf_op jit(solution)/shard_map/ppermute | solution.py:203
  48.6 5.3 %collective-permute-start.5 = (bf16[16,1536]{1,0:T(8,128)(2,1)S(1)}, bf16[16,1536]{1,0:T(8,128)(2,1)S(1)}, u32[]{:S(2)}, u32[]{:S(2)}) collective-permute-start(bf16[16,1536]{1,0:T(8,128)(2,1)S(1)} %slice.35), channel_id=1, source_target_pairs={{0,8},{2,10},{4,12},{6,14},{8,0},{10,2},{12,4},{14,6},{1,9},{3,11}... | collective-permute-start | bytes 147464 | tf_op jit(solution)/shard_map/ppermute | solution.py:203
  53.9 3.9 %collective-permute-start.6 = (bf16[8,1536]{1,0:T(8,128)(2,1)S(1)}, bf16[8,1536]{1,0:T(8,128)(2,1)S(1)}, u32[]{:S(2)}, u32[]{:S(2)}) collective-permute-start(bf16[8,1536]{1,0:T(8,128)(2,1)S(1)} %slice.37), channel_id=1, source_target_pairs={{0,4},{2,6},{4,0},{6,2},{8,12},{10,14},{12,8},{14,10},{1,5},{3,7},... | collective-permute-start | bytes 73736 | tf_op jit(solution)/shard_map/ppermute | solution.py:203
  57.8 3.8 %collective-permute-start.7 = (bf16[4,1536]{1,0:T(4,128)(2,1)S(1)}, bf16[4,1536]{1,0:T(4,128)(2,1)S(1)}, u32[]{:S(2)}, u32[]{:S(2)}) collective-permute-start(bf16[4,1536]{1,0:T(4,128)(2,1)S(1)} %slice.39), channel_id=1, source_target_pairs={{0,2},{2,0},{4,6},{6,4},{8,10},{10,8},{12,14},{14,12},{1,3},{3,1},... | collective-permute-start | bytes 36872 | tf_op jit(solution)/shard_map/ppermute | solution.py:203

commit v2 on v1

--- a/solution.py
+++ b/solution.py
@@ -28,7 +28,19 @@
     return jnp.concatenate([ref[idx].astype(jnp.float32) for idx in range(ref.shape[0])], axis=0)
 
 
-def attend_kernel(where_ref, pages_ref, len_ref, routes_ref, gate_ref, res_ref, q_ref, k_ref, v_ref, _w0_ref, _w1_ref, out_ref):
+def attend_kernel(*refs):
+    count = 8
+    _where, sources, buffers = refs[0], refs[1 : 1 + count], refs[-1 - count : -1]
+    out_ref, sem = refs[-2 - count], refs[-1]
+    copies = [
+        pltpu.make_async_copy(source, buffer, sem.at[idx])
+        for idx, (source, buffer) in enumerate(zip(sources, buffers))
+    ]
+    for copy in copies:
+        copy.start()
+    for copy in copies:
+        copy.wait()
+    pages_ref, len_ref, routes_ref, gate_ref, res_ref, q_ref, k_ref, v_ref = buffers
     micro, dev, half = res_ref.shape
     tok = micro * dev
     pages, page, kv_width = k_ref.shape
@@ -97,27 +109,40 @@
     out_ref[...] = jnp.concatenate([one_ref[...], two_ref[...]], axis=0)
 
 
-def fetch(w_ref, buf_ref, sem, start):
-    chunks, depth, _ = buf_ref.shape
-    copies = []
-    for idx in range(chunks):
-        copies.append(
-            pltpu.make_async_copy(
-                w_ref.at[pl.ds(pl.multiple_of(start + idx * depth, depth), depth), :],
-                buf_ref.at[idx],
-                sem.at[idx],
-            )
-        )
-        copies[-1].start()
-    return copies
+def half_copy(w_ref, out_ref, which, sem):
+    depth = out_ref.shape[0]
+    start = pl.multiple_of(which * depth, depth)
+    return pltpu.make_async_copy(w_ref.at[pl.ds(start, depth), :], out_ref, sem)
 
 
 def hidden_kernel(
-    where_ref, own_ref, other_ref, gain_ref, wg_ref, wu_ref, out_ref, x_ref, gate_ref, buf_ref, sem
+    where_ref,
+    own_ref,
+    other_ref,
+    gain_ref,
+    wg_ref,
+    wu_ref,
+    wd_ref,
+    out_ref,
+    down_ref,
+    x_ref,
+    gate_ref,
+    buf_ref,
+    sem,
+    down_sem,
 ):
-    chunks, depth, _ = buf_ref.shape
+    slots, depth, _ = buf_ref.shape
     half = own_ref.shape[1] - LANES
-    copies = fetch(wu_ref, buf_ref, sem, 0)
+    chunks = 2 * half // depth
+    copies = [
+        pltpu.make_async_copy(
+            wu_ref.at[pl.ds(idx * depth, depth), :], buf_ref.at[idx % slots], sem.at[idx % slots]
+        )
+        for idx in range(chunks)
+    ]
+    for copy in copies[:slots]:
+        copy.start()
+    down = half_copy(wd_ref, down_ref, where_ref[0], down_sem)
     is_first = where_ref[0] == 0
     own = own_ref[:, :half].astype(jnp.float32)
     other = other_ref[:, :half].astype(jnp.float32)
@@ -136,42 +161,44 @@
         copy.wait()
         part = jnp.dot(
             x_ref[:, idx * depth : (idx + 1) * depth],
-            buf_ref[idx],
+            buf_ref[idx % slots],
             preferred_element_type=jnp.float32,
         )
+        if idx + slots < chunks:
+            copies[idx + slots].start()
+        if idx + slots == chunks:
+            down.start()
         up = part if up is None else up + part
     out_ref[...] = (gate_ref[...] * up).astype(jnp.bfloat16)
-
-
-def down_own_kernel(where_ref, hid_ref, w_ref, out_ref, buf_ref, sem):
-    chunks, depth, _ = buf_ref.shape
-    copies = fetch(w_ref, buf_ref, sem, where_ref[0] * chunks * depth)
-    for idx, copy in enumerate(copies):
-        copy.wait()
-        part = jnp.dot(
-            hid_ref[:, idx * depth : (idx + 1) * depth],
-            buf_ref[idx],
-            preferred_element_type=jnp.float32,
-        )
-        out_ref[...] = part if idx == 0 else out_ref[...] + part
-
-
-def down_other_kernel(where_ref, hid_ref, part_ref, extra_ref, w_ref, out_ref, buf_ref, sem):
-    chunks, depth, _ = buf_ref.shape
-    copies = fetch(w_ref, buf_ref, sem, (1 - where_ref[0]) * chunks * depth)
-    total = part_ref[...]
-    for idx, copy in enumerate(copies):
-        copy.wait()
-        total = total + jnp.dot(
-            hid_ref[:, idx * depth : (idx + 1) * depth],
-            buf_ref[idx],
-            preferred_element_type=jnp.float32,
-        )
-    extra = extra_ref[...].astype(jnp.float32)
+    down.wait()
+
+
+def down_own_kernel(where_ref, hid_ref, own_ref, w_ref, out_ref, other_ref, sem):
+    copy = half_copy(w_ref, other_ref, 1 - where_ref[0], sem)
+    copy.start()
+    out_ref[...] = jnp.dot(hid_ref[...], own_ref[...], preferred_element_type=jnp.float32)
+    copy.wait()
+
+
+def down_other_kernel(where_ref, hid_ref, part_ref, extra_ref, w_ref, out_ref):
+    total = part_ref[...] + jnp.dot(
+        hid_ref[...], w_ref[...], preferred_element_type=jnp.float32
+    )
+    extra = extra_ref[:, -LANES:].astype(jnp.float32)
     lane = lax.broadcasted_iota(jnp.int32, extra.shape, 1)
     mine = (lane % EXPERTS == where_ref[1]) & (lane < 3 * EXPERTS)
     weight = jnp.sum(jnp.where(mine, extra, 0.0), axis=-1, keepdims=True)
     out_ref[...] = (total * weight).astype(jnp.bfloat16)
+
+
+def final_kernel(carried_ref, mine_ref, received_ref, out_ref):
+    micro, dev, half = out_ref.shape
+    total = carried_ref[:, :half].astype(jnp.float32)
+    total = total + (
+        mine_ref[: micro * dev].astype(jnp.float32) + received_ref[...].astype(jnp.float32)
+    )
+    for idx in range(micro):
+        out_ref[idx] = total[idx * dev : (idx + 1) * dev].astype(jnp.bfloat16)
 
 
 SMEM = pl.BlockSpec(memory_space=pltpu.SMEM)
@@ -184,7 +211,7 @@
         kernel,
         out_shape=out_shape,
         in_specs=in_specs,
-        out_specs=jax.tree.map(lambda _: VMEM, out_shape),
+        out_specs=[VMEM] * len(out_shape) if isinstance(out_shape, tuple) else VMEM,
         scratch_shapes=scratch,
         compiler_params=pltpu.CompilerParams(vmem_limit_bytes=limit),
     )(*args)
@@ -225,22 +252,17 @@
     small = SMALL + 64 * rows * half
     width = w_gate.shape[1]
     where = jnp.stack([lax.axis_index("tp"), lax.axis_index("side") // span]).astype(jnp.int32)
+    small_args = (page_table, lengths, routes, gate_fixed)
+    large_args = (residual, queries, key_cache, value_cache)
     local = call(
         attend_kernel,
         jax.ShapeDtypeStruct((tok, half + LANES), jnp.bfloat16),
-        [SMEM] * 5 + [VMEM] * 4 + [ANY] * 2,
+        [SMEM] + [ANY] * 10,
+        (where, *[in_hbm(arg) for arg in (*small_args, *large_args, w_gate, w_up)]),
         (
-            where,
-            page_table,
-            lengths,
-            routes,
-            gate_fixed,
-            residual,
-            queries,
-            key_cache,
-            value_cache,
-            in_hbm(w_gate),
-            in_hbm(w_up),
+            *[pltpu.SMEM(arg.shape, arg.dtype) for arg in small_args],
+            *[pltpu.VMEM(arg.shape, arg.dtype) for arg in large_args],
+            pltpu.SemaphoreType.DMA((8,)),
         ),
     )
     gathered = local
@@ -255,50 +277,50 @@
             limit=small,
         )
     other = swap(gathered, "tp", 1)
-    up_chunks = 6
-    hidden = call(
+    slots, depth = 6, 256
+    held = pltpu.VMEM((width, half), w_down.dtype)
+    hidden, down_own = call(
         hidden_kernel,
-        jax.ShapeDtypeStruct((rows, width), jnp.bfloat16),
-        [SMEM] + [VMEM] * 4 + [ANY],
-        (where, gathered, other, norm_gain, in_vmem(w_gate), in_hbm(w_up)),
+        (jax.ShapeDtypeStruct((rows, width), jnp.bfloat16), held),
+        [SMEM] + [VMEM] * 4 + [ANY] * 2,
+        (where, gathered, other, norm_gain, in_vmem(w_gate), in_hbm(w_up), in_hbm(w_down)),
         (
             pltpu.VMEM((rows, 2 * half), jnp.bfloat16),
             pltpu.VMEM((rows, width), jnp.float32),
-            pltpu.VMEM((up_chunks, 2 * half // up_chunks, width), jnp.bfloat16),
-            pltpu.SemaphoreType.DMA((up_chunks,)),
+            pltpu.VMEM((slots, depth, width), jnp.bfloat16),
+            pltpu.SemaphoreType.DMA((slots,)),
+            pltpu.SemaphoreType.DMA,
         ),
-        small + w_up.size * w_up.dtype.itemsize,
+        small + slots * depth * width * 2,
     )
     hidden_other = swap(hidden, "tp", 1)
-    chunks = max(1, width // 1024)
-    stream = (
-        pltpu.VMEM((chunks, width // chunks, half), jnp.bfloat16),
-        pltpu.SemaphoreType.DMA((chunks,)),
-    )
-    part = call(
+    part, down_other = call(
         down_own_kernel,
-        jax.ShapeDtypeStruct((rows, half), jnp.float32),
-        [SMEM, VMEM, ANY],
-        (where, hidden, in_hbm(w_down)),
-        stream,
-        small + w_down.size * w_down.dtype.itemsize // 2,
+        (jax.ShapeDtypeStruct((rows, half), jnp.float32), held),
+        [SMEM] + [VMEM] * 2 + [ANY],
+        (where, hidden, in_vmem(down_own), in_hbm(w_down)),
+        (pltpu.SemaphoreType.DMA,),
+        small,
     )
     sent = call(
         down_other_kernel,
         jax.ShapeDtypeStruct((rows, half), jnp.bfloat16),
-        [SMEM] + [VMEM] * 3 + [ANY],
-        (where, hidden_other, part, gathered[:, half:], in_hbm(w_down)),
-        stream,
-        small + w_down.size * w_down.dtype.itemsize // 2,
+        [SMEM] + [VMEM] * 4,
+        (where, hidden_other, part, gathered, in_vmem(down_other)),
+        limit=small,
     )
     for mask in reversed(masks):
         count = sent.shape[0] // 2
         received = swap(sent[count:], "side", mask)
-        sent = sent[:count].astype(jnp.float32) + received.astype(jnp.float32)
         if mask > 1:
+            sent = sent[:count].astype(jnp.float32) + received.astype(jnp.float32)
             sent = sent.astype(jnp.bfloat16)
-    carried = local[:, :half].astype(jnp.float32)
-    return (carried + sent).astype(jnp.bfloat16).reshape(residual.shape)
+    return call(
+        final_kernel,
+        jax.ShapeDtypeStruct(residual.shape, residual.dtype),
+        [VMEM] * 3,
+        (local, sent, received),
+    )
 
 
 def solution(mesh):

time: 62.6 us -> 58.9 us (0.941)
  local copies, waits for them, and re-layouts: 6.45 us -> 0.03 us
  Pallas kernels: 27.1 us -> 30.1 us
    unnamed x20 -> x4, local copies, waits for them, and re-layouts: 5.82 us -> 0.01 us
    pallas_call x7 -> x8, Pallas kernels: 27.1 us -> 30.1 us  [call(): pl.pallas_call(kernel, out_shape=out_shape, in_specs=in_specs, out_specs=...]
  transfers between devices with their start and end apart: 8 -> 8, of which waited for: 7 -> 7; matrix products, arithmetic and copies ran while one was open for 0% -> 0% of each run, Pallas kernels for 9% -> 12%
where the time goes in v2:
time: 58.9 us; the launch traced here: 58.7 us
  Pallas kernels  30.1 us (51%)
  starting transfers between devices  15.3 us (26%)
  waiting for transfers between devices  13.1 us (22%)
    pallas_call x8, Pallas kernels, call(): pl.pallas_call(kernel, out_shape=out_shape, in_specs=in_specs, out_specs=...  30.1 us
    ppermute x8, starting transfers between devices, swap(): return lax.ppermute(array, axis, [(i, i ^ mask) for i in range(size)])  15.3 us
    ppermute x8, waiting for transfers between devices, swap(): return lax.ppermute(array, axis, [(i, i ^ mask) for i in range(size)])  13.1 us
  transfers between devices with their start and end apart: 8, of which 7 were waited for; matrix products, arithmetic and copies ran while one was open for 0% of the time, Pallas kernels for 12%

profile of v2, /device:TPU:0, one launch (start us, length us, event | category | flops | bytes accessed | tf_op | source)
XLA Modules:
  0.0 58.7 jit_solution(8999501560799378737)
XLA Ops:
  0.0 0.1 pad_add_fusion.refs_0_.where_ref
  0.1 2.3 %shard_map.118.one_ref.carried_ref = bf16[4,1664]{1,0:T(4,128)(2,1)S(1)} custom-call(s32[2]{0:T(128)S(1)} %pad_add_fusion.refs_0_.where_ref, s32[2,2,2]{2,1,0:T(2,128)} %refs_1_.1, s32[2,2]{1,0:T(2,128)} %refs_2_.1, s32[2,2,2]{2,1,0:T(2,128)} %refs_3_.1, s32[2,2]{1,0:T(2,128)} %refs_4_.1, bf16[2,2,1536]{2,1,0:T(2,128)(2,1)} %refs_5_.1, ...), custom_call_target="tpu_custom_call" | custom-call | tf_op jit(solution)/shard_map/pallas_call | solution.py:210
  2.4 3.0 %collective-permute-start = (bf16[4,1664]{1,0:T(4,128)(2,1)S(1)}, bf16[4,1664]{1,0:T(4,128)(2,1)S(1)}, u32[]{:S(2)}, u32[]{:S(2)}) collective-permute-start(bf16[4,1664]{1,0:T(4,128)(2,1)S(1)} %shard_map.118.one_ref.carried_ref), channel_id=1, source_target_pairs={{0,2},{2,0},{4,6},{6,4},{8,10},{10,8},{12,14},{14,12},{1,3},{3,1},... | collective-permute-start | bytes 39944 | tf_op jit(solution)/shard_map/ppermute | solution.py:230
  5.4 1.7 %collective-permute-done.two_ref = bf16[4,1664]{1,0:T(4,128)(2,1)S(1)} collective-permute-done((bf16[4,1664]{1,0:T(4,128)(2,1)S(1)}, bf16[4,1664]{1,0:T(4,128)(2,1)S(1)}, u32[]{:S(2)}, u32[]{:S(2)}) %collective-permute-start) | collective-permute-done | bytes 13344 | tf_op jit(solution)/shard_map/ppermute | solution.py:230
  7.1 2.2 %collective-permute-start.1 = (bf16[8,1664]{1,0:T(8,128)(2,1)S(1)}, bf16[8,1664]{1,0:T(8,128)(2,1)S(1)}, u32[]{:S(2)}, u32[]{:S(2)}) collective-permute-start(bf16[8,1664]{1,0:T(8,128)(2,1)S(1)} %shard_map.119.one_ref), channel_id=1, source_target_pairs={{0,4},{2,6},{4,0},{6,2},{8,12},{10,14},{12,8},{14,10},{1,5},{3,7},... | collective-permute-start | bytes 79880 | tf_op jit(solution)/shard_map/ppermute | solution.py:230
  9.3 1.8 %collective-permute-done.1.two_ref = bf16[8,1664]{1,0:T(8,128)(2,1)S(1)} collective-permute-done((bf16[8,1664]{1,0:T(8,128)(2,1)S(1)}, bf16[8,1664]{1,0:T(8,128)(2,1)S(1)}, u32[]{:S(2)}, u32[]{:S(2)}) %collective-permute-start.1) | collective-permute-done | bytes 26656 | tf_op jit(solution)/shard_map/ppermute | solution.py:230
  11.1 3.1 %collective-permute-start.2 = (bf16[16,1664]{1,0:T(8,128)(2,1)S(1)}, bf16[16,1664]{1,0:T(8,128)(2,1)S(1)}, u32[]{:S(2)}, u32[]{:S(2)}) collective-permute-start(bf16[16,1664]{1,0:T(8,128)(2,1)S(1)} %shard_map.120.one_ref), channel_id=1, source_target_pairs={{0,8},{2,10},{4,12},{6,14},{8,0},{10,2},{12,4},{14,6},{1,9},{3,11}... | collective-permute-start | bytes 159752 | tf_op jit(solution)/shard_map/ppermute | solution.py:230
  14.2 2.1 %collective-permute-done.2.two_ref = bf16[16,1664]{1,0:T(8,128)(2,1)S(1)} collective-permute-done((bf16[16,1664]{1,0:T(8,128)(2,1)S(1)}, bf16[16,1664]{1,0:T(8,128)(2,1)S(1)}, u32[]{:S(2)}, u32[]{:S(2)}) %collective-permute-start.2) | collective-permute-done | bytes 53280 | tf_op jit(solution)/shard_map/ppermute | solution.py:230
  16.4 0.1 collective-permute-start.3
  16.4 1.3 %collective-permute-done.3.other_ref = bf16[32,1664]{1,0:T(8,128)(2,1)S(1)} collective-permute-done((bf16[32,1664]{1,0:T(8,128)(2,1)S(1)}, bf16[32,1664]{1,0:T(8,128)(2,1)S(1)}, u32[]{:S(2)}, u32[]{:S(2)}) %collective-permute-start.3) | collective-permute-done | bytes 106528 | tf_op jit(solution)/shard_map/ppermute | solution.py:230
  17.7 0.0 copy-done
  17.7 0.0 copy-done.1
  17.7 17.1 %shard_map.122 = (bf16[32,4096]{1,0:T(8,128)(2,1)S(1)}, bf16[4096,1536]{1,0:T(8,128)(2,1)S(1)}) custom-call(s32[2]{0:T(128)S(1)} %pad_add_fusion.refs_0_.where_ref, bf16[32,1664]{1,0:T(8,128)(2,1)S(1)} %shard_map.121.own_ref.extra_ref, bf16[32,1664]{1,0:T(8,128)(2,1)S(1)} %collective-permute-done.3.other_ref, bf16[3072]{0:T(1024)(128)(2,1)S(1)} %copy-done.1, ...), custom_call_target="tpu_custom_call" | custom-call | tf_op jit(solution)/shard_map/pallas_call | solution.py:210
  34.9 0.2 collective-permute-start.4
  35.1 7.2 %shard_map.123 = (f32[32,1536]{1,0:T(8,128)S(1)}, bf16[4096,1536]{1,0:T(8,128)(2,1)S(1)}) custom-call(s32[2]{0:T(128)S(1)} %pad_add_fusion.refs_0_.where_ref, bf16[32,4096]{1,0:T(8,128)(2,1)S(1)} %get-tuple-element.9.hid_ref, bf16[4096,1536]{1,0:T(8,128)(2,1)S(1)} %get-tuple-element.10.own_ref, bf16[8192,1536]{1,0:T(8,128)(2,1)} %w_ref.1), custom_call_target="tpu_custom_call" | custom-call | tf_op jit(solution)/shard_map/pallas_call | solution.py:210
  42.3 0.0 collective-permute-done.4.hid_ref
  42.3 2.8 %shard_map.124 = bf16[32,1536]{1,0:T(8,128)(2,1)S(1)} custom-call(s32[2]{0:T(128)S(1)} %pad_add_fusion.refs_0_.where_ref, bf16[32,4096]{1,0:T(8,128)(2,1)S(1)} %collective-permute-done.4.hid_ref, f32[32,1536]{1,0:T(8,128)S(1)} %get-tuple-element.11.part_ref, bf16[32,1664]{1,0:T(8,128)(2,1)S(1)} %shard_map.121.own_ref.extra_ref, ...), custom_call_target="tpu_custom_call" | custom-call | tf_op jit(solution)/shard_map/pallas_call | solution.py:210
  45.1 3.0 %collective-permute-start.5 = (bf16[16,1536]{1,0:T(8,128)(2,1)S(1)}, bf16[16,1536]{1,0:T(8,128)(2,1)S(1)}, u32[]{:S(2)}, u32[]{:S(2)}) collective-permute-start(bf16[16,1536]{1,0:T(8,128)(2,1)S(1)} %slice.21), channel_id=1, source_target_pairs={{0,8},{2,10},{4,12},{6,14},{8,0},{10,2},{12,4},{14,6},{1,9},{3,11}... | collective-permute-start | bytes 147464 | tf_op jit(solution)/shard_map/ppermute | solution.py:230
  48.2 2.2 %collective-permute-done.5 = bf16[16,1536]{1,0:T(8,128)(2,1)S(1)} collective-permute-done((bf16[16,1536]{1,0:T(8,128)(2,1)S(1)}, bf16[16,1536]{1,0:T(8,128)(2,1)S(1)}, u32[]{:S(2)}, u32[]{:S(2)}) %collective-permute-start.5) | collective-permute-done | bytes 49184 | tf_op jit(solution)/shard_map/ppermute | solution.py:230
  50.4 2.0 %collective-permute-start.6 = (bf16[8,1536]{1,0:T(8,128)(2,1)S(1)}, bf16[8,1536]{1,0:T(8,128)(2,1)S(1)}, u32[]{:S(2)}, u32[]{:S(2)}) collective-permute-start(bf16[8,1536]{1,0:T(8,128)(2,1)S(1)} %slice.23), channel_id=1, source_target_pairs={{0,4},{2,6},{4,0},{6,2},{8,12},{10,14},{12,8},{14,10},{1,5},{3,7},... | collective-permute-start | bytes 73736 | tf_op jit(solution)/shard_map/ppermute | solution.py:230
  52.5 1.8 %collective-permute-done.6 = bf16[8,1536]{1,0:T(8,128)(2,1)S(1)} collective-permute-done((bf16[8,1536]{1,0:T(8,128)(2,1)S(1)}, bf16[8,1536]{1,0:T(8,128)(2,1)S(1)}, u32[]{:S(2)}, u32[]{:S(2)}) %collective-permute-start.6) | collective-permute-done | bytes 24608 | tf_op jit(solution)/shard_map/ppermute | solution.py:230
  54.4 1.7 %collective-permute-start.7 = (bf16[4,1536]{1,0:T(4,128)(2,1)S(1)}, bf16[4,1536]{1,0:T(4,128)(2,1)S(1)}, u32[]{:S(2)}, u32[]{:S(2)}) collective-permute-start(bf16[4,1536]{1,0:T(4,128)(2,1)S(1)} %slice.24), channel_id=1, source_target_pairs={{0,2},{2,0},{4,6},{6,4},{8,10},{10,8},{12,14},{14,12},{1,3},{3,1},... | collective-permute-start | bytes 36872 | tf_op jit(solution)/shard_map/ppermute | solution.py:230
  56.0 2.1 %collective-permute-done.7.received_ref = bf16[4,1536]{1,0:T(4,128)(2,1)S(1)} collective-permute-done((bf16[4,1536]{1,0:T(4,128)(2,1)S(1)}, bf16[4,1536]{1,0:T(4,128)(2,1)S(1)}, u32[]{:S(2)}, u32[]{:S(2)}) %collective-permute-start.7) | collective-permute-done | bytes 12320 | tf_op jit(solution)/shard_map/ppermute | solution.py:230
  58.1 0.6 %shard_map.125 = bf16[2,2,1536]{2,1,0:T(2,128)(2,1)} custom-call(bf16[4,1664]{1,0:T(4,128)(2,1)S(1)} %shard_map.118.one_ref.carried_ref, bf16[8,1536]{1,0:T(8,128)(2,1)S(1)} %add_convert_fusion.1.mine_ref, bf16[4,1536]{1,0:T(4,128)(2,1)S(1)} %collective-permute-done.7.received_ref), custom_call_target="tpu_custom_call" | custom-call | tf_op jit(solution)/shard_map/pallas_call | solution.py:210
  (10 shorter events, 0.1 us)
Async XLA Ops:
  0.1 17.7 %copy-start = (bf16[3072,4096]{1,0:T(8,128)(2,1)S(1)}, bf16[3072,4096]{1,0:T(8,128)(2,1)}, u32[]{:S(2)}) copy-start(bf16[3072,4096]{1,0:T(8,128)(2,1)} %wg_ref.1) | copy-start | bytes 75497472
  0.1 17.7 %copy-start.1 = (bf16[3072]{0:T(1024)(128)(2,1)S(1)}, bf16[3072]{0:T(1024)(128)(2,1)}, u32[]{:S(2)}) copy-start(bf16[3072]{0:T(1024)(128)(2,1)} %gain_ref.1) | copy-start | bytes 18436
  2.4 4.7 %collective-permute-start = (bf16[4,1664]{1,0:T(4,128)(2,1)S(1)}, bf16[4,1664]{1,0:T(4,128)(2,1)S(1)}, u32[]{:S(2)}, u32[]{:S(2)}) collective-permute-start(bf16[4,1664]{1,0:T(4,128)(2,1)S(1)} %shard_map.118.one_ref.carried_ref), channel_id=1, source_target_pairs={{0,2},{2,0},{4,6},{6,4},{8,10},{10,8},{12,14},{14,12},{1,3},{3,1},... | collective-permute-start | bytes 39944 | tf_op jit(solution)/shard_map/ppermute | solution.py:230
  7.1 4.0 %collective-permute-start.1 = (bf16[8,1664]{1,0:T(8,128)(2,1)S(1)}, bf16[8,1664]{1,0:T(8,128)(2,1)S(1)}, u32[]{:S(2)}, u32[]{:S(2)}) collective-permute-start(bf16[8,1664]{1,0:T(8,128)(2,1)S(1)} %shard_map.119.one_ref), channel_id=1, source_target_pairs={{0,4},{2,6},{4,0},{6,2},{8,12},{10,14},{12,8},{14,10},{1,5},{3,7},... | collective-permute-start | bytes 79880 | tf_op jit(solution)/shard_map/ppermute | solution.py:230
  11.1 5.2 %collective-permute-start.2 = (bf16[16,1664]{1,0:T(8,128)(2,1)S(1)}, bf16[16,1664]{1,0:T(8,128)(2,1)S(1)}, u32[]{:S(2)}, u32[]{:S(2)}) collective-permute-start(bf16[16,1664]{1,0:T(8,128)(2,1)S(1)} %shard_map.120.one_ref), channel_id=1, source_target_pairs={{0,8},{2,10},{4,12},{6,14},{8,0},{10,2},{12,4},{14,6},{1,9},{3,11}... | collective-permute-start | bytes 159752 | tf_op jit(solution)/shard_map/ppermute | solution.py:230
  16.4 1.4 %collective-permute-start.3 = (bf16[32,1664]{1,0:T(8,128)(2,1)S(1)}, bf16[32,1664]{1,0:T(8,128)(2,1)S(1)}, u32[]{:S(2)}, u32[]{:S(2)}) collective-permute-start(bf16[32,1664]{1,0:T(8,128)(2,1)S(1)} %shard_map.121.own_ref.extra_ref), channel_id=1, source_target_pairs={{0,1},{1,0},{2,3},{3,2},{4,5},{5,4},{6,7},{7,6},{8,9},{9,8},{10,11... | collective-permute-start | bytes 319496 | tf_op jit(solution)/shard_map/ppermute | solution.py:230
  34.9 7.4 %collective-permute-start.4 = (bf16[32,4096]{1,0:T(8,128)(2,1)S(1)}, bf16[32,4096]{1,0:T(8,128)(2,1)S(1)}, u32[]{:S(2)}, u32[]{:S(2)}) collective-permute-start(bf16[32,4096]{1,0:T(8,128)(2,1)S(1)} %get-tuple-element.9.hid_ref), channel_id=1, source_target_pairs={{0,1},{1,0},{2,3},{3,2},{4,5},{5,4},{6,7},{7,6},{8,9},{9,8},{10,11... | collective-permute-start | bytes 786440 | tf_op jit(solution)/shard_map/ppermute | solution.py:230
  45.1 5.3 %collective-permute-start.5 = (bf16[16,1536]{1,0:T(8,128)(2,1)S(1)}, bf16[16,1536]{1,0:T(8,128)(2,1)S(1)}, u32[]{:S(2)}, u32[]{:S(2)}) collective-permute-start(bf16[16,1536]{1,0:T(8,128)(2,1)S(1)} %slice.21), channel_id=1, source_target_pairs={{0,8},{2,10},{4,12},{6,14},{8,0},{10,2},{12,4},{14,6},{1,9},{3,11}... | collective-permute-start | bytes 147464 | tf_op jit(solution)/shard_map/ppermute | solution.py:230
  50.4 3.9 %collective-permute-start.6 = (bf16[8,1536]{1,0:T(8,128)(2,1)S(1)}, bf16[8,1536]{1,0:T(8,128)(2,1)S(1)}, u32[]{:S(2)}, u32[]{:S(2)}) collective-permute-start(bf16[8,1536]{1,0:T(8,128)(2,1)S(1)} %slice.23), channel_id=1, source_target_pairs={{0,4},{2,6},{4,0},{6,2},{8,12},{10,14},{12,8},{14,10},{1,5},{3,7},... | collective-permute-start | bytes 73736 | tf_op jit(solution)/shard_map/ppermute | solution.py:230
  54.4 3.8 %collective-permute-start.7 = (bf16[4,1536]{1,0:T(4,128)(2,1)S(1)}, bf16[4,1536]{1,0:T(4,128)(2,1)S(1)}, u32[]{:S(2)}, u32[]{:S(2)}) collective-permute-start(bf16[4,1536]{1,0:T(4,128)(2,1)S(1)} %slice.24), channel_id=1, source_target_pairs={{0,2},{2,0},{4,6},{6,4},{8,10},{10,8},{12,14},{14,12},{1,3},{3,1},... | collective-permute-start | bytes 36872 | tf_op jit(solution)/shard_map/ppermute | solution.py:230

commit v3 on v2

--- a/solution.py
+++ b/solution.py
@@ -13,6 +13,7 @@
 EPS = 1e-05
 GATE_ONE = 65536.0
 LANES = 128
+DOWN_TILES = 3
 SMALL = 2 << 20
 
 
@@ -131,18 +132,19 @@
     sem,
     down_sem,
 ):
-    slots, depth, _ = buf_ref.shape
+    slots, _, tile = buf_ref.shape
     half = own_ref.shape[1] - LANES
-    chunks = 2 * half // depth
-    copies = [
-        pltpu.make_async_copy(
-            wu_ref.at[pl.ds(idx * depth, depth), :], buf_ref.at[idx % slots], sem.at[idx % slots]
-        )
-        for idx in range(chunks)
-    ]
-    for copy in copies[:slots]:
-        copy.start()
+    chunks = out_ref.shape[1] // tile
     down = half_copy(wd_ref, down_ref, where_ref[0], down_sem)
+
+    def columns(idx):
+        return pl.ds(pl.multiple_of(idx * tile, tile), tile)
+
+    def up_copy(idx):
+        slot = lax.rem(idx, slots)
+        return pltpu.make_async_copy(wu_ref.at[:, columns(idx)], buf_ref.at[slot], sem.at[slot])
+
+    lax.fori_loop(0, slots, lambda idx, _: up_copy(idx).start(), None)
     is_first = where_ref[0] == 0
     own = own_ref[:, :half].astype(jnp.float32)
     other = other_ref[:, :half].astype(jnp.float32)
@@ -154,29 +156,44 @@
     gain = gain_ref[...].astype(jnp.float32).reshape(1, -1)
     x_ref[:, :half] = (left * inv_rms * gain[:, :half]).astype(jnp.bfloat16)
     x_ref[:, half:] = (right * inv_rms * gain[:, half:]).astype(jnp.bfloat16)
-    gate = jnp.dot(x_ref[...], wg_ref[...], preferred_element_type=jnp.float32)
-    gate_ref[...] = gate / (1.0 + jnp.exp(-gate))
-    up = None
-    for idx, copy in enumerate(copies):
-        copy.wait()
-        part = jnp.dot(
-            x_ref[:, idx * depth : (idx + 1) * depth],
-            buf_ref[idx % slots],
-            preferred_element_type=jnp.float32,
+
+    def gate_step(idx, _):
+        at = columns(idx)
+        gate = jnp.dot(x_ref[...], wg_ref[:, at], preferred_element_type=jnp.float32)
+        gate_ref[:, at] = gate / (1.0 + jnp.exp(-gate))
+
+    lax.fori_loop(0, chunks, gate_step, None)
+
+    def up_step(idx, _):
+        up_copy(idx).wait()
+        up = jnp.dot(
+            x_ref[...], buf_ref[lax.rem(idx, slots)], preferred_element_type=jnp.float32
         )
-        if idx + slots < chunks:
-            copies[idx + slots].start()
-        if idx + slots == chunks:
+        at = columns(idx)
+        out_ref[:, at] = (gate_ref[:, at] * up).astype(jnp.bfloat16)
+
+        @pl.when(idx + slots < chunks)
+        def _():
+            up_copy(idx + slots).start()
+
+        @pl.when(idx + slots == chunks)
+        def _():
             down.start()
-        up = part if up is None else up + part
-    out_ref[...] = (gate_ref[...] * up).astype(jnp.bfloat16)
+
+    lax.fori_loop(0, chunks, up_step, None)
     down.wait()
 
 
 def down_own_kernel(where_ref, hid_ref, own_ref, w_ref, out_ref, other_ref, sem):
+    tile = out_ref.shape[1] // DOWN_TILES
     copy = half_copy(w_ref, other_ref, 1 - where_ref[0], sem)
     copy.start()
-    out_ref[...] = jnp.dot(hid_ref[...], own_ref[...], preferred_element_type=jnp.float32)
+
+    def step(idx, _):
+        at = pl.ds(pl.multiple_of(idx * tile, tile), tile)
+        out_ref[:, at] = jnp.dot(hid_ref[...], own_ref[:, at], preferred_element_type=jnp.float32)
+
+    lax.fori_loop(0, DOWN_TILES, step, None)
     copy.wait()
 
 
@@ -277,7 +294,8 @@
             limit=small,
         )
     other = swap(gathered, "tp", 1)
-    slots, depth = 6, 256
+    tile = math.gcd(width, 512)
+    slots = min(width // tile, 6)
     held = pltpu.VMEM((width, half), w_down.dtype)
     hidden, down_own = call(
         hidden_kernel,
@@ -287,11 +305,11 @@
         (
             pltpu.VMEM((rows, 2 * half), jnp.bfloat16),
             pltpu.VMEM((rows, width), jnp.float32),
-            pltpu.VMEM((slots, depth, width), jnp.bfloat16),
+            pltpu.VMEM((slots, 2 * half, tile), jnp.bfloat16),
             pltpu.SemaphoreType.DMA((slots,)),
             pltpu.SemaphoreType.DMA,
         ),
-        small + slots * depth * width * 2,
+        small + slots * half * tile * 4,
     )
     hidden_other = swap(hidden, "tp", 1)
     part, down_other = call(

time: 58.9 us -> 56 us (0.951)
  Pallas kernels: 30.1 us -> 25.5 us
  local copies, waits for them, and re-layouts: 0.03 us -> 1.63 us
    pallas_call x8, Pallas kernels: 30.1 us -> 25.5 us  [call(): pl.pallas_call(kernel, out_shape=out_shape, in_specs=in_specs, out_specs=...]
    unnamed x4 -> x14, local copies, waits for them, and re-layouts: 0.01 us -> 1.61 us
  transfers between devices with their start and end apart: 8 -> 8, of which waited for: 7 -> 7; matrix products, arithmetic and copies ran while one was open for 0% -> 0% of each run, Pallas kernels for 12% -> 9%
where the time goes in v3:
time: 56 us; the launch traced here: 55.8 us
  Pallas kernels  25.5 us (46%)
  starting transfers between devices  15.3 us (27%)
  waiting for transfers between devices  13.1 us (23%)
  local copies, waits for them, and re-layouts  1.63 us (3%)
    pallas_call x8, Pallas kernels, call(): pl.pallas_call(kernel, out_shape=out_shape, in_specs=in_specs, out_specs=...  25.5 us
    ppermute x8, starting transfers between devices, swap(): return lax.ppermute(array, axis, [(i, i ^ mask) for i in range(size)])  15.3 us
    ppermute x8, waiting for transfers between devices, swap(): return lax.ppermute(array, axis, [(i, i ^ mask) for i in range(size)])  13.1 us
    unnamed x14, local copies, waits for them, and re-layouts  1.61 us
  transfers between devices with their start and end apart: 8, of which 7 were waited for; matrix products, arithmetic and copies ran while one was open for 0% of the time, Pallas kernels for 9%

profile of v3, /device:TPU:0, one launch (start us, length us, event | category | flops | bytes accessed | tf_op | source)
XLA Modules:
  0.0 55.8 jit_solution(2784003962087911010)
XLA Ops:
  0.0 0.1 pad_add_fusion.refs_0_.where_ref
  0.1 2.3 %shard_map.118.one_ref.carried_ref = bf16[4,1664]{1,0:T(4,128)(2,1)S(1)} custom-call(s32[2]{0:T(128)S(1)} %pad_add_fusion.refs_0_.where_ref, s32[2,2,2]{2,1,0:T(2,128)} %refs_1_.1, s32[2,2]{1,0:T(2,128)} %refs_2_.1, s32[2,2,2]{2,1,0:T(2,128)} %refs_3_.1, s32[2,2]{1,0:T(2,128)} %refs_4_.1, bf16[2,2,1536]{2,1,0:T(2,128)(2,1)} %refs_5_.1, ...), custom_call_target="tpu_custom_call" | custom-call | tf_op jit(solution)/shard_map/pallas_call | solution.py:227
  2.4 3.0 %collective-permute-start = (bf16[4,1664]{1,0:T(4,128)(2,1)S(1)}, bf16[4,1664]{1,0:T(4,128)(2,1)S(1)}, u32[]{:S(2)}, u32[]{:S(2)}) collective-permute-start(bf16[4,1664]{1,0:T(4,128)(2,1)S(1)} %shard_map.118.one_ref.carried_ref), channel_id=1, source_target_pairs={{0,2},{2,0},{4,6},{6,4},{8,10},{10,8},{12,14},{14,12},{1,3},{3,1},... | collective-permute-start | bytes 39944 | tf_op jit(solution)/shard_map/ppermute | solution.py:247
  5.4 1.7 %collective-permute-done.two_ref = bf16[4,1664]{1,0:T(4,128)(2,1)S(1)} collective-permute-done((bf16[4,1664]{1,0:T(4,128)(2,1)S(1)}, bf16[4,1664]{1,0:T(4,128)(2,1)S(1)}, u32[]{:S(2)}, u32[]{:S(2)}) %collective-permute-start) | collective-permute-done | bytes 13344 | tf_op jit(solution)/shard_map/ppermute | solution.py:247
  7.1 2.2 %collective-permute-start.1 = (bf16[8,1664]{1,0:T(8,128)(2,1)S(1)}, bf16[8,1664]{1,0:T(8,128)(2,1)S(1)}, u32[]{:S(2)}, u32[]{:S(2)}) collective-permute-start(bf16[8,1664]{1,0:T(8,128)(2,1)S(1)} %shard_map.119.one_ref), channel_id=1, source_target_pairs={{0,4},{2,6},{4,0},{6,2},{8,12},{10,14},{12,8},{14,10},{1,5},{3,7},... | collective-permute-start | bytes 79880 | tf_op jit(solution)/shard_map/ppermute | solution.py:247
  9.3 1.8 %collective-permute-done.1.two_ref = bf16[8,1664]{1,0:T(8,128)(2,1)S(1)} collective-permute-done((bf16[8,1664]{1,0:T(8,128)(2,1)S(1)}, bf16[8,1664]{1,0:T(8,128)(2,1)S(1)}, u32[]{:S(2)}, u32[]{:S(2)}) %collective-permute-start.1) | collective-permute-done | bytes 26656 | tf_op jit(solution)/shard_map/ppermute | solution.py:247
  11.1 3.1 %collective-permute-start.2 = (bf16[16,1664]{1,0:T(8,128)(2,1)S(1)}, bf16[16,1664]{1,0:T(8,128)(2,1)S(1)}, u32[]{:S(2)}, u32[]{:S(2)}) collective-permute-start(bf16[16,1664]{1,0:T(8,128)(2,1)S(1)} %shard_map.120.one_ref), channel_id=1, source_target_pairs={{0,8},{2,10},{4,12},{6,14},{8,0},{10,2},{12,4},{14,6},{1,9},{3,11}... | collective-permute-start | bytes 159752 | tf_op jit(solution)/shard_map/ppermute | solution.py:247
  14.2 2.1 %collective-permute-done.2.two_ref = bf16[16,1664]{1,0:T(8,128)(2,1)S(1)} collective-permute-done((bf16[16,1664]{1,0:T(8,128)(2,1)S(1)}, bf16[16,1664]{1,0:T(8,128)(2,1)S(1)}, u32[]{:S(2)}, u32[]{:S(2)}) %collective-permute-start.2) | collective-permute-done | bytes 53280 | tf_op jit(solution)/shard_map/ppermute | solution.py:247
  16.4 0.0 copy-start.5
  16.4 0.1 collective-permute-start.3
  16.5 1.3 %collective-permute-done.3.other_ref = bf16[32,1664]{1,0:T(8,128)(2,1)S(1)} collective-permute-done((bf16[32,1664]{1,0:T(8,128)(2,1)S(1)}, bf16[32,1664]{1,0:T(8,128)(2,1)S(1)}, u32[]{:S(2)}, u32[]{:S(2)}) %collective-permute-start.3) | collective-permute-done | bytes 106528 | tf_op jit(solution)/shard_map/ppermute | solution.py:247
  17.8 0.6 %copy-done.6 = bf16[32,1664]{1,0:T(8,128)(2,1)} copy-done((bf16[32,1664]{1,0:T(8,128)(2,1)}, bf16[32,1664]{1,0:T(8,128)(2,1)S(1)}, u32[]{:S(2)}) %copy-start.6) | copy-done | bytes 106520
  18.4 14.6 %shard_map.122 = (bf16[32,4096]{1,0:T(8,128)(2,1)}, bf16[4096,1536]{1,0:T(8,128)(2,1)S(1)}) custom-call(s32[2]{0:T(128)} %copy-done.4, bf16[32,1664]{1,0:T(8,128)(2,1)} %copy-done.1, bf16[32,1664]{1,0:T(8,128)(2,1)} %copy-done.6, bf16[3072]{0:T(1024)(128)(2,1)} %gain_ref.1, bf16[3072,4096]{1,0:T(8,128)(2,1)S(1)} %copy-done, bf16[3072,4096]{1,0:T(8,128)(2,1)} %wu_ref.1, ...), custom_call_target="tpu_custom_call" | custom-call | tf_op jit(solution)/shard_map/pallas_call | solution.py:227
  33.0 0.2 collective-permute-start.4
  33.2 0.9 %copy-done.3 = bf16[32,4096]{1,0:T(8,128)(2,1)S(1)} copy-done((bf16[32,4096]{1,0:T(8,128)(2,1)S(1)}, bf16[32,4096]{1,0:T(8,128)(2,1)}, u32[]{:S(2)}) %copy-start.3) | copy-done | bytes 262168
  34.2 5.1 %shard_map.123 = (f32[32,1536]{1,0:T(8,128)S(1)}, bf16[4096,1536]{1,0:T(8,128)(2,1)S(1)}) custom-call(s32[2]{0:T(128)S(1)} %copy-done.5, bf16[32,4096]{1,0:T(8,128)(2,1)S(1)} %copy-done.3, bf16[4096,1536]{1,0:T(8,128)(2,1)S(1)} %get-tuple-element.10.own_ref, bf16[8192,1536]{1,0:T(8,128)(2,1)} %w_ref.1), custom_call_target="tpu_custom_call" | custom-call | tf_op jit(solution)/shard_map/pallas_call | solution.py:227
  39.3 2.8 %shard_map.124 = bf16[32,1536]{1,0:T(8,128)(2,1)S(1)} custom-call(s32[2]{0:T(128)S(1)} %copy-done.5, bf16[32,4096]{1,0:T(8,128)(2,1)S(1)} %collective-permute-done.4.hid_ref, f32[32,1536]{1,0:T(8,128)S(1)} %get-tuple-element.11.part_ref, bf16[32,1664]{1,0:T(8,128)(2,1)S(1)} %copy-done.2, bf16[4096,1536]{1,0:T(8,128)(2,1)S(1)} %get-tuple-element.12.w_ref), custom_call_target="tpu_custom_call" | custom-call | tf_op jit(solution)/shard_map/pallas_call | solution.py:227
  42.1 3.0 %collective-permute-start.5 = (bf16[16,1536]{1,0:T(8,128)(2,1)S(1)}, bf16[16,1536]{1,0:T(8,128)(2,1)S(1)}, u32[]{:S(2)}, u32[]{:S(2)}) collective-permute-start(bf16[16,1536]{1,0:T(8,128)(2,1)S(1)} %slice.21), channel_id=1, source_target_pairs={{0,8},{2,10},{4,12},{6,14},{8,0},{10,2},{12,4},{14,6},{1,9},{3,11}... | collective-permute-start | bytes 147464 | tf_op jit(solution)/shard_map/ppermute | solution.py:247
  45.2 2.3 %collective-permute-done.5 = bf16[16,1536]{1,0:T(8,128)(2,1)S(1)} collective-permute-done((bf16[16,1536]{1,0:T(8,128)(2,1)S(1)}, bf16[16,1536]{1,0:T(8,128)(2,1)S(1)}, u32[]{:S(2)}, u32[]{:S(2)}) %collective-permute-start.5) | collective-permute-done | bytes 49184 | tf_op jit(solution)/shard_map/ppermute | solution.py:247
  47.5 2.1 %collective-permute-start.6 = (bf16[8,1536]{1,0:T(8,128)(2,1)S(1)}, bf16[8,1536]{1,0:T(8,128)(2,1)S(1)}, u32[]{:S(2)}, u32[]{:S(2)}) collective-permute-start(bf16[8,1536]{1,0:T(8,128)(2,1)S(1)} %slice.23), channel_id=1, source_target_pairs={{0,4},{2,6},{4,0},{6,2},{8,12},{10,14},{12,8},{14,10},{1,5},{3,7},... | collective-permute-start | bytes 73736 | tf_op jit(solution)/shard_map/ppermute | solution.py:247
  49.5 1.8 %collective-permute-done.6 = bf16[8,1536]{1,0:T(8,128)(2,1)S(1)} collective-permute-done((bf16[8,1536]{1,0:T(8,128)(2,1)S(1)}, bf16[8,1536]{1,0:T(8,128)(2,1)S(1)}, u32[]{:S(2)}, u32[]{:S(2)}) %collective-permute-start.6) | collective-permute-done | bytes 24608 | tf_op jit(solution)/shard_map/ppermute | solution.py:247
  51.4 1.7 %collective-permute-start.7 = (bf16[4,1536]{1,0:T(4,128)(2,1)S(1)}, bf16[4,1536]{1,0:T(4,128)(2,1)S(1)}, u32[]{:S(2)}, u32[]{:S(2)}) collective-permute-start(bf16[4,1536]{1,0:T(4,128)(2,1)S(1)} %slice.24), channel_id=1, source_target_pairs={{0,2},{2,0},{4,6},{6,4},{8,10},{10,8},{12,14},{14,12},{1,3},{3,1},... | collective-permute-start | bytes 36872 | tf_op jit(solution)/shard_map/ppermute | solution.py:247
  53.0 2.1 %collective-permute-done.7.received_ref = bf16[4,1536]{1,0:T(4,128)(2,1)S(1)} collective-permute-done((bf16[4,1536]{1,0:T(4,128)(2,1)S(1)}, bf16[4,1536]{1,0:T(4,128)(2,1)S(1)}, u32[]{:S(2)}, u32[]{:S(2)}) %collective-permute-start.7) | collective-permute-done | bytes 12320 | tf_op jit(solution)/shard_map/ppermute | solution.py:247
  55.1 0.6 %shard_map.125 = bf16[2,2,1536]{2,1,0:T(2,128)(2,1)} custom-call(bf16[4,1664]{1,0:T(4,128)(2,1)S(1)} %shard_map.118.one_ref.carried_ref, bf16[8,1536]{1,0:T(8,128)(2,1)S(1)} %add_convert_fusion.1.mine_ref, bf16[4,1536]{1,0:T(4,128)(2,1)S(1)} %collective-permute-done.7.received_ref), custom_call_target="tpu_custom_call" | custom-call | tf_op jit(solution)/shard_map/pallas_call | solution.py:227
  (20 shorter events, 0.1 us)
Async XLA Ops:
  0.1 2.3 %copy-start.4 = (s32[2]{0:T(128)}, s32[2]{0:T(128)S(1)}, u32[]{:S(2)}) copy-start(s32[2]{0:T(128)S(1)} %pad_add_fusion.refs_0_.where_ref) | copy-start | bytes 28
  0.1 18.3 %copy-start = (bf16[3072,4096]{1,0:T(8,128)(2,1)S(1)}, bf16[3072,4096]{1,0:T(8,128)(2,1)}, u32[]{:S(2)}) copy-start(bf16[3072,4096]{1,0:T(8,128)(2,1)} %wg_ref.1) | copy-start | bytes 75497472
  2.4 4.7 %collective-permute-start = (bf16[4,1664]{1,0:T(4,128)(2,1)S(1)}, bf16[4,1664]{1,0:T(4,128)(2,1)S(1)}, u32[]{:S(2)}, u32[]{:S(2)}) collective-permute-start(bf16[4,1664]{1,0:T(4,128)(2,1)S(1)} %shard_map.118.one_ref.carried_ref), channel_id=1, source_target_pairs={{0,2},{2,0},{4,6},{6,4},{8,10},{10,8},{12,14},{14,12},{1,3},{3,1},... | collective-permute-start | bytes 39944 | tf_op jit(solution)/shard_map/ppermute | solution.py:247
  7.1 4.0 %collective-permute-start.1 = (bf16[8,1664]{1,0:T(8,128)(2,1)S(1)}, bf16[8,1664]{1,0:T(8,128)(2,1)S(1)}, u32[]{:S(2)}, u32[]{:S(2)}) collective-permute-start(bf16[8,1664]{1,0:T(8,128)(2,1)S(1)} %shard_map.119.one_ref), channel_id=1, source_target_pairs={{0,4},{2,6},{4,0},{6,2},{8,12},{10,14},{12,8},{14,10},{1,5},{3,7},... | collective-permute-start | bytes 79880 | tf_op jit(solution)/shard_map/ppermute | solution.py:247
  11.1 5.2 %collective-permute-start.2 = (bf16[16,1664]{1,0:T(8,128)(2,1)S(1)}, bf16[16,1664]{1,0:T(8,128)(2,1)S(1)}, u32[]{:S(2)}, u32[]{:S(2)}) collective-permute-start(bf16[16,1664]{1,0:T(8,128)(2,1)S(1)} %shard_map.120.one_ref), channel_id=1, source_target_pairs={{0,8},{2,10},{4,12},{6,14},{8,0},{10,2},{12,4},{14,6},{1,9},{3,11}... | collective-permute-start | bytes 159752 | tf_op jit(solution)/shard_map/ppermute | solution.py:247
  16.4 1.4 %copy-start.1 = (bf16[32,1664]{1,0:T(8,128)(2,1)}, bf16[32,1664]{1,0:T(8,128)(2,1)S(1)}, u32[]{:S(2)}) copy-start(bf16[32,1664]{1,0:T(8,128)(2,1)S(1)} %shard_map.121.own_ref.extra_ref) | copy-start | bytes 319492
  16.4 16.8 %copy-start.5 = (s32[2]{0:T(128)S(1)}, s32[2]{0:T(128)}, u32[]{:S(2)}) copy-start(s32[2]{0:T(128)} %copy-done.4) | copy-start | bytes 28
  16.4 1.4 %collective-permute-start.3 = (bf16[32,1664]{1,0:T(8,128)(2,1)S(1)}, bf16[32,1664]{1,0:T(8,128)(2,1)S(1)}, u32[]{:S(2)}, u32[]{:S(2)}) collective-permute-start(bf16[32,1664]{1,0:T(8,128)(2,1)S(1)} %shard_map.121.own_ref.extra_ref), channel_id=1, source_target_pairs={{0,1},{1,0},{2,3},{3,2},{4,5},{5,4},{6,7},{7,6},{8,9},{9,8},{10,11... | collective-permute-start | bytes 319496 | tf_op jit(solution)/shard_map/ppermute | solution.py:247
  17.8 0.6 %copy-start.6 = (bf16[32,1664]{1,0:T(8,128)(2,1)}, bf16[32,1664]{1,0:T(8,128)(2,1)S(1)}, u32[]{:S(2)}) copy-start(bf16[32,1664]{1,0:T(8,128)(2,1)S(1)} %collective-permute-done.3.other_ref) | copy-start | bytes 319492
  33.0 6.3 %copy-start.2 = (bf16[32,1664]{1,0:T(8,128)(2,1)S(1)}, bf16[32,1664]{1,0:T(8,128)(2,1)}, u32[]{:S(2)}) copy-start(bf16[32,1664]{1,0:T(8,128)(2,1)} %copy-done.1) | copy-start | bytes 319492
  33.0 6.3 %collective-permute-start.4 = (bf16[32,4096]{1,0:T(8,128)(2,1)}, bf16[32,4096]{1,0:T(8,128)(2,1)S(1)}, u32[]{:S(2)}, u32[]{:S(2)}) collective-permute-start(bf16[32,4096]{1,0:T(8,128)(2,1)} %get-tuple-element.9.hid_ref), channel_id=1, source_target_pairs={{0,1},{1,0},{2,3},{3,2},{4,5},{5,4},{6,7},{7,6},{8,9},{9,8},{10,11... | collective-permute-start | bytes 786440 | tf_op jit(solution)/shard_map/ppermute | solution.py:247
  33.2 1.0 %copy-start.3 = (bf16[32,4096]{1,0:T(8,128)(2,1)S(1)}, bf16[32,4096]{1,0:T(8,128)(2,1)}, u32[]{:S(2)}) copy-start(bf16[32,4096]{1,0:T(8,128)(2,1)} %get-tuple-element.9.hid_ref) | copy-start | bytes 786436
  42.1 5.3 %collective-permute-start.5 = (bf16[16,1536]{1,0:T(8,128)(2,1)S(1)}, bf16[16,1536]{1,0:T(8,128)(2,1)S(1)}, u32[]{:S(2)}, u32[]{:S(2)}) collective-permute-start(bf16[16,1536]{1,0:T(8,128)(2,1)S(1)} %slice.21), channel_id=1, source_target_pairs={{0,8},{2,10},{4,12},{6,14},{8,0},{10,2},{12,4},{14,6},{1,9},{3,11}... | collective-permute-start | bytes 147464 | tf_op jit(solution)/shard_map/ppermute | solution.py:247
  47.5 3.9 %collective-permute-start.6 = (bf16[8,1536]{1,0:T(8,128)(2,1)S(1)}, bf16[8,1536]{1,0:T(8,128)(2,1)S(1)}, u32[]{:S(2)}, u32[]{:S(2)}) collective-permute-start(bf16[8,1536]{1,0:T(8,128)(2,1)S(1)} %slice.23), channel_id=1, source_target_pairs={{0,4},{2,6},{4,0},{6,2},{8,12},{10,14},{12,8},{14,10},{1,5},{3,7},... | collective-permute-start | bytes 73736 | tf_op jit(solution)/shard_map/ppermute | solution.py:247
  51.4 3.8 %collective-permute-start.7 = (bf16[4,1536]{1,0:T(4,128)(2,1)S(1)}, bf16[4,1536]{1,0:T(4,128)(2,1)S(1)}, u32[]{:S(2)}, u32[]{:S(2)}) collective-permute-start(bf16[4,1536]{1,0:T(4,128)(2,1)S(1)} %slice.24), channel_id=1, source_target_pairs={{0,2},{2,0},{4,6},{6,4},{8,10},{10,8},{12,14},{14,12},{1,3},{3,1},... | collective-permute-start | bytes 36872 | tf_op jit(solution)/shard_map/ppermute | solution.py:247

commit v4 on v3

--- a/solution.py
+++ b/solution.py
@@ -205,15 +205,18 @@
     lane = lax.broadcasted_iota(jnp.int32, extra.shape, 1)
     mine = (lane % EXPERTS == where_ref[1]) & (lane < 3 * EXPERTS)
     weight = jnp.sum(jnp.where(mine, extra, 0.0), axis=-1, keepdims=True)
-    out_ref[...] = (total * weight).astype(jnp.bfloat16)
-
-
-def final_kernel(carried_ref, mine_ref, received_ref, out_ref):
+    total = total * weight
+    blocks, tok, _ = out_ref.shape
+    for idx in range(blocks):
+        out_ref[where_ref[2] ^ idx] = total[idx * tok : (idx + 1) * tok].astype(jnp.bfloat16)
+
+
+def final_kernel(carried_ref, received_ref, out_ref):
     micro, dev, half = out_ref.shape
-    total = carried_ref[:, :half].astype(jnp.float32)
-    total = total + (
-        mine_ref[: micro * dev].astype(jnp.float32) + received_ref[...].astype(jnp.float32)
-    )
+    moe = received_ref[0].astype(jnp.float32)
+    for idx in range(1, received_ref.shape[0]):
+        moe = moe + received_ref[idx].astype(jnp.float32)
+    total = carried_ref[:, :half].astype(jnp.float32) + moe
     for idx in range(micro):
         out_ref[idx] = total[idx * dev : (idx + 1) * dev].astype(jnp.bfloat16)
 
@@ -268,7 +271,8 @@
     span = side_size // EXPERTS
     small = SMALL + 64 * rows * half
     width = w_gate.shape[1]
-    where = jnp.stack([lax.axis_index("tp"), lax.axis_index("side") // span]).astype(jnp.int32)
+    side = lax.axis_index("side")
+    where = jnp.stack([lax.axis_index("tp"), side // span, side]).astype(jnp.int32)
     small_args = (page_table, lengths, routes, gate_fixed)
     large_args = (residual, queries, key_cache, value_cache)
     local = call(
@@ -299,9 +303,9 @@
     held = pltpu.VMEM((width, half), w_down.dtype)
     hidden, down_own = call(
         hidden_kernel,
-        (jax.ShapeDtypeStruct((rows, width), jnp.bfloat16), held),
+        (pltpu.VMEM((rows, width), jnp.bfloat16), held),
         [SMEM] + [VMEM] * 4 + [ANY] * 2,
-        (where, gathered, other, norm_gain, in_vmem(w_gate), in_hbm(w_up), in_hbm(w_down)),
+        (where, in_vmem(gathered), in_vmem(other), norm_gain, in_vmem(w_gate), in_hbm(w_up), in_hbm(w_down)),
         (
             pltpu.VMEM((rows, 2 * half), jnp.bfloat16),
             pltpu.VMEM((rows, width), jnp.float32),
@@ -309,35 +313,31 @@
             pltpu.SemaphoreType.DMA((slots,)),
             pltpu.SemaphoreType.DMA,
         ),
-        small + slots * half * tile * 4,
+        SMALL + rows * half * 24 + slots * half * tile * 4,
     )
     hidden_other = swap(hidden, "tp", 1)
     part, down_other = call(
         down_own_kernel,
         (jax.ShapeDtypeStruct((rows, half), jnp.float32), held),
         [SMEM] + [VMEM] * 2 + [ANY],
-        (where, hidden, in_vmem(down_own), in_hbm(w_down)),
+        (where, in_vmem(hidden), in_vmem(down_own), in_hbm(w_down)),
         (pltpu.SemaphoreType.DMA,),
         small,
     )
     sent = call(
         down_other_kernel,
-        jax.ShapeDtypeStruct((rows, half), jnp.bfloat16),
+        jax.ShapeDtypeStruct((side_size, tok, half), jnp.bfloat16),
         [SMEM] + [VMEM] * 4,
         (where, hidden_other, part, gathered, in_vmem(down_other)),
         limit=small,
     )
-    for mask in reversed(masks):
-        count = sent.shape[0] // 2
-        received = swap(sent[count:], "side", mask)
-        if mask > 1:
-            sent = sent[:count].astype(jnp.float32) + received.astype(jnp.float32)
-            sent = sent.astype(jnp.bfloat16)
+    received = lax.all_to_all(sent, "side", split_axis=0, concat_axis=0, tiled=True)
     return call(
         final_kernel,
         jax.ShapeDtypeStruct(residual.shape, residual.dtype),
-        [VMEM] * 3,
-        (local, sent, received),
+        [VMEM] * 2,
+        (local, received),
+        limit=small,
     )
 
 

time: 56 us -> 53.9 us (0.963)
  blocking collectives: 0 us -> 13.5 us
  starting transfers between devices: 15.3 us -> 8.56 us
  waiting for transfers between devices: 13.1 us -> 6.93 us
  local copies, waits for them, and re-layouts: 1.63 us -> 0.01 us
  Pallas kernels: 25.5 us -> 24.5 us
    all_to_all x0 -> x1, blocking collectives: none -> 13.5 us  [per_device(): lax.all_to_all(sent, 'side', split_axis=0, concat_axis=0, tiled=True)]
    ppermute x8 -> x5, starting transfers between devices: 15.3 us -> 8.56 us  [swap(): return lax.ppermute(array, axis, [(i, i ^ mask) for i in range(size)])]
    ppermute x8 -> x5, waiting for transfers between devices: 13.1 us -> 6.93 us  [swap(): return lax.ppermute(array, axis, [(i, i ^ mask) for i in range(size)])]
    unnamed x14 -> x6, local copies, waits for them, and re-layouts: 1.61 us -> 0.01 us
    pallas_call x8, Pallas kernels: 25.5 us -> 24.5 us  [call(): pl.pallas_call(kernel, out_shape=out_shape, in_specs=in_specs, out_specs=...]
  transfers between devices with their start and end apart: 8 -> 5, of which waited for: 7 -> 4; matrix products, arithmetic and copies ran while one was open for 0% -> 0% of each run, Pallas kernels for 9% -> 10%
where the time goes in v4:
time: 53.9 us; the launch traced here: 53.7 us
  Pallas kernels  24.5 us (45%)
  blocking collectives  13.5 us (25%)
  starting transfers between devices  8.56 us (16%)
  waiting for transfers between devices  6.93 us (13%)
    pallas_call x8, Pallas kernels, call(): pl.pallas_call(kernel, out_shape=out_shape, in_specs=in_specs, out_specs=...  24.5 us
    all_to_all x1, blocking collectives, per_device(): lax.all_to_all(sent, 'side', split_axis=0, concat_axis=0, tiled=True)  13.5 us
    ppermute x5, starting transfers between devices, swap(): return lax.ppermute(array, axis, [(i, i ^ mask) for i in range(size)])  8.56 us
    ppermute x5, waiting for transfers between devices, swap(): return lax.ppermute(array, axis, [(i, i ^ mask) for i in range(size)])  6.93 us
  transfers between devices with their start and end apart: 5, of which 4 were waited for; matrix products, arithmetic and copies ran while one was open for 0% of the time, Pallas kernels for 10%

profile of v4, /device:TPU:0, one launch (start us, length us, event | category | flops | bytes accessed | tf_op | source)
XLA Modules:
  0.0 53.7 jit_solution(15168176118446572263)
XLA Ops:
  0.0 0.1 pad_add_fusion.refs_0_.where_ref
  0.1 0.0 copy-start.1
  0.1 0.0 copy-start
  0.1 2.3 %shard_map.118.one_ref.carried_ref = bf16[4,1664]{1,0:T(4,128)(2,1)S(1)} custom-call(s32[3]{0:T(128)S(1)} %pad_add_fusion.refs_0_.where_ref, s32[2,2,2]{2,1,0:T(2,128)} %refs_1_.1, s32[2,2]{1,0:T(2,128)} %refs_2_.1, s32[2,2,2]{2,1,0:T(2,128)} %refs_3_.1, s32[2,2]{1,0:T(2,128)} %refs_4_.1, bf16[2,2,1536]{2,1,0:T(2,128)(2,1)} %refs_5_.1, ...), custom_call_target="tpu_custom_call" | custom-call | tf_op jit(solution)/shard_map/pallas_call | solution.py:230
  2.4 0.0 copy-done.1
  2.4 3.0 %collective-permute-start = (bf16[4,1664]{1,0:T(4,128)(2,1)S(1)}, bf16[4,1664]{1,0:T(4,128)(2,1)S(1)}, u32[]{:S(2)}, u32[]{:S(2)}) collective-permute-start(bf16[4,1664]{1,0:T(4,128)(2,1)S(1)} %shard_map.118.one_ref.carried_ref), channel_id=1, source_target_pairs={{0,2},{2,0},{4,6},{6,4},{8,10},{10,8},{12,14},{14,12},{1,3},{3,1},... | collective-permute-start | bytes 39944 | tf_op jit(solution)/shard_map/ppermute | solution.py:250
  5.4 1.7 %collective-permute-done.two_ref = bf16[4,1664]{1,0:T(4,128)(2,1)S(1)} collective-permute-done((bf16[4,1664]{1,0:T(4,128)(2,1)S(1)}, bf16[4,1664]{1,0:T(4,128)(2,1)S(1)}, u32[]{:S(2)}, u32[]{:S(2)}) %collective-permute-start) | collective-permute-done | bytes 13344 | tf_op jit(solution)/shard_map/ppermute | solution.py:250
  7.1 2.2 %collective-permute-start.1 = (bf16[8,1664]{1,0:T(8,128)(2,1)S(1)}, bf16[8,1664]{1,0:T(8,128)(2,1)S(1)}, u32[]{:S(2)}, u32[]{:S(2)}) collective-permute-start(bf16[8,1664]{1,0:T(8,128)(2,1)S(1)} %shard_map.119.one_ref), channel_id=1, source_target_pairs={{0,4},{2,6},{4,0},{6,2},{8,12},{10,14},{12,8},{14,10},{1,5},{3,7},... | collective-permute-start | bytes 79880 | tf_op jit(solution)/shard_map/ppermute | solution.py:250
  9.3 1.8 %collective-permute-done.1.two_ref = bf16[8,1664]{1,0:T(8,128)(2,1)S(1)} collective-permute-done((bf16[8,1664]{1,0:T(8,128)(2,1)S(1)}, bf16[8,1664]{1,0:T(8,128)(2,1)S(1)}, u32[]{:S(2)}, u32[]{:S(2)}) %collective-permute-start.1) | collective-permute-done | bytes 26656 | tf_op jit(solution)/shard_map/ppermute | solution.py:250
  11.2 3.1 %collective-permute-start.2 = (bf16[16,1664]{1,0:T(8,128)(2,1)S(1)}, bf16[16,1664]{1,0:T(8,128)(2,1)S(1)}, u32[]{:S(2)}, u32[]{:S(2)}) collective-permute-start(bf16[16,1664]{1,0:T(8,128)(2,1)S(1)} %shard_map.120.one_ref), channel_id=1, source_target_pairs={{0,8},{2,10},{4,12},{6,14},{8,0},{10,2},{12,4},{14,6},{1,9},{3,11}... | collective-permute-start | bytes 159752 | tf_op jit(solution)/shard_map/ppermute | solution.py:250
  14.2 2.1 %collective-permute-done.2.two_ref = bf16[16,1664]{1,0:T(8,128)(2,1)S(1)} collective-permute-done((bf16[16,1664]{1,0:T(8,128)(2,1)S(1)}, bf16[16,1664]{1,0:T(8,128)(2,1)S(1)}, u32[]{:S(2)}, u32[]{:S(2)}) %collective-permute-start.2) | collective-permute-done | bytes 53280 | tf_op jit(solution)/shard_map/ppermute | solution.py:250
  16.4 0.0 copy-start.2
  16.4 0.1 collective-permute-start.3
  16.5 1.3 %collective-permute-done.3.other_ref = bf16[32,1664]{1,0:T(8,128)(2,1)S(1)} collective-permute-done((bf16[32,1664]{1,0:T(8,128)(2,1)S(1)}, bf16[32,1664]{1,0:T(8,128)(2,1)S(1)}, u32[]{:S(2)}, u32[]{:S(2)}) %collective-permute-start.3) | collective-permute-done | bytes 106528 | tf_op jit(solution)/shard_map/ppermute | solution.py:250
  17.8 0.0 copy-done
  17.8 13.6 %shard_map.122 = (bf16[32,4096]{1,0:T(8,128)(2,1)S(1)}, bf16[4096,1536]{1,0:T(8,128)(2,1)S(1)}) custom-call(s32[3]{0:T(128)} %copy-done.1, bf16[32,1664]{1,0:T(8,128)(2,1)S(1)} %shard_map.121.own_ref.extra_ref, bf16[32,1664]{1,0:T(8,128)(2,1)S(1)} %collective-permute-done.3.other_ref, bf16[3072]{0:T(1024)(128)(2,1)} %gain_ref.1, ...), custom_call_target="tpu_custom_call" | custom-call | tf_op jit(solution)/shard_map/pallas_call | solution.py:230
  31.4 0.2 collective-permute-start.4
  31.6 0.0 copy-done.2
  31.6 5.1 %shard_map.123 = (f32[32,1536]{1,0:T(8,128)S(1)}, bf16[4096,1536]{1,0:T(8,128)(2,1)S(1)}) custom-call(s32[3]{0:T(128)S(1)} %copy-done.2, bf16[32,4096]{1,0:T(8,128)(2,1)S(1)} %get-tuple-element.9.hid_ref, bf16[4096,1536]{1,0:T(8,128)(2,1)S(1)} %get-tuple-element.10.own_ref, bf16[8192,1536]{1,0:T(8,128)(2,1)} %w_ref.1), custom_call_target="tpu_custom_call" | custom-call | tf_op jit(solution)/shard_map/pallas_call | solution.py:230
  36.7 0.0 collective-permute-done.4.hid_ref
  36.8 2.8 %shard_map.124 = bf16[8,4,1536]{2,1,0:T(4,128)(2,1)S(1)} custom-call(s32[3]{0:T(128)S(1)} %copy-done.2, bf16[32,4096]{1,0:T(8,128)(2,1)S(1)} %collective-permute-done.4.hid_ref, f32[32,1536]{1,0:T(8,128)S(1)} %get-tuple-element.11.part_ref, bf16[32,1664]{1,0:T(8,128)(2,1)S(1)} %shard_map.121.own_ref.extra_ref, bf16[4096,1536]{1,0:T(8,128)(2,1)S(1)} %get-tuple-element.12.w_ref), custom_call_target="tpu_custom_call" | custom-call | tf_op jit(solution)/shard_map/pallas_call | solution.py:230
  39.6 13.5 %all_to_all.5.received_ref = bf16[8,4,1536]{2,1,0:T(4,128)(2,1)S(1)} all-to-all(bf16[8,4,1536]{2,1,0:T(4,128)(2,1)S(1)} %shard_map.124), channel_id=1, replica_groups=mesh['groups'=2,'side'=8,'tp'=2] {'side'}, dimensions={0} | all-to-all | bytes 196608 | tf_op jit(solution)/shard_map/all_to_all | solution.py:334
  53.1 0.6 %shard_map.125 = bf16[2,2,1536]{2,1,0:T(2,128)(2,1)} custom-call(bf16[4,1664]{1,0:T(4,128)(2,1)S(1)} %shard_map.118.one_ref.carried_ref, bf16[8,4,1536]{2,1,0:T(4,128)(2,1)S(1)} %all_to_all.5.received_ref), custom_call_target="tpu_custom_call" | custom-call | tf_op jit(solution)/shard_map/pallas_call | solution.py:230
  (3 shorter events, 0.0 us)
Async XLA Ops:
  0.1 2.3 %copy-start.1 = (s32[3]{0:T(128)}, s32[3]{0:T(128)S(1)}, u32[]{:S(2)}) copy-start(s32[3]{0:T(128)S(1)} %pad_add_fusion.refs_0_.where_ref) | copy-start | bytes 40
  0.1 17.7 %copy-start = (bf16[3072,4096]{1,0:T(8,128)(2,1)S(1)}, bf16[3072,4096]{1,0:T(8,128)(2,1)}, u32[]{:S(2)}) copy-start(bf16[3072,4096]{1,0:T(8,128)(2,1)} %wg_ref.1) | copy-start | bytes 75497472
  2.4 4.7 %collective-permute-start = (bf16[4,1664]{1,0:T(4,128)(2,1)S(1)}, bf16[4,1664]{1,0:T(4,128)(2,1)S(1)}, u32[]{:S(2)}, u32[]{:S(2)}) collective-permute-start(bf16[4,1664]{1,0:T(4,128)(2,1)S(1)} %shard_map.118.one_ref.carried_ref), channel_id=1, source_target_pairs={{0,2},{2,0},{4,6},{6,4},{8,10},{10,8},{12,14},{14,12},{1,3},{3,1},... | collective-permute-start | bytes 39944 | tf_op jit(solution)/shard_map/ppermute | solution.py:250
  7.1 4.0 %collective-permute-start.1 = (bf16[8,1664]{1,0:T(8,128)(2,1)S(1)}, bf16[8,1664]{1,0:T(8,128)(2,1)S(1)}, u32[]{:S(2)}, u32[]{:S(2)}) collective-permute-start(bf16[8,1664]{1,0:T(8,128)(2,1)S(1)} %shard_map.119.one_ref), channel_id=1, source_target_pairs={{0,4},{2,6},{4,0},{6,2},{8,12},{10,14},{12,8},{14,10},{1,5},{3,7},... | collective-permute-start | bytes 79880 | tf_op jit(solution)/shard_map/ppermute | solution.py:250
  11.2 5.2 %collective-permute-start.2 = (bf16[16,1664]{1,0:T(8,128)(2,1)S(1)}, bf16[16,1664]{1,0:T(8,128)(2,1)S(1)}, u32[]{:S(2)}, u32[]{:S(2)}) collective-permute-start(bf16[16,1664]{1,0:T(8,128)(2,1)S(1)} %shard_map.120.one_ref), channel_id=1, source_target_pairs={{0,8},{2,10},{4,12},{6,14},{8,0},{10,2},{12,4},{14,6},{1,9},{3,11}... | collective-permute-start | bytes 159752 | tf_op jit(solution)/shard_map/ppermute | solution.py:250
  16.4 15.2 %copy-start.2 = (s32[3]{0:T(128)S(1)}, s32[3]{0:T(128)}, u32[]{:S(2)}) copy-start(s32[3]{0:T(128)} %copy-done.1) | copy-start | bytes 40
  16.4 1.4 %collective-permute-start.3 = (bf16[32,1664]{1,0:T(8,128)(2,1)S(1)}, bf16[32,1664]{1,0:T(8,128)(2,1)S(1)}, u32[]{:S(2)}, u32[]{:S(2)}) collective-permute-start(bf16[32,1664]{1,0:T(8,128)(2,1)S(1)} %shard_map.121.own_ref.extra_ref), channel_id=1, source_target_pairs={{0,1},{1,0},{2,3},{3,2},{4,5},{5,4},{6,7},{7,6},{8,9},{9,8},{10,11... | collective-permute-start | bytes 319496 | tf_op jit(solution)/shard_map/ppermute | solution.py:250
  31.4 5.4 %collective-permute-start.4 = (bf16[32,4096]{1,0:T(8,128)(2,1)S(1)}, bf16[32,4096]{1,0:T(8,128)(2,1)S(1)}, u32[]{:S(2)}, u32[]{:S(2)}) collective-permute-start(bf16[32,4096]{1,0:T(8,128)(2,1)S(1)} %get-tuple-element.9.hid_ref), channel_id=1, source_target_pairs={{0,1},{1,0},{2,3},{3,2},{4,5},{5,4},{6,7},{7,6},{8,9},{9,8},{10,11... | collective-permute-start | bytes 786440 | tf_op jit(solution)/shard_map/ppermute | solution.py:250

commit v5 on v4

--- a/solution.py
+++ b/solution.py
@@ -86,7 +86,7 @@
         for g in range(group):
             at = slice((first + g) * HEAD_DIM, (first + g + 1) * HEAD_DIM)
             carried = residual[:, at] + blended[g * tok : (g + 1) * tok]
-            out_ref[:, at] = carried.astype(jnp.bfloat16)
+            out_ref[0, :, at] = carried.astype(jnp.bfloat16)
     lane = lax.broadcasted_iota(jnp.int32, (tok, LANES), 1)
     expert = lane % EXPERTS
     fixed = by_row((tok, LANES), [gate_ref[t // dev, t % dev] for t in range(tok)])
@@ -103,11 +103,9 @@
     packed = jnp.where(
         term == 0, high, jnp.where(term == 1, mid, jnp.where(term == 2, low, 0.0))
     )
-    out_ref[:, half:] = packed.astype(jnp.bfloat16)
-
-
-def join_kernel(one_ref, two_ref, out_ref):
-    out_ref[...] = jnp.concatenate([one_ref[...], two_ref[...]], axis=0)
+    out_ref[0, :, half:] = packed.astype(jnp.bfloat16)
+    for idx in range(1, out_ref.shape[0]):
+        out_ref[idx] = out_ref[0]
 
 
 def half_copy(w_ref, out_ref, which, sem):
@@ -133,7 +131,7 @@
     down_sem,
 ):
     slots, _, tile = buf_ref.shape
-    half = own_ref.shape[1] - LANES
+    half = own_ref.shape[2] - LANES
     chunks = out_ref.shape[1] // tile
     down = half_copy(wd_ref, down_ref, where_ref[0], down_sem)
 
@@ -146,8 +144,8 @@
 
     lax.fori_loop(0, slots, lambda idx, _: up_copy(idx).start(), None)
     is_first = where_ref[0] == 0
-    own = own_ref[:, :half].astype(jnp.float32)
-    other = other_ref[:, :half].astype(jnp.float32)
+    own = flat(own_ref)[:, :half]
+    other = flat(other_ref)[:, :half]
     square = jnp.sum(own * own, axis=-1, keepdims=True)
     square = square + jnp.sum(other * other, axis=-1, keepdims=True)
     inv_rms = lax.rsqrt(square / (2 * half) + EPS)
@@ -201,14 +199,14 @@
     total = part_ref[...] + jnp.dot(
         hid_ref[...], w_ref[...], preferred_element_type=jnp.float32
     )
-    extra = extra_ref[:, -LANES:].astype(jnp.float32)
+    extra = flat(extra_ref)[:, -LANES:]
     lane = lax.broadcasted_iota(jnp.int32, extra.shape, 1)
     mine = (lane % EXPERTS == where_ref[1]) & (lane < 3 * EXPERTS)
     weight = jnp.sum(jnp.where(mine, extra, 0.0), axis=-1, keepdims=True)
     total = total * weight
     blocks, tok, _ = out_ref.shape
     for idx in range(blocks):
-        out_ref[where_ref[2] ^ idx] = total[idx * tok : (idx + 1) * tok].astype(jnp.bfloat16)
+        out_ref[idx] = total[idx * tok : (idx + 1) * tok].astype(jnp.bfloat16)
 
 
 def final_kernel(carried_ref, received_ref, out_ref):
@@ -216,7 +214,7 @@
     moe = received_ref[0].astype(jnp.float32)
     for idx in range(1, received_ref.shape[0]):
         moe = moe + received_ref[idx].astype(jnp.float32)
-    total = carried_ref[:, :half].astype(jnp.float32) + moe
+    total = carried_ref[0, :, :half].astype(jnp.float32) + moe
     for idx in range(micro):
         out_ref[idx] = total[idx * dev : (idx + 1) * dev].astype(jnp.bfloat16)
 
@@ -271,13 +269,12 @@
     span = side_size // EXPERTS
     small = SMALL + 64 * rows * half
     width = w_gate.shape[1]
-    side = lax.axis_index("side")
-    where = jnp.stack([lax.axis_index("tp"), side // span, side]).astype(jnp.int32)
+    where = jnp.stack([lax.axis_index("tp"), lax.axis_index("side") // span]).astype(jnp.int32)
     small_args = (page_table, lengths, routes, gate_fixed)
     large_args = (residual, queries, key_cache, value_cache)
     local = call(
         attend_kernel,
-        jax.ShapeDtypeStruct((tok, half + LANES), jnp.bfloat16),
+        jax.ShapeDtypeStruct((side_size, tok, half + LANES), jnp.bfloat16),
         [SMEM] + [ANY] * 10,
         (where, *[in_hbm(arg) for arg in (*small_args, *large_args, w_gate, w_up)]),
         (
@@ -285,18 +282,9 @@
             *[pltpu.VMEM(arg.shape, arg.dtype) for arg in large_args],
             pltpu.SemaphoreType.DMA((8,)),
         ),
-    )
-    gathered = local
-    masks = [1 << bit for bit in range(side_size.bit_length() - 1)]
-    for mask in masks:
-        shape = (2 * gathered.shape[0], gathered.shape[1])
-        gathered = call(
-            join_kernel,
-            jax.ShapeDtypeStruct(shape, gathered.dtype),
-            [VMEM] * 2,
-            (gathered, swap(gathered, "side", mask)),
-            limit=small,
-        )
+        small,
+    )
+    gathered = lax.all_to_all(local, "side", split_axis=0, concat_axis=0, tiled=True)
     other = swap(gathered, "tp", 1)
     tile = math.gcd(width, 512)
     slots = min(width // tile, 6)

time: 53.9 us -> 50.6 us (0.939)
  blocking collectives: 13.5 us -> 24.2 us
  starting transfers between devices: 8.56 us -> 0.22 us
  waiting for transfers between devices: 6.93 us -> 1.31 us
    all_to_all x0 -> x1, blocking collectives: none -> 14.5 us  [per_device(): lax.all_to_all(local, 'side', split_axis=0, concat_axis=0, tiled=True)]
    ppermute x5 -> x2, starting transfers between devices: 8.56 us -> 0.22 us  [swap(): return lax.ppermute(array, axis, [(i, i ^ mask) for i in range(size)])]
    ppermute x5 -> x2, waiting for transfers between devices: 6.93 us -> 1.31 us  [swap(): return lax.ppermute(array, axis, [(i, i ^ mask) for i in range(size)])]
    all_to_all x1, blocking collectives: 13.5 us -> 9.69 us  [per_device(): lax.all_to_all(sent, 'side', split_axis=0, concat_axis=0, tiled=True)]
    pallas_call x8 -> x5, Pallas kernels: 24.5 us -> 24.5 us  [call(): pl.pallas_call(kernel, out_shape=out_shape, in_specs=in_specs, out_specs=...]
  transfers between devices with their start and end apart: 5 -> 2, of which waited for: 4 -> 1; matrix products, arithmetic and copies ran while one was open for 0% -> 0% of each run, Pallas kernels for 10% -> 10%
where the time goes in v5:
time: 50.6 us; the launch traced here: 50.4 us
  Pallas kernels  24.5 us (48%)
  blocking collectives  24.2 us (48%)
  waiting for transfers between devices  1.31 us (3%)
    pallas_call x5, Pallas kernels, call(): pl.pallas_call(kernel, out_shape=out_shape, in_specs=in_specs, out_specs=...  24.5 us
    all_to_all x1, blocking collectives, per_device(): lax.all_to_all(local, 'side', split_axis=0, concat_axis=0, tiled=True)  14.5 us
    all_to_all x1, blocking collectives, per_device(): lax.all_to_all(sent, 'side', split_axis=0, concat_axis=0, tiled=True)  9.69 us
    ppermute x2, waiting for transfers between devices, swap(): return lax.ppermute(array, axis, [(i, i ^ mask) for i in range(size)])  1.31 us
  transfers between devices with their start and end apart: 2, of which 1 were waited for; matrix products, arithmetic and copies ran while one was open for 0% of the time, Pallas kernels for 10%

profile of v5, /device:TPU:0, one launch (start us, length us, event | category | flops | bytes accessed | tf_op | source)
XLA Modules:
  0.0 50.4 jit_solution(9329985916283607134)
XLA Ops:
  0.0 0.1 pad_add_fusion.refs_0_.where_ref
  0.1 0.0 copy-start.1
  0.1 0.0 copy-start
  0.1 2.3 %shard_map.118.carried_ref = bf16[8,4,1664]{2,1,0:T(4,128)(2,1)S(1)} custom-call(s32[2]{0:T(128)S(1)} %pad_add_fusion.refs_0_.where_ref, s32[2,2,2]{2,1,0:T(2,128)} %refs_1_.1, s32[2,2]{1,0:T(2,128)} %refs_2_.1, s32[2,2,2]{2,1,0:T(2,128)} %refs_3_.1, s32[2,2]{1,0:T(2,128)} %refs_4_.1, bf16[2,2,1536]{2,1,0:T(2,128)(2,1)} %refs_5_.1, ...), custom_call_target="tpu_custom_call" | custom-call | tf_op jit(solution)/shard_map/pallas_call | solution.py:228
  2.4 0.0 copy-done.1
  2.4 14.5 %all_to_all.10.own_ref.extra_ref = bf16[8,4,1664]{2,1,0:T(4,128)(2,1)S(1)} all-to-all(bf16[8,4,1664]{2,1,0:T(4,128)(2,1)S(1)} %shard_map.118.carried_ref), channel_id=1, replica_groups=mesh['groups'=2,'side'=8,'tp'=2] {'side'}, dimensions={0} | all-to-all | bytes 212992 | tf_op jit(solution)/shard_map/all_to_all | solution.py:287
  16.9 0.0 copy-start.2
  16.9 0.0 collective-permute-start
  16.9 1.3 %collective-permute-done.other_ref = bf16[8,4,1664]{2,1,0:T(4,128)(2,1)S(1)} collective-permute-done((bf16[8,4,1664]{2,1,0:T(4,128)(2,1)S(1)}, bf16[8,4,1664]{2,1,0:T(4,128)(2,1)S(1)}, u32[]{:S(2)}, u32[]{:S(2)}) %collective-permute-start) | collective-permute-done | bytes 106528 | tf_op jit(solution)/shard_map/ppermute | solution.py:248
  18.2 0.0 copy-done
  18.2 13.6 %shard_map.119 = (bf16[32,4096]{1,0:T(8,128)(2,1)S(1)}, bf16[4096,1536]{1,0:T(8,128)(2,1)S(1)}) custom-call(s32[2]{0:T(128)} %copy-done.1, bf16[8,4,1664]{2,1,0:T(4,128)(2,1)S(1)} %all_to_all.10.own_ref.extra_ref, bf16[8,4,1664]{2,1,0:T(4,128)(2,1)S(1)} %collective-permute-done.other_ref, bf16[3072]{0:T(1024)(128)(2,1)} %gain_ref.1, ...), custom_call_target="tpu_custom_call" | custom-call | tf_op jit(solution)/shard_map/pallas_call | solution.py:228
  31.9 0.2 collective-permute-start.1
  32.1 0.0 copy-done.2
  32.1 5.1 %shard_map.120 = (f32[32,1536]{1,0:T(8,128)S(1)}, bf16[4096,1536]{1,0:T(8,128)(2,1)S(1)}) custom-call(s32[2]{0:T(128)S(1)} %copy-done.2, bf16[32,4096]{1,0:T(8,128)(2,1)S(1)} %get-tuple-element.9.hid_ref, bf16[4096,1536]{1,0:T(8,128)(2,1)S(1)} %get-tuple-element.10.own_ref, bf16[8192,1536]{1,0:T(8,128)(2,1)} %w_ref.1), custom_call_target="tpu_custom_call" | custom-call | tf_op jit(solution)/shard_map/pallas_call | solution.py:228
  37.2 0.0 collective-permute-done.1.hid_ref
  37.2 2.8 %shard_map.121 = bf16[8,4,1536]{2,1,0:T(4,128)(2,1)S(1)} custom-call(s32[2]{0:T(128)S(1)} %copy-done.2, bf16[32,4096]{1,0:T(8,128)(2,1)S(1)} %collective-permute-done.1.hid_ref, f32[32,1536]{1,0:T(8,128)S(1)} %get-tuple-element.11.part_ref, bf16[8,4,1664]{2,1,0:T(4,128)(2,1)S(1)} %all_to_all.10.own_ref.extra_ref, bf16[4096,1536]{1,0:T(8,128)(2,1)S(1)} %get-tuple-element.12.w_ref), custom_call_target="tpu_custom_call" | custom-call | tf_op jit(solution)/shard_map/pallas_call | solution.py:228
  40.0 9.7 %all_to_all.11.received_ref = bf16[8,4,1536]{2,1,0:T(4,128)(2,1)S(1)} all-to-all(bf16[8,4,1536]{2,1,0:T(4,128)(2,1)S(1)} %shard_map.121), channel_id=1, replica_groups=mesh['groups'=2,'side'=8,'tp'=2] {'side'}, dimensions={0} | all-to-all | bytes 196608 | tf_op jit(solution)/shard_map/all_to_all | solution.py:322
  49.7 0.6 %shard_map.122 = bf16[2,2,1536]{2,1,0:T(2,128)(2,1)} custom-call(bf16[8,4,1664]{2,1,0:T(4,128)(2,1)S(1)} %shard_map.118.carried_ref, bf16[8,4,1536]{2,1,0:T(4,128)(2,1)S(1)} %all_to_all.11.received_ref), custom_call_target="tpu_custom_call" | custom-call | tf_op jit(solution)/shard_map/pallas_call | solution.py:228
Async XLA Ops:
  0.1 2.4 %copy-start.1 = (s32[2]{0:T(128)}, s32[2]{0:T(128)S(1)}, u32[]{:S(2)}) copy-start(s32[2]{0:T(128)S(1)} %pad_add_fusion.refs_0_.where_ref) | copy-start | bytes 28
  0.1 18.2 %copy-start = (bf16[3072,4096]{1,0:T(8,128)(2,1)S(1)}, bf16[3072,4096]{1,0:T(8,128)(2,1)}, u32[]{:S(2)}) copy-start(bf16[3072,4096]{1,0:T(8,128)(2,1)} %wg_ref.1) | copy-start | bytes 75497472
  16.9 15.2 %copy-start.2 = (s32[2]{0:T(128)S(1)}, s32[2]{0:T(128)}, u32[]{:S(2)}) copy-start(s32[2]{0:T(128)} %copy-done.1) | copy-start | bytes 28
  16.9 1.3 %collective-permute-start = (bf16[8,4,1664]{2,1,0:T(4,128)(2,1)S(1)}, bf16[8,4,1664]{2,1,0:T(4,128)(2,1)S(1)}, u32[]{:S(2)}, u32[]{:S(2)}) collective-permute-start(bf16[8,4,1664]{2,1,0:T(4,128)(2,1)S(1)} %all_to_all.10.own_ref.extra_ref), channel_id=1, source_target_pairs={{0,1},{1,0},{2,3},{3,2},{4,5},{5,4},{6,7},{7,6},{8,9},{9,8},{10,11... | collective-permute-start | bytes 319496 | tf_op jit(solution)/shard_map/ppermute | solution.py:248
  31.9 5.4 %collective-permute-start.1 = (bf16[32,4096]{1,0:T(8,128)(2,1)S(1)}, bf16[32,4096]{1,0:T(8,128)(2,1)S(1)}, u32[]{:S(2)}, u32[]{:S(2)}) collective-permute-start(bf16[32,4096]{1,0:T(8,128)(2,1)S(1)} %get-tuple-element.9.hid_ref), channel_id=1, source_target_pairs={{0,1},{1,0},{2,3},{3,2},{4,5},{5,4},{6,7},{7,6},{8,9},{9,8},{10,11... | collective-permute-start | bytes 786440 | tf_op jit(solution)/shard_map/ppermute | solution.py:248

commit v6 on v5

--- a/solution.py
+++ b/solution.py
@@ -108,10 +108,26 @@
         out_ref[idx] = out_ref[0]
 
 
-def half_copy(w_ref, out_ref, which, sem):
+def row_copy(w_ref, start, out_ref, sem):
     depth = out_ref.shape[0]
-    start = pl.multiple_of(which * depth, depth)
+    start = pl.multiple_of(start, depth)
     return pltpu.make_async_copy(w_ref.at[pl.ds(start, depth), :], out_ref, sem)
+
+
+def add_rows(hid_ref, offset, w_ref, out_ref, buf_ref, sem, start):
+    chunks, depth, _ = buf_ref.shape
+
+    def copy(idx):
+        return row_copy(w_ref, start + idx * depth, buf_ref.at[idx], sem.at[idx])
+
+    lax.fori_loop(0, chunks, lambda idx, _: copy(idx).start(), None)
+
+    def step(idx, _):
+        copy(idx).wait()
+        at = pl.ds(pl.multiple_of(offset + idx * depth, depth), depth)
+        out_ref[...] += jnp.dot(hid_ref[:, at], buf_ref[idx], preferred_element_type=jnp.float32)
+
+    return lambda: lax.fori_loop(0, chunks, step, None)
 
 
 def hidden_kernel(
@@ -133,7 +149,7 @@
     slots, _, tile = buf_ref.shape
     half = own_ref.shape[2] - LANES
     chunks = out_ref.shape[1] // tile
-    down = half_copy(wd_ref, down_ref, where_ref[0], down_sem)
+    down = row_copy(wd_ref, where_ref[0] * out_ref.shape[1], down_ref, down_sem)
 
     def columns(idx):
         return pl.ds(pl.multiple_of(idx * tile, tile), tile)
@@ -182,23 +198,30 @@
     down.wait()
 
 
-def down_own_kernel(where_ref, hid_ref, own_ref, w_ref, out_ref, other_ref, sem):
+def down_own_kernel(where_ref, hid_ref, held_ref, w_ref, out_ref, buf_ref, sem):
+    held = held_ref.shape[0]
+    start = where_ref[0] * hid_ref.shape[1] + held
+    rest = add_rows(hid_ref, held, w_ref, out_ref, buf_ref, sem, start)
     tile = out_ref.shape[1] // DOWN_TILES
-    copy = half_copy(w_ref, other_ref, 1 - where_ref[0], sem)
-    copy.start()
 
     def step(idx, _):
         at = pl.ds(pl.multiple_of(idx * tile, tile), tile)
-        out_ref[:, at] = jnp.dot(hid_ref[...], own_ref[:, at], preferred_element_type=jnp.float32)
+        out_ref[:, at] = jnp.dot(
+            hid_ref[:, :held], held_ref[:, at], preferred_element_type=jnp.float32
+        )
 
     lax.fori_loop(0, DOWN_TILES, step, None)
-    copy.wait()
-
-
-def down_other_kernel(where_ref, hid_ref, part_ref, extra_ref, w_ref, out_ref):
-    total = part_ref[...] + jnp.dot(
-        hid_ref[...], w_ref[...], preferred_element_type=jnp.float32
-    )
+    rest()
+
+
+def down_other_kernel(
+    where_ref, hid_ref, part_ref, extra_ref, w_ref, out_ref, total_ref, buf_ref, sem
+):
+    start = (1 - where_ref[0]) * hid_ref.shape[1]
+    rest = add_rows(hid_ref, 0, w_ref, total_ref, buf_ref, sem, start)
+    total_ref[...] = part_ref[...]
+    rest()
+    total = total_ref[...]
     extra = flat(extra_ref)[:, -LANES:]
     lane = lax.broadcasted_iota(jnp.int32, extra.shape, 1)
     mine = (lane % EXPERTS == where_ref[1]) & (lane < 3 * EXPERTS)
@@ -288,7 +311,16 @@
     other = swap(gathered, "tp", 1)
     tile = math.gcd(width, 512)
     slots = min(width // tile, 6)
-    held = pltpu.VMEM((width, half), w_down.dtype)
+    early = width // 2
+    depth = math.gcd(width - early, 512)
+    held = pltpu.VMEM((early, half), w_down.dtype)
+
+    def stream(count):
+        return (
+            pltpu.VMEM((count // depth, depth, half), w_down.dtype),
+            pltpu.SemaphoreType.DMA((count // depth,)),
+        )
+
     hidden, down_own = call(
         hidden_kernel,
         (pltpu.VMEM((rows, width), jnp.bfloat16), held),
@@ -304,20 +336,21 @@
         SMALL + rows * half * 24 + slots * half * tile * 4,
     )
     hidden_other = swap(hidden, "tp", 1)
-    part, down_other = call(
+    part = call(
         down_own_kernel,
-        (jax.ShapeDtypeStruct((rows, half), jnp.float32), held),
+        jax.ShapeDtypeStruct((rows, half), jnp.float32),
         [SMEM] + [VMEM] * 2 + [ANY],
         (where, in_vmem(hidden), in_vmem(down_own), in_hbm(w_down)),
-        (pltpu.SemaphoreType.DMA,),
-        small,
+        stream(width - early),
+        small + width * half * 2,
     )
     sent = call(
         down_other_kernel,
         jax.ShapeDtypeStruct((side_size, tok, half), jnp.bfloat16),
-        [SMEM] + [VMEM] * 4,
-        (where, hidden_other, part, gathered, in_vmem(down_other)),
-        limit=small,
+        [SMEM] + [VMEM] * 3 + [ANY],
+        (where, hidden_other, part, gathered, in_hbm(w_down)),
+        (pltpu.VMEM((rows, half), jnp.float32), *stream(width)),
+        small + width * half * 2,
     )
     received = lax.all_to_all(sent, "side", split_axis=0, concat_axis=0, tiled=True)
     return call(

time: 50.6 us -> 50.2 us (level)
  transfers between devices with their start and end apart: 2 -> 2, of which waited for: 1 -> 1; matrix products, arithmetic and copies ran while one was open for 0% -> 0% of each run, Pallas kernels for 10% -> 8%
where the time goes in v6:
time: 50.2 us; the launch traced here: 50 us
  Pallas kernels  24.2 us (48%)
  blocking collectives  24.2 us (48%)
  waiting for transfers between devices  1.31 us (3%)
    pallas_call x5, Pallas kernels, call(): pl.pallas_call(kernel, out_shape=out_shape, in_specs=in_specs, out_specs=...  24.2 us
    all_to_all x1, blocking collectives, per_device(): lax.all_to_all(local, 'side', split_axis=0, concat_axis=0, tiled=True)  14.5 us
    all_to_all x1, blocking collectives, per_device(): lax.all_to_all(sent, 'side', split_axis=0, concat_axis=0, tiled=True)  9.69 us
    ppermute x2, waiting for transfers between devices, swap(): return lax.ppermute(array, axis, [(i, i ^ mask) for i in range(size)])  1.31 us
  transfers between devices with their start and end apart: 2, of which 1 were waited for; matrix products, arithmetic and copies ran while one was open for 0% of the time, Pallas kernels for 8%

profile of v6, /device:TPU:0, one launch (start us, length us, event | category | flops | bytes accessed | tf_op | source)
XLA Modules:
  0.0 50.0 jit_solution(18091771834545528113)
XLA Ops:
  0.0 0.1 pad_add_fusion.refs_0_.where_ref
  0.1 0.0 copy-start
  0.1 0.0 copy-start.1
  0.1 2.3 %shard_map.118.carried_ref = bf16[8,4,1664]{2,1,0:T(4,128)(2,1)S(1)} custom-call(s32[2]{0:T(128)S(1)} %pad_add_fusion.refs_0_.where_ref, s32[2,2,2]{2,1,0:T(2,128)} %refs_1_.1, s32[2,2]{1,0:T(2,128)} %refs_2_.1, s32[2,2,2]{2,1,0:T(2,128)} %refs_3_.1, s32[2,2]{1,0:T(2,128)} %refs_4_.1, bf16[2,2,1536]{2,1,0:T(2,128)(2,1)} %refs_5_.1, ...), custom_call_target="tpu_custom_call" | custom-call | tf_op jit(solution)/shard_map/pallas_call | solution.py:251
  2.4 14.5 %all_to_all.10.own_ref.extra_ref = bf16[8,4,1664]{2,1,0:T(4,128)(2,1)S(1)} all-to-all(bf16[8,4,1664]{2,1,0:T(4,128)(2,1)S(1)} %shard_map.118.carried_ref), channel_id=1, replica_groups=mesh['groups'=2,'side'=8,'tp'=2] {'side'}, dimensions={0} | all-to-all | bytes 212992 | tf_op jit(solution)/shard_map/all_to_all | solution.py:310
  16.9 0.0 collective-permute-start
  16.9 1.3 %collective-permute-done.other_ref = bf16[8,4,1664]{2,1,0:T(4,128)(2,1)S(1)} collective-permute-done((bf16[8,4,1664]{2,1,0:T(4,128)(2,1)S(1)}, bf16[8,4,1664]{2,1,0:T(4,128)(2,1)S(1)}, u32[]{:S(2)}, u32[]{:S(2)}) %collective-permute-start) | collective-permute-done | bytes 106528 | tf_op jit(solution)/shard_map/ppermute | solution.py:271
  18.2 0.0 copy-done
  18.2 0.0 copy-done.1
  18.2 11.7 %shard_map.119 = (bf16[32,4096]{1,0:T(8,128)(2,1)S(1)}, bf16[2048,1536]{1,0:T(8,128)(2,1)S(1)}) custom-call(s32[2]{0:T(128)S(1)} %pad_add_fusion.refs_0_.where_ref, bf16[8,4,1664]{2,1,0:T(4,128)(2,1)S(1)} %all_to_all.10.own_ref.extra_ref, bf16[8,4,1664]{2,1,0:T(4,128)(2,1)S(1)} %collective-permute-done.other_ref, bf16[3072]{0:T(1024)(128)(2,1)S(1)} %copy-done.1, ...), custom_call_target="tpu_custom_call" | custom-call | tf_op jit(solution)/shard_map/pallas_call | solution.py:251
  29.9 0.2 collective-permute-start.1
  30.1 3.8 %shard_map.120.part_ref = f32[32,1536]{1,0:T(8,128)S(1)} custom-call(s32[2]{0:T(128)S(1)} %pad_add_fusion.refs_0_.where_ref, bf16[32,4096]{1,0:T(8,128)(2,1)S(1)} %get-tuple-element.7.hid_ref, bf16[2048,1536]{1,0:T(8,128)(2,1)S(1)} %get-tuple-element.8.held_ref, bf16[8192,1536]{1,0:T(8,128)(2,1)} %w_ref.3), custom_call_target="tpu_custom_call" | custom-call | tf_op jit(solution)/shard_map/pallas_call | solution.py:251
  33.9 0.0 collective-permute-done.1.hid_ref
  34.0 5.7 %shard_map.121 = bf16[8,4,1536]{2,1,0:T(4,128)(2,1)S(1)} custom-call(s32[2]{0:T(128)S(1)} %pad_add_fusion.refs_0_.where_ref, bf16[32,4096]{1,0:T(8,128)(2,1)S(1)} %collective-permute-done.1.hid_ref, f32[32,1536]{1,0:T(8,128)S(1)} %shard_map.120.part_ref, bf16[8,4,1664]{2,1,0:T(4,128)(2,1)S(1)} %all_to_all.10.own_ref.extra_ref, bf16[8192,1536]{1,0:T(8,128)(2,1)} %w_ref.3), custom_call_target="tpu_custom_call" | custom-call | tf_op jit(solution)/shard_map/pallas_call | solution.py:251
  39.7 9.7 %all_to_all.11.received_ref = bf16[8,4,1536]{2,1,0:T(4,128)(2,1)S(1)} all-to-all(bf16[8,4,1536]{2,1,0:T(4,128)(2,1)S(1)} %shard_map.121), channel_id=1, replica_groups=mesh['groups'=2,'side'=8,'tp'=2] {'side'}, dimensions={0} | all-to-all | bytes 196608 | tf_op jit(solution)/shard_map/all_to_all | solution.py:355
  49.4 0.6 %shard_map.122 = bf16[2,2,1536]{2,1,0:T(2,128)(2,1)} custom-call(bf16[8,4,1664]{2,1,0:T(4,128)(2,1)S(1)} %shard_map.118.carried_ref, bf16[8,4,1536]{2,1,0:T(4,128)(2,1)S(1)} %all_to_all.11.received_ref), custom_call_target="tpu_custom_call" | custom-call | tf_op jit(solution)/shard_map/pallas_call | solution.py:251
Async XLA Ops:
  0.1 18.2 %copy-start = (bf16[3072,4096]{1,0:T(8,128)(2,1)S(1)}, bf16[3072,4096]{1,0:T(8,128)(2,1)}, u32[]{:S(2)}) copy-start(bf16[3072,4096]{1,0:T(8,128)(2,1)} %wg_ref.1) | copy-start | bytes 75497472
  0.1 18.2 %copy-start.1 = (bf16[3072]{0:T(1024)(128)(2,1)S(1)}, bf16[3072]{0:T(1024)(128)(2,1)}, u32[]{:S(2)}) copy-start(bf16[3072]{0:T(1024)(128)(2,1)} %gain_ref.1) | copy-start | bytes 18436
  16.9 1.3 %collective-permute-start = (bf16[8,4,1664]{2,1,0:T(4,128)(2,1)S(1)}, bf16[8,4,1664]{2,1,0:T(4,128)(2,1)S(1)}, u32[]{:S(2)}, u32[]{:S(2)}) collective-permute-start(bf16[8,4,1664]{2,1,0:T(4,128)(2,1)S(1)} %all_to_all.10.own_ref.extra_ref), channel_id=1, source_target_pairs={{0,1},{1,0},{2,3},{3,2},{4,5},{5,4},{6,7},{7,6},{8,9},{9,8},{10,11... | collective-permute-start | bytes 319496 | tf_op jit(solution)/shard_map/ppermute | solution.py:271
  29.9 4.0 %collective-permute-start.1 = (bf16[32,4096]{1,0:T(8,128)(2,1)S(1)}, bf16[32,4096]{1,0:T(8,128)(2,1)S(1)}, u32[]{:S(2)}, u32[]{:S(2)}) collective-permute-start(bf16[32,4096]{1,0:T(8,128)(2,1)S(1)} %get-tuple-element.7.hid_ref), channel_id=1, source_target_pairs={{0,1},{1,0},{2,3},{3,2},{4,5},{5,4},{6,7},{7,6},{8,9},{9,8},{10,11... | collective-permute-start | bytes 786440 | tf_op jit(solution)/shard_map/ppermute | solution.py:271

commit v7 on v6

--- a/solution.py
+++ b/solution.py
@@ -13,7 +13,6 @@
 EPS = 1e-05
 GATE_ONE = 65536.0
 LANES = 128
-DOWN_TILES = 3
 SMALL = 2 << 20
 
 
@@ -139,17 +138,27 @@
     wu_ref,
     wd_ref,
     out_ref,
+    part_ref,
     down_ref,
     x_ref,
     gate_ref,
     buf_ref,
+    own_buf_ref,
     sem,
+    own_sem,
     down_sem,
 ):
     slots, _, tile = buf_ref.shape
     half = own_ref.shape[2] - LANES
     chunks = out_ref.shape[1] // tile
-    down = row_copy(wd_ref, where_ref[0] * out_ref.shape[1], down_ref, down_sem)
+    own_chunks, depth, _ = own_buf_ref.shape
+    own_ahead = own_chunks // 2
+    own_start = where_ref[0] * out_ref.shape[1]
+    other_start = (1 - where_ref[0]) * out_ref.shape[1]
+    down = row_copy(wd_ref, other_start, down_ref, down_sem)
+
+    def own_copy(idx):
+        return row_copy(wd_ref, own_start + idx * depth, own_buf_ref.at[idx], own_sem.at[idx])
 
     def columns(idx):
         return pl.ds(pl.multiple_of(idx * tile, tile), tile)
@@ -159,6 +168,7 @@
         return pltpu.make_async_copy(wu_ref.at[:, columns(idx)], buf_ref.at[slot], sem.at[slot])
 
     lax.fori_loop(0, slots, lambda idx, _: up_copy(idx).start(), None)
+    lax.fori_loop(0, own_ahead, lambda idx, _: own_copy(idx).start(), None)
     is_first = where_ref[0] == 0
     own = flat(own_ref)[:, :half]
     other = flat(other_ref)[:, :half]
@@ -192,34 +202,36 @@
 
         @pl.when(idx + slots == chunks)
         def _():
+            lax.fori_loop(own_ahead, own_chunks, lambda nth, _: own_copy(nth).start(), None)
             down.start()
 
     lax.fori_loop(0, chunks, up_step, None)
+    part_ref[...] = jnp.zeros_like(part_ref)
+
+    def own_step(idx, _):
+        own_copy(idx).wait()
+        at = pl.ds(pl.multiple_of(idx * depth, depth), depth)
+        part_ref[...] += jnp.dot(
+            out_ref[:, at], own_buf_ref[idx], preferred_element_type=jnp.float32
+        )
+
+    lax.fori_loop(0, own_chunks, own_step, None)
     down.wait()
 
 
-def down_own_kernel(where_ref, hid_ref, held_ref, w_ref, out_ref, buf_ref, sem):
-    held = held_ref.shape[0]
-    start = where_ref[0] * hid_ref.shape[1] + held
-    rest = add_rows(hid_ref, held, w_ref, out_ref, buf_ref, sem, start)
-    tile = out_ref.shape[1] // DOWN_TILES
+def down_other_kernel(
+    where_ref, hid_ref, part_ref, extra_ref, held_ref, w_ref, out_ref, total_ref, buf_ref, sem
+):
+    held, depth = held_ref.shape[0], buf_ref.shape[1]
+    start = (1 - where_ref[0]) * hid_ref.shape[1] + held
+    rest = add_rows(hid_ref, held, w_ref, total_ref, buf_ref, sem, start)
+    total_ref[...] = part_ref[...]
 
     def step(idx, _):
-        at = pl.ds(pl.multiple_of(idx * tile, tile), tile)
-        out_ref[:, at] = jnp.dot(
-            hid_ref[:, :held], held_ref[:, at], preferred_element_type=jnp.float32
-        )
-
-    lax.fori_loop(0, DOWN_TILES, step, None)
-    rest()
-
-
-def down_other_kernel(
-    where_ref, hid_ref, part_ref, extra_ref, w_ref, out_ref, total_ref, buf_ref, sem
-):
-    start = (1 - where_ref[0]) * hid_ref.shape[1]
-    rest = add_rows(hid_ref, 0, w_ref, total_ref, buf_ref, sem, start)
-    total_ref[...] = part_ref[...]
+        at = pl.ds(pl.multiple_of(idx * depth, depth), depth)
+        total_ref[...] += jnp.dot(hid_ref[:, at], held_ref[at, :], preferred_element_type=jnp.float32)
+
+    lax.fori_loop(0, held // depth, step, None)
     rest()
     total = total_ref[...]
     extra = flat(extra_ref)[:, -LANES:]
@@ -310,9 +322,9 @@
     gathered = lax.all_to_all(local, "side", split_axis=0, concat_axis=0, tiled=True)
     other = swap(gathered, "tp", 1)
     tile = math.gcd(width, 512)
-    slots = min(width // tile, 6)
-    early = width // 2
-    depth = math.gcd(width - early, 512)
+    slots = min(width // tile, 4)
+    early = width * 1 // 2
+    depth = math.gcd(width - early, early, 512)
     held = pltpu.VMEM((early, half), w_down.dtype)
 
     def stream(count):
@@ -321,35 +333,33 @@
             pltpu.SemaphoreType.DMA((count // depth,)),
         )
 
-    hidden, down_own = call(
+    hidden, part, down_other = call(
         hidden_kernel,
-        (pltpu.VMEM((rows, width), jnp.bfloat16), held),
+        (
+            pltpu.VMEM((rows, width), jnp.bfloat16),
+            pltpu.VMEM((rows, half), jnp.float32),
+            held,
+        ),
         [SMEM] + [VMEM] * 4 + [ANY] * 2,
         (where, in_vmem(gathered), in_vmem(other), norm_gain, in_vmem(w_gate), in_hbm(w_up), in_hbm(w_down)),
         (
             pltpu.VMEM((rows, 2 * half), jnp.bfloat16),
             pltpu.VMEM((rows, width), jnp.float32),
             pltpu.VMEM((slots, 2 * half, tile), jnp.bfloat16),
+            pltpu.VMEM((width // depth, depth, half), w_down.dtype),
             pltpu.SemaphoreType.DMA((slots,)),
+            pltpu.SemaphoreType.DMA((width // depth,)),
             pltpu.SemaphoreType.DMA,
         ),
-        SMALL + rows * half * 24 + slots * half * tile * 4,
+        SMALL + rows * half * 24 + slots * half * tile * 4 + width * half * 2,
     )
     hidden_other = swap(hidden, "tp", 1)
-    part = call(
-        down_own_kernel,
-        jax.ShapeDtypeStruct((rows, half), jnp.float32),
-        [SMEM] + [VMEM] * 2 + [ANY],
-        (where, in_vmem(hidden), in_vmem(down_own), in_hbm(w_down)),
-        stream(width - early),
-        small + width * half * 2,
-    )
     sent = call(
         down_other_kernel,
         jax.ShapeDtypeStruct((side_size, tok, half), jnp.bfloat16),
-        [SMEM] + [VMEM] * 3 + [ANY],
-        (where, hidden_other, part, gathered, in_hbm(w_down)),
-        (pltpu.VMEM((rows, half), jnp.float32), *stream(width)),
+        [SMEM] + [VMEM] * 4 + [ANY],
+        (where, hidden_other, in_vmem(part), gathered, in_vmem(down_other), in_hbm(w_down)),
+        (pltpu.VMEM((rows, half), jnp.float32), *stream(width - early)),
         small + width * half * 2,
     )
     received = lax.all_to_all(sent, "side", split_axis=0, concat_axis=0, tiled=True)

time: 50.2 us -> 49.8 us (level)
  Pallas kernels: 24.2 us -> 22.5 us
  waiting for transfers between devices: 1.31 us -> 2.69 us
    pallas_call x5 -> x4, Pallas kernels: 24.2 us -> 22.5 us  [call(): pl.pallas_call(kernel, out_shape=out_shape, in_specs=in_specs, out_specs=...]
    ppermute x2, waiting for transfers between devices: 1.31 us -> 2.69 us  [swap(): return lax.ppermute(array, axis, [(i, i ^ mask) for i in range(size)])]
  transfers between devices with their start and end apart: 2 -> 2, of which waited for: 1 -> 2; matrix products, arithmetic and copies ran while one was open for 0% -> 0% of each run, Pallas kernels for 8% -> 0%
where the time goes in v7:
time: 49.8 us; the launch traced here: 49.5 us
  blocking collectives  24 us (48%)
  Pallas kernels  22.5 us (45%)
  waiting for transfers between devices  2.69 us (5%)
    pallas_call x4, Pallas kernels, call(): pl.pallas_call(kernel, out_shape=out_shape, in_specs=in_specs, out_specs=...  22.5 us
    all_to_all x1, blocking collectives, per_device(): lax.all_to_all(local, 'side', split_axis=0, concat_axis=0, tiled=True)  14.5 us
    all_to_all x1, blocking collectives, per_device(): lax.all_to_all(sent, 'side', split_axis=0, concat_axis=0, tiled=True)  9.51 us
    ppermute x2, waiting for transfers between devices, swap(): return lax.ppermute(array, axis, [(i, i ^ mask) for i in range(size)])  2.69 us
  transfers between devices with their start and end apart: 2, of which 2 were waited for; matrix products, arithmetic and copies ran while one was open for 0% of the time, Pallas kernels for 0%

profile of v7, /device:TPU:0, one launch (start us, length us, event | category | flops | bytes accessed | tf_op | source)
XLA Modules:
  0.0 49.5 jit_solution(14500389920435222717)
XLA Ops:
  0.0 0.1 pad_add_fusion.refs_0_.where_ref
  0.1 0.0 copy-start.1
  0.1 0.0 copy-start
  0.1 2.3 %shard_map.118.carried_ref = bf16[8,4,1664]{2,1,0:T(4,128)(2,1)S(1)} custom-call(s32[2]{0:T(128)S(1)} %pad_add_fusion.refs_0_.where_ref, s32[2,2,2]{2,1,0:T(2,128)} %refs_1_.1, s32[2,2]{1,0:T(2,128)} %refs_2_.1, s32[2,2,2]{2,1,0:T(2,128)} %refs_3_.1, s32[2,2]{1,0:T(2,128)} %refs_4_.1, bf16[2,2,1536]{2,1,0:T(2,128)(2,1)} %refs_5_.1, ...), custom_call_target="tpu_custom_call" | custom-call | tf_op jit(solution)/shard_map/pallas_call | solution.py:263
  2.4 0.0 copy-done.1
  2.4 14.5 %all_to_all.10.own_ref.extra_ref = bf16[8,4,1664]{2,1,0:T(4,128)(2,1)S(1)} all-to-all(bf16[8,4,1664]{2,1,0:T(4,128)(2,1)S(1)} %shard_map.118.carried_ref), channel_id=1, replica_groups=mesh['groups'=2,'side'=8,'tp'=2] {'side'}, dimensions={0} | all-to-all | bytes 212992 | tf_op jit(solution)/shard_map/all_to_all | solution.py:322
  16.9 0.0 copy-start.2
  16.9 0.0 collective-permute-start
  16.9 1.3 %collective-permute-done.other_ref = bf16[8,4,1664]{2,1,0:T(4,128)(2,1)S(1)} collective-permute-done((bf16[8,4,1664]{2,1,0:T(4,128)(2,1)S(1)}, bf16[8,4,1664]{2,1,0:T(4,128)(2,1)S(1)}, u32[]{:S(2)}, u32[]{:S(2)}) %collective-permute-start) | collective-permute-done | bytes 106528 | tf_op jit(solution)/shard_map/ppermute | solution.py:283
  18.2 0.0 copy-done
  18.2 15.6 %shard_map.119 = (bf16[32,4096]{1,0:T(8,128)(2,1)S(1)}, f32[32,1536]{1,0:T(8,128)S(1)}, bf16[2048,1536]{1,0:T(8,128)(2,1)S(1)}) custom-call(s32[2]{0:T(128)} %copy-done.1, bf16[8,4,1664]{2,1,0:T(4,128)(2,1)S(1)} %all_to_all.10.own_ref.extra_ref, bf16[8,4,1664]{2,1,0:T(4,128)(2,1)S(1)} %collective-permute-done.other_ref, bf16[3072]{0:T(1024)(128)(2,1)} %gain_ref.1, ...), custom_call_target="tpu_custom_call" | custom-call | tf_op jit(solution)/shard_map/pallas_call | solution.py:263
  33.9 0.2 collective-permute-start.1
  34.1 1.4 %collective-permute-done.1.hid_ref = bf16[32,4096]{1,0:T(8,128)(2,1)S(1)} collective-permute-done((bf16[32,4096]{1,0:T(8,128)(2,1)S(1)}, bf16[32,4096]{1,0:T(8,128)(2,1)S(1)}, u32[]{:S(2)}, u32[]{:S(2)}) %collective-permute-start.1) | collective-permute-done | bytes 262176 | tf_op jit(solution)/shard_map/ppermute | solution.py:283
  35.5 0.0 copy-done.2
  35.5 3.9 %shard_map.120 = bf16[8,4,1536]{2,1,0:T(4,128)(2,1)S(1)} custom-call(s32[2]{0:T(128)S(1)} %copy-done.2, bf16[32,4096]{1,0:T(8,128)(2,1)S(1)} %collective-permute-done.1.hid_ref, f32[32,1536]{1,0:T(8,128)S(1)} %get-tuple-element.9.part_ref, bf16[8,4,1664]{2,1,0:T(4,128)(2,1)S(1)} %all_to_all.10.own_ref.extra_ref, ...), custom_call_target="tpu_custom_call" | custom-call | tf_op jit(solution)/shard_map/pallas_call | solution.py:263
  39.4 9.5 %all_to_all.11.received_ref = bf16[8,4,1536]{2,1,0:T(4,128)(2,1)S(1)} all-to-all(bf16[8,4,1536]{2,1,0:T(4,128)(2,1)S(1)} %shard_map.120), channel_id=1, replica_groups=mesh['groups'=2,'side'=8,'tp'=2] {'side'}, dimensions={0} | all-to-all | bytes 196608 | tf_op jit(solution)/shard_map/all_to_all | solution.py:365
  48.9 0.6 %shard_map.121 = bf16[2,2,1536]{2,1,0:T(2,128)(2,1)} custom-call(bf16[8,4,1664]{2,1,0:T(4,128)(2,1)S(1)} %shard_map.118.carried_ref, bf16[8,4,1536]{2,1,0:T(4,128)(2,1)S(1)} %all_to_all.11.received_ref), custom_call_target="tpu_custom_call" | custom-call | tf_op jit(solution)/shard_map/pallas_call | solution.py:263
Async XLA Ops:
  0.1 2.4 %copy-start.1 = (s32[2]{0:T(128)}, s32[2]{0:T(128)S(1)}, u32[]{:S(2)}) copy-start(s32[2]{0:T(128)S(1)} %pad_add_fusion.refs_0_.where_ref) | copy-start | bytes 28
  0.1 18.2 %copy-start = (bf16[3072,4096]{1,0:T(8,128)(2,1)S(1)}, bf16[3072,4096]{1,0:T(8,128)(2,1)}, u32[]{:S(2)}) copy-start(bf16[3072,4096]{1,0:T(8,128)(2,1)} %wg_ref.1) | copy-start | bytes 75497472
  16.9 18.6 %copy-start.2 = (s32[2]{0:T(128)S(1)}, s32[2]{0:T(128)}, u32[]{:S(2)}) copy-start(s32[2]{0:T(128)} %copy-done.1) | copy-start | bytes 28
  16.9 1.3 %collective-permute-start = (bf16[8,4,1664]{2,1,0:T(4,128)(2,1)S(1)}, bf16[8,4,1664]{2,1,0:T(4,128)(2,1)S(1)}, u32[]{:S(2)}, u32[]{:S(2)}) collective-permute-start(bf16[8,4,1664]{2,1,0:T(4,128)(2,1)S(1)} %all_to_all.10.own_ref.extra_ref), channel_id=1, source_target_pairs={{0,1},{1,0},{2,3},{3,2},{4,5},{5,4},{6,7},{7,6},{8,9},{9,8},{10,11... | collective-permute-start | bytes 319496 | tf_op jit(solution)/shard_map/ppermute | solution.py:283
  33.9 1.6 %collective-permute-start.1 = (bf16[32,4096]{1,0:T(8,128)(2,1)S(1)}, bf16[32,4096]{1,0:T(8,128)(2,1)S(1)}, u32[]{:S(2)}, u32[]{:S(2)}) collective-permute-start(bf16[32,4096]{1,0:T(8,128)(2,1)S(1)} %get-tuple-element.8), channel_id=1, source_target_pairs={{0,1},{1,0},{2,3},{3,2},{4,5},{5,4},{6,7},{7,6},{8,9},{9,8},{10,11... | collective-permute-start | bytes 786440 | tf_op jit(solution)/shard_map/ppermute | solution.py:283

commit v8 on v7

--- a/solution.py
+++ b/solution.py
@@ -109,7 +109,7 @@
 
 def row_copy(w_ref, start, out_ref, sem):
     depth = out_ref.shape[0]
-    start = pl.multiple_of(start, depth)
+    start = pl.multiple_of(start, math.gcd(depth, 512))
     return pltpu.make_async_copy(w_ref.at[pl.ds(start, depth), :], out_ref, sem)
 
 
@@ -181,12 +181,14 @@
     x_ref[:, :half] = (left * inv_rms * gain[:, :half]).astype(jnp.bfloat16)
     x_ref[:, half:] = (right * inv_rms * gain[:, half:]).astype(jnp.bfloat16)
 
+    wide = math.gcd(out_ref.shape[1], 2048)
+
     def gate_step(idx, _):
-        at = columns(idx)
+        at = pl.ds(pl.multiple_of(idx * wide, wide), wide)
         gate = jnp.dot(x_ref[...], wg_ref[:, at], preferred_element_type=jnp.float32)
         gate_ref[:, at] = gate / (1.0 + jnp.exp(-gate))
 
-    lax.fori_loop(0, chunks, gate_step, None)
+    lax.fori_loop(0, out_ref.shape[1] // wide, gate_step, None)
 
     def up_step(idx, _):
         up_copy(idx).wait()
@@ -325,6 +327,7 @@
     slots = min(width // tile, 4)
     early = width * 1 // 2
     depth = math.gcd(width - early, early, 512)
+    own_depth = math.gcd(width, 1024)
     held = pltpu.VMEM((early, half), w_down.dtype)
 
     def stream(count):
@@ -346,9 +349,9 @@
             pltpu.VMEM((rows, 2 * half), jnp.bfloat16),
             pltpu.VMEM((rows, width), jnp.float32),
             pltpu.VMEM((slots, 2 * half, tile), jnp.bfloat16),
-            pltpu.VMEM((width // depth, depth, half), w_down.dtype),
+            pltpu.VMEM((width // own_depth, own_depth, half), w_down.dtype),
             pltpu.SemaphoreType.DMA((slots,)),
-            pltpu.SemaphoreType.DMA((width // depth,)),
+            pltpu.SemaphoreType.DMA((width // own_depth,)),
             pltpu.SemaphoreType.DMA,
         ),
         SMALL + rows * half * 24 + slots * half * tile * 4 + width * half * 2,

time: 49.8 us -> 48.9 us (0.982)
  Pallas kernels: 22.5 us -> 21.6 us
    pallas_call x4, Pallas kernels: 22.5 us -> 21.6 us  [call(): pl.pallas_call(kernel, out_shape=out_shape, in_specs=in_specs, out_specs=...]
where the time goes in v8:
time: 48.9 us; the launch traced here: 48.6 us
  blocking collectives  24 us (49%)
  Pallas kernels  21.6 us (44%)
  waiting for transfers between devices  2.69 us (6%)
    pallas_call x4, Pallas kernels, call(): pl.pallas_call(kernel, out_shape=out_shape, in_specs=in_specs, out_specs=...  21.6 us
    all_to_all x1, blocking collectives, per_device(): lax.all_to_all(local, 'side', split_axis=0, concat_axis=0, tiled=True)  14.5 us
    all_to_all x1, blocking collectives, per_device(): lax.all_to_all(sent, 'side', split_axis=0, concat_axis=0, tiled=True)  9.51 us
    ppermute x2, waiting for transfers between devices, swap(): return lax.ppermute(array, axis, [(i, i ^ mask) for i in range(size)])  2.69 us
  transfers between devices with their start and end apart: 2, of which 2 were waited for; matrix products, arithmetic and copies ran while one was open for 0% of the time, Pallas kernels for 0%

profile of v8, /device:TPU:0, one launch (start us, length us, event | category | flops | bytes accessed | tf_op | source)
XLA Modules:
  0.0 48.6 jit_solution(15852778701655097391)
XLA Ops:
  0.0 0.1 pad_add_fusion.refs_0_.where_ref
  0.1 0.0 copy-start.1
  0.1 0.0 copy-start
  0.1 2.3 %shard_map.118.carried_ref = bf16[8,4,1664]{2,1,0:T(4,128)(2,1)S(1)} custom-call(s32[2]{0:T(128)S(1)} %pad_add_fusion.refs_0_.where_ref, s32[2,2,2]{2,1,0:T(2,128)} %refs_1_.1, s32[2,2]{1,0:T(2,128)} %refs_2_.1, s32[2,2,2]{2,1,0:T(2,128)} %refs_3_.1, s32[2,2]{1,0:T(2,128)} %refs_4_.1, bf16[2,2,1536]{2,1,0:T(2,128)(2,1)} %refs_5_.1, ...), custom_call_target="tpu_custom_call" | custom-call | tf_op jit(solution)/shard_map/pallas_call | solution.py:265
  2.4 0.0 copy-done.1
  2.4 14.5 %all_to_all.10.own_ref.extra_ref = bf16[8,4,1664]{2,1,0:T(4,128)(2,1)S(1)} all-to-all(bf16[8,4,1664]{2,1,0:T(4,128)(2,1)S(1)} %shard_map.118.carried_ref), channel_id=1, replica_groups=mesh['groups'=2,'side'=8,'tp'=2] {'side'}, dimensions={0} | all-to-all | bytes 212992 | tf_op jit(solution)/shard_map/all_to_all | solution.py:324
  16.9 0.0 copy-start.2
  16.9 0.0 collective-permute-start
  16.9 1.3 %collective-permute-done.other_ref = bf16[8,4,1664]{2,1,0:T(4,128)(2,1)S(1)} collective-permute-done((bf16[8,4,1664]{2,1,0:T(4,128)(2,1)S(1)}, bf16[8,4,1664]{2,1,0:T(4,128)(2,1)S(1)}, u32[]{:S(2)}, u32[]{:S(2)}) %collective-permute-start) | collective-permute-done | bytes 106528 | tf_op jit(solution)/shard_map/ppermute | solution.py:285
  18.2 0.0 copy-done
  18.2 14.7 %shard_map.119 = (bf16[32,4096]{1,0:T(8,128)(2,1)S(1)}, f32[32,1536]{1,0:T(8,128)S(1)}, bf16[2048,1536]{1,0:T(8,128)(2,1)S(1)}) custom-call(s32[2]{0:T(128)} %copy-done.1, bf16[8,4,1664]{2,1,0:T(4,128)(2,1)S(1)} %all_to_all.10.own_ref.extra_ref, bf16[8,4,1664]{2,1,0:T(4,128)(2,1)S(1)} %collective-permute-done.other_ref, bf16[3072]{0:T(1024)(128)(2,1)} %gain_ref.1, ...), custom_call_target="tpu_custom_call" | custom-call | tf_op jit(solution)/shard_map/pallas_call | solution.py:265
  33.0 0.2 collective-permute-start.1
  33.2 1.4 %collective-permute-done.1.hid_ref = bf16[32,4096]{1,0:T(8,128)(2,1)S(1)} collective-permute-done((bf16[32,4096]{1,0:T(8,128)(2,1)S(1)}, bf16[32,4096]{1,0:T(8,128)(2,1)S(1)}, u32[]{:S(2)}, u32[]{:S(2)}) %collective-permute-start.1) | collective-permute-done | bytes 262176 | tf_op jit(solution)/shard_map/ppermute | solution.py:285
  34.6 0.0 copy-done.2
  34.6 3.9 %shard_map.120 = bf16[8,4,1536]{2,1,0:T(4,128)(2,1)S(1)} custom-call(s32[2]{0:T(128)S(1)} %copy-done.2, bf16[32,4096]{1,0:T(8,128)(2,1)S(1)} %collective-permute-done.1.hid_ref, f32[32,1536]{1,0:T(8,128)S(1)} %get-tuple-element.9.part_ref, bf16[8,4,1664]{2,1,0:T(4,128)(2,1)S(1)} %all_to_all.10.own_ref.extra_ref, ...), custom_call_target="tpu_custom_call" | custom-call | tf_op jit(solution)/shard_map/pallas_call | solution.py:265
  38.5 9.5 %all_to_all.11.received_ref = bf16[8,4,1536]{2,1,0:T(4,128)(2,1)S(1)} all-to-all(bf16[8,4,1536]{2,1,0:T(4,128)(2,1)S(1)} %shard_map.120), channel_id=1, replica_groups=mesh['groups'=2,'side'=8,'tp'=2] {'side'}, dimensions={0} | all-to-all | bytes 196608 | tf_op jit(solution)/shard_map/all_to_all | solution.py:368
  48.0 0.6 %shard_map.121 = bf16[2,2,1536]{2,1,0:T(2,128)(2,1)} custom-call(bf16[8,4,1664]{2,1,0:T(4,128)(2,1)S(1)} %shard_map.118.carried_ref, bf16[8,4,1536]{2,1,0:T(4,128)(2,1)S(1)} %all_to_all.11.received_ref), custom_call_target="tpu_custom_call" | custom-call | tf_op jit(solution)/shard_map/pallas_call | solution.py:265
Async XLA Ops:
  0.1 2.4 %copy-start.1 = (s32[2]{0:T(128)}, s32[2]{0:T(128)S(1)}, u32[]{:S(2)}) copy-start(s32[2]{0:T(128)S(1)} %pad_add_fusion.refs_0_.where_ref) | copy-start | bytes 28
  0.1 18.2 %copy-start = (bf16[3072,4096]{1,0:T(8,128)(2,1)S(1)}, bf16[3072,4096]{1,0:T(8,128)(2,1)}, u32[]{:S(2)}) copy-start(bf16[3072,4096]{1,0:T(8,128)(2,1)} %wg_ref.1) | copy-start | bytes 75497472
  16.9 17.7 %copy-start.2 = (s32[2]{0:T(128)S(1)}, s32[2]{0:T(128)}, u32[]{:S(2)}) copy-start(s32[2]{0:T(128)} %copy-done.1) | copy-start | bytes 28
  16.9 1.3 %collective-permute-start = (bf16[8,4,1664]{2,1,0:T(4,128)(2,1)S(1)}, bf16[8,4,1664]{2,1,0:T(4,128)(2,1)S(1)}, u32[]{:S(2)}, u32[]{:S(2)}) collective-permute-start(bf16[8,4,1664]{2,1,0:T(4,128)(2,1)S(1)} %all_to_all.10.own_ref.extra_ref), channel_id=1, source_target_pairs={{0,1},{1,0},{2,3},{3,2},{4,5},{5,4},{6,7},{7,6},{8,9},{9,8},{10,11... | collective-permute-start | bytes 319496 | tf_op jit(solution)/shard_map/ppermute | solution.py:285
  33.0 1.6 %collective-permute-start.1 = (bf16[32,4096]{1,0:T(8,128)(2,1)S(1)}, bf16[32,4096]{1,0:T(8,128)(2,1)S(1)}, u32[]{:S(2)}, u32[]{:S(2)}) collective-permute-start(bf16[32,4096]{1,0:T(8,128)(2,1)S(1)} %get-tuple-element.8), channel_id=1, source_target_pairs={{0,1},{1,0},{2,3},{3,2},{4,5},{5,4},{6,7},{7,6},{8,9},{9,8},{10,11... | collective-permute-start | bytes 786440 | tf_op jit(solution)/shard_map/ppermute | solution.py:285

commit v9 on v8

--- a/solution.py
+++ b/solution.py
@@ -142,15 +142,16 @@
     down_ref,
     x_ref,
     gate_ref,
+    up_ref,
     buf_ref,
     own_buf_ref,
     sem,
     own_sem,
     down_sem,
 ):
-    slots, _, tile = buf_ref.shape
+    slots, deep, _ = buf_ref.shape
     half = own_ref.shape[2] - LANES
-    chunks = out_ref.shape[1] // tile
+    chunks = 2 * half // deep
     own_chunks, depth, _ = own_buf_ref.shape
     own_ahead = own_chunks // 2
     own_start = where_ref[0] * out_ref.shape[1]
@@ -160,12 +161,12 @@
     def own_copy(idx):
         return row_copy(wd_ref, own_start + idx * depth, own_buf_ref.at[idx], own_sem.at[idx])
 
-    def columns(idx):
-        return pl.ds(pl.multiple_of(idx * tile, tile), tile)
+    def lines(idx):
+        return pl.ds(pl.multiple_of(idx * deep, deep), deep)
 
     def up_copy(idx):
         slot = lax.rem(idx, slots)
-        return pltpu.make_async_copy(wu_ref.at[:, columns(idx)], buf_ref.at[slot], sem.at[slot])
+        return pltpu.make_async_copy(wu_ref.at[lines(idx), :], buf_ref.at[slot], sem.at[slot])
 
     lax.fori_loop(0, slots, lambda idx, _: up_copy(idx).start(), None)
     lax.fori_loop(0, own_ahead, lambda idx, _: own_copy(idx).start(), None)
@@ -190,13 +191,13 @@
 
     lax.fori_loop(0, out_ref.shape[1] // wide, gate_step, None)
 
+    up_ref[...] = jnp.zeros_like(up_ref)
+
     def up_step(idx, _):
         up_copy(idx).wait()
-        up = jnp.dot(
-            x_ref[...], buf_ref[lax.rem(idx, slots)], preferred_element_type=jnp.float32
-        )
-        at = columns(idx)
-        out_ref[:, at] = (gate_ref[:, at] * up).astype(jnp.bfloat16)
+        up_ref[...] += jnp.dot(
+            x_ref[:, lines(idx)], buf_ref[lax.rem(idx, slots)], preferred_element_type=jnp.float32
+        )
 
         @pl.when(idx + slots < chunks)
         def _():
@@ -208,6 +209,7 @@
             down.start()
 
     lax.fori_loop(0, chunks, up_step, None)
+    out_ref[...] = (gate_ref[...] * up_ref[...]).astype(jnp.bfloat16)
     part_ref[...] = jnp.zeros_like(part_ref)
 
     def own_step(idx, _):
@@ -323,8 +325,8 @@
     )
     gathered = lax.all_to_all(local, "side", split_axis=0, concat_axis=0, tiled=True)
     other = swap(gathered, "tp", 1)
-    tile = math.gcd(width, 512)
-    slots = min(width // tile, 4)
+    deep = math.gcd(2 * half, 256)
+    slots = 6
     early = width * 1 // 2
     depth = math.gcd(width - early, early, 512)
     own_depth = math.gcd(width, 1024)
@@ -348,13 +350,14 @@
         (
             pltpu.VMEM((rows, 2 * half), jnp.bfloat16),
             pltpu.VMEM((rows, width), jnp.float32),
-            pltpu.VMEM((slots, 2 * half, tile), jnp.bfloat16),
+            pltpu.VMEM((rows, width), jnp.float32),
+            pltpu.VMEM((slots, deep, width), jnp.bfloat16),
             pltpu.VMEM((width // own_depth, own_depth, half), w_down.dtype),
             pltpu.SemaphoreType.DMA((slots,)),
             pltpu.SemaphoreType.DMA((width // own_depth,)),
             pltpu.SemaphoreType.DMA,
         ),
-        SMALL + rows * half * 24 + slots * half * tile * 4 + width * half * 2,
+        SMALL + rows * half * 24 + slots * deep * width * 2 + rows * width * 4 + width * half * 2,
     )
     hidden_other = swap(hidden, "tp", 1)
     sent = call(

time: 48.9 us -> 48.8 us (level)
  no operation moved by 1% of the time
where the time goes in v9:
time: 48.8 us; the launch traced here: 48.5 us
  blocking collectives  24 us (49%)
  Pallas kernels  21.5 us (44%)
  waiting for transfers between devices  2.69 us (6%)
    pallas_call x4, Pallas kernels, call(): pl.pallas_call(kernel, out_shape=out_shape, in_specs=in_specs, out_specs=...  21.5 us
    all_to_all x1, blocking collectives, per_device(): lax.all_to_all(local, 'side', split_axis=0, concat_axis=0, tiled=True)  14.5 us
    all_to_all x1, blocking collectives, per_device(): lax.all_to_all(sent, 'side', split_axis=0, concat_axis=0, tiled=True)  9.51 us
    ppermute x2, waiting for transfers between devices, swap(): return lax.ppermute(array, axis, [(i, i ^ mask) for i in range(size)])  2.69 us
  transfers between devices with their start and end apart: 2, of which 2 were waited for; matrix products, arithmetic and copies ran while one was open for 0% of the time, Pallas kernels for 0%

profile of v9, /device:TPU:0, one launch (start us, length us, event | category | flops | bytes accessed | tf_op | source)
XLA Modules:
  0.0 48.5 jit_solution(556970837702543013)
XLA Ops:
  0.0 0.1 pad_add_fusion.refs_0_.where_ref
  0.1 0.0 copy-start.1
  0.1 0.0 copy-start
  0.1 2.3 %shard_map.118.carried_ref = bf16[8,4,1664]{2,1,0:T(4,128)(2,1)S(1)} custom-call(s32[2]{0:T(128)S(1)} %pad_add_fusion.refs_0_.where_ref, s32[2,2,2]{2,1,0:T(2,128)} %refs_1_.1, s32[2,2]{1,0:T(2,128)} %refs_2_.1, s32[2,2,2]{2,1,0:T(2,128)} %refs_3_.1, s32[2,2]{1,0:T(2,128)} %refs_4_.1, bf16[2,2,1536]{2,1,0:T(2,128)(2,1)} %refs_5_.1, ...), custom_call_target="tpu_custom_call" | custom-call | tf_op jit(solution)/shard_map/pallas_call | solution.py:267
  2.4 0.0 copy-done.1
  2.4 14.5 %all_to_all.10.own_ref.extra_ref = bf16[8,4,1664]{2,1,0:T(4,128)(2,1)S(1)} all-to-all(bf16[8,4,1664]{2,1,0:T(4,128)(2,1)S(1)} %shard_map.118.carried_ref), channel_id=1, replica_groups=mesh['groups'=2,'side'=8,'tp'=2] {'side'}, dimensions={0} | all-to-all | bytes 212992 | tf_op jit(solution)/shard_map/all_to_all | solution.py:326
  16.9 0.0 copy-start.2
  16.9 0.0 collective-permute-start
  16.9 1.3 %collective-permute-done.other_ref = bf16[8,4,1664]{2,1,0:T(4,128)(2,1)S(1)} collective-permute-done((bf16[8,4,1664]{2,1,0:T(4,128)(2,1)S(1)}, bf16[8,4,1664]{2,1,0:T(4,128)(2,1)S(1)}, u32[]{:S(2)}, u32[]{:S(2)}) %collective-permute-start) | collective-permute-done | bytes 106528 | tf_op jit(solution)/shard_map/ppermute | solution.py:287
  18.2 0.0 copy-done
  18.2 14.6 %shard_map.119 = (bf16[32,4096]{1,0:T(8,128)(2,1)S(1)}, f32[32,1536]{1,0:T(8,128)S(1)}, bf16[2048,1536]{1,0:T(8,128)(2,1)S(1)}) custom-call(s32[2]{0:T(128)} %copy-done.1, bf16[8,4,1664]{2,1,0:T(4,128)(2,1)S(1)} %all_to_all.10.own_ref.extra_ref, bf16[8,4,1664]{2,1,0:T(4,128)(2,1)S(1)} %collective-permute-done.other_ref, bf16[3072]{0:T(1024)(128)(2,1)} %gain_ref.1, ...), custom_call_target="tpu_custom_call" | custom-call | tf_op jit(solution)/shard_map/pallas_call | solution.py:267
  32.9 0.2 collective-permute-start.1
  33.1 1.4 %collective-permute-done.1.hid_ref = bf16[32,4096]{1,0:T(8,128)(2,1)S(1)} collective-permute-done((bf16[32,4096]{1,0:T(8,128)(2,1)S(1)}, bf16[32,4096]{1,0:T(8,128)(2,1)S(1)}, u32[]{:S(2)}, u32[]{:S(2)}) %collective-permute-start.1) | collective-permute-done | bytes 262176 | tf_op jit(solution)/shard_map/ppermute | solution.py:287
  34.5 0.0 copy-done.2
  34.5 3.9 %shard_map.120 = bf16[8,4,1536]{2,1,0:T(4,128)(2,1)S(1)} custom-call(s32[2]{0:T(128)S(1)} %copy-done.2, bf16[32,4096]{1,0:T(8,128)(2,1)S(1)} %collective-permute-done.1.hid_ref, f32[32,1536]{1,0:T(8,128)S(1)} %get-tuple-element.9.part_ref, bf16[8,4,1664]{2,1,0:T(4,128)(2,1)S(1)} %all_to_all.10.own_ref.extra_ref, ...), custom_call_target="tpu_custom_call" | custom-call | tf_op jit(solution)/shard_map/pallas_call | solution.py:267
  38.4 9.5 %all_to_all.11.received_ref = bf16[8,4,1536]{2,1,0:T(4,128)(2,1)S(1)} all-to-all(bf16[8,4,1536]{2,1,0:T(4,128)(2,1)S(1)} %shard_map.120), channel_id=1, replica_groups=mesh['groups'=2,'side'=8,'tp'=2] {'side'}, dimensions={0} | all-to-all | bytes 196608 | tf_op jit(solution)/shard_map/all_to_all | solution.py:371
  47.9 0.6 %shard_map.121 = bf16[2,2,1536]{2,1,0:T(2,128)(2,1)} custom-call(bf16[8,4,1664]{2,1,0:T(4,128)(2,1)S(1)} %shard_map.118.carried_ref, bf16[8,4,1536]{2,1,0:T(4,128)(2,1)S(1)} %all_to_all.11.received_ref), custom_call_target="tpu_custom_call" | custom-call | tf_op jit(solution)/shard_map/pallas_call | solution.py:267
Async XLA Ops:
  0.1 2.4 %copy-start.1 = (s32[2]{0:T(128)}, s32[2]{0:T(128)S(1)}, u32[]{:S(2)}) copy-start(s32[2]{0:T(128)S(1)} %pad_add_fusion.refs_0_.where_ref) | copy-start | bytes 28
  0.1 18.2 %copy-start = (bf16[3072,4096]{1,0:T(8,128)(2,1)S(1)}, bf16[3072,4096]{1,0:T(8,128)(2,1)}, u32[]{:S(2)}) copy-start(bf16[3072,4096]{1,0:T(8,128)(2,1)} %wg_ref.1) | copy-start | bytes 75497472
  16.9 17.6 %copy-start.2 = (s32[2]{0:T(128)S(1)}, s32[2]{0:T(128)}, u32[]{:S(2)}) copy-start(s32[2]{0:T(128)} %copy-done.1) | copy-start | bytes 28
  16.9 1.3 %collective-permute-start = (bf16[8,4,1664]{2,1,0:T(4,128)(2,1)S(1)}, bf16[8,4,1664]{2,1,0:T(4,128)(2,1)S(1)}, u32[]{:S(2)}, u32[]{:S(2)}) collective-permute-start(bf16[8,4,1664]{2,1,0:T(4,128)(2,1)S(1)} %all_to_all.10.own_ref.extra_ref), channel_id=1, source_target_pairs={{0,1},{1,0},{2,3},{3,2},{4,5},{5,4},{6,7},{7,6},{8,9},{9,8},{10,11... | collective-permute-start | bytes 319496 | tf_op jit(solution)/shard_map/ppermute | solution.py:287
  32.9 1.6 %collective-permute-start.1 = (bf16[32,4096]{1,0:T(8,128)(2,1)S(1)}, bf16[32,4096]{1,0:T(8,128)(2,1)S(1)}, u32[]{:S(2)}, u32[]{:S(2)}) collective-permute-start(bf16[32,4096]{1,0:T(8,128)(2,1)S(1)} %get-tuple-element.8), channel_id=1, source_target_pairs={{0,1},{1,0},{2,3},{3,2},{4,5},{5,4},{6,7},{7,6},{8,9},{9,8},{10,11... | collective-permute-start | bytes 786440 | tf_op jit(solution)/shard_map/ppermute | solution.py:287

commit v10 on v9

--- a/solution.py
+++ b/solution.py
@@ -226,16 +226,12 @@
 def down_other_kernel(
     where_ref, hid_ref, part_ref, extra_ref, held_ref, w_ref, out_ref, total_ref, buf_ref, sem
 ):
-    held, depth = held_ref.shape[0], buf_ref.shape[1]
+    held = held_ref.shape[0]
     start = (1 - where_ref[0]) * hid_ref.shape[1] + held
     rest = add_rows(hid_ref, held, w_ref, total_ref, buf_ref, sem, start)
-    total_ref[...] = part_ref[...]
-
-    def step(idx, _):
-        at = pl.ds(pl.multiple_of(idx * depth, depth), depth)
-        total_ref[...] += jnp.dot(hid_ref[:, at], held_ref[at, :], preferred_element_type=jnp.float32)
-
-    lax.fori_loop(0, held // depth, step, None)
+    total_ref[...] = part_ref[...] + jnp.dot(
+        hid_ref[:, :held], held_ref[...], preferred_element_type=jnp.float32
+    )
     rest()
     total = total_ref[...]
     extra = flat(extra_ref)[:, -LANES:]

time: 48.8 us -> 48.8 us (level)
  no operation moved by 1% of the time
where the time goes in v10:
time: 48.8 us; the launch traced here: 48.5 us
  blocking collectives  24 us (49%)
  Pallas kernels  21.5 us (44%)
  waiting for transfers between devices  2.69 us (6%)
    pallas_call x4, Pallas kernels, call(): pl.pallas_call(kernel, out_shape=out_shape, in_specs=in_specs, out_specs=...  21.5 us
    all_to_all x1, blocking collectives, per_device(): lax.all_to_all(local, 'side', split_axis=0, concat_axis=0, tiled=True)  14.5 us
    all_to_all x1, blocking collectives, per_device(): lax.all_to_all(sent, 'side', split_axis=0, concat_axis=0, tiled=True)  9.51 us
    ppermute x2, waiting for transfers between devices, swap(): return lax.ppermute(array, axis, [(i, i ^ mask) for i in range(size)])  2.69 us
  transfers between devices with their start and end apart: 2, of which 2 were waited for; matrix products, arithmetic and copies ran while one was open for 0% of the time, Pallas kernels for 0%

profile of v10, /device:TPU:0, one launch (start us, length us, event | category | flops | bytes accessed | tf_op | source)
XLA Modules:
  0.0 48.5 jit_solution(1862370926069825815)
XLA Ops:
  0.0 0.1 pad_add_fusion.refs_0_.where_ref
  0.1 0.0 copy-start.1
  0.1 0.0 copy-start
  0.1 2.3 %shard_map.118.carried_ref = bf16[8,4,1664]{2,1,0:T(4,128)(2,1)S(1)} custom-call(s32[2]{0:T(128)S(1)} %pad_add_fusion.refs_0_.where_ref, s32[2,2,2]{2,1,0:T(2,128)} %refs_1_.1, s32[2,2]{1,0:T(2,128)} %refs_2_.1, s32[2,2,2]{2,1,0:T(2,128)} %refs_3_.1, s32[2,2]{1,0:T(2,128)} %refs_4_.1, bf16[2,2,1536]{2,1,0:T(2,128)(2,1)} %refs_5_.1, ...), custom_call_target="tpu_custom_call" | custom-call | tf_op jit(solution)/shard_map/pallas_call | solution.py:263
  2.4 0.0 copy-done.1
  2.4 14.5 %all_to_all.10.own_ref.extra_ref = bf16[8,4,1664]{2,1,0:T(4,128)(2,1)S(1)} all-to-all(bf16[8,4,1664]{2,1,0:T(4,128)(2,1)S(1)} %shard_map.118.carried_ref), channel_id=1, replica_groups=mesh['groups'=2,'side'=8,'tp'=2] {'side'}, dimensions={0} | all-to-all | bytes 212992 | tf_op jit(solution)/shard_map/all_to_all | solution.py:322
  16.9 0.0 copy-start.2
  16.9 0.0 collective-permute-start
  16.9 1.3 %collective-permute-done.other_ref = bf16[8,4,1664]{2,1,0:T(4,128)(2,1)S(1)} collective-permute-done((bf16[8,4,1664]{2,1,0:T(4,128)(2,1)S(1)}, bf16[8,4,1664]{2,1,0:T(4,128)(2,1)S(1)}, u32[]{:S(2)}, u32[]{:S(2)}) %collective-permute-start) | collective-permute-done | bytes 106528 | tf_op jit(solution)/shard_map/ppermute | solution.py:283
  18.2 0.0 copy-done
  18.2 14.6 %shard_map.119 = (bf16[32,4096]{1,0:T(8,128)(2,1)S(1)}, f32[32,1536]{1,0:T(8,128)S(1)}, bf16[2048,1536]{1,0:T(8,128)(2,1)S(1)}) custom-call(s32[2]{0:T(128)} %copy-done.1, bf16[8,4,1664]{2,1,0:T(4,128)(2,1)S(1)} %all_to_all.10.own_ref.extra_ref, bf16[8,4,1664]{2,1,0:T(4,128)(2,1)S(1)} %collective-permute-done.other_ref, bf16[3072]{0:T(1024)(128)(2,1)} %gain_ref.1, ...), custom_call_target="tpu_custom_call" | custom-call | tf_op jit(solution)/shard_map/pallas_call | solution.py:263
  32.9 0.2 collective-permute-start.1
  33.1 1.4 %collective-permute-done.1.hid_ref = bf16[32,4096]{1,0:T(8,128)(2,1)S(1)} collective-permute-done((bf16[32,4096]{1,0:T(8,128)(2,1)S(1)}, bf16[32,4096]{1,0:T(8,128)(2,1)S(1)}, u32[]{:S(2)}, u32[]{:S(2)}) %collective-permute-start.1) | collective-permute-done | bytes 262176 | tf_op jit(solution)/shard_map/ppermute | solution.py:283
  34.5 0.0 copy-done.2
  34.5 3.9 %shard_map.120 = bf16[8,4,1536]{2,1,0:T(4,128)(2,1)S(1)} custom-call(s32[2]{0:T(128)S(1)} %copy-done.2, bf16[32,4096]{1,0:T(8,128)(2,1)S(1)} %collective-permute-done.1.hid_ref, f32[32,1536]{1,0:T(8,128)S(1)} %get-tuple-element.9.part_ref, bf16[8,4,1664]{2,1,0:T(4,128)(2,1)S(1)} %all_to_all.10.own_ref.extra_ref, ...), custom_call_target="tpu_custom_call" | custom-call | tf_op jit(solution)/shard_map/pallas_call | solution.py:263
  38.4 9.5 %all_to_all.11.received_ref = bf16[8,4,1536]{2,1,0:T(4,128)(2,1)S(1)} all-to-all(bf16[8,4,1536]{2,1,0:T(4,128)(2,1)S(1)} %shard_map.120), channel_id=1, replica_groups=mesh['groups'=2,'side'=8,'tp'=2] {'side'}, dimensions={0} | all-to-all | bytes 196608 | tf_op jit(solution)/shard_map/all_to_all | solution.py:367
  47.9 0.6 %shard_map.121 = bf16[2,2,1536]{2,1,0:T(2,128)(2,1)} custom-call(bf16[8,4,1664]{2,1,0:T(4,128)(2,1)S(1)} %shard_map.118.carried_ref, bf16[8,4,1536]{2,1,0:T(4,128)(2,1)S(1)} %all_to_all.11.received_ref), custom_call_target="tpu_custom_call" | custom-call | tf_op jit(solution)/shard_map/pallas_call | solution.py:263
Async XLA Ops:
  0.1 2.4 %copy-start.1 = (s32[2]{0:T(128)}, s32[2]{0:T(128)S(1)}, u32[]{:S(2)}) copy-start(s32[2]{0:T(128)S(1)} %pad_add_fusion.refs_0_.where_ref) | copy-start | bytes 28
  0.1 18.2 %copy-start = (bf16[3072,4096]{1,0:T(8,128)(2,1)S(1)}, bf16[3072,4096]{1,0:T(8,128)(2,1)}, u32[]{:S(2)}) copy-start(bf16[3072,4096]{1,0:T(8,128)(2,1)} %wg_ref.1) | copy-start | bytes 75497472
  16.9 17.6 %copy-start.2 = (s32[2]{0:T(128)S(1)}, s32[2]{0:T(128)}, u32[]{:S(2)}) copy-start(s32[2]{0:T(128)} %copy-done.1) | copy-start | bytes 28
  16.9 1.3 %collective-permute-start = (bf16[8,4,1664]{2,1,0:T(4,128)(2,1)S(1)}, bf16[8,4,1664]{2,1,0:T(4,128)(2,1)S(1)}, u32[]{:S(2)}, u32[]{:S(2)}) collective-permute-start(bf16[8,4,1664]{2,1,0:T(4,128)(2,1)S(1)} %all_to_all.10.own_ref.extra_ref), channel_id=1, source_target_pairs={{0,1},{1,0},{2,3},{3,2},{4,5},{5,4},{6,7},{7,6},{8,9},{9,8},{10,11... | collective-permute-start | bytes 319496 | tf_op jit(solution)/shard_map/ppermute | solution.py:283
  32.9 1.6 %collective-permute-start.1 = (bf16[32,4096]{1,0:T(8,128)(2,1)S(1)}, bf16[32,4096]{1,0:T(8,128)(2,1)S(1)}, u32[]{:S(2)}, u32[]{:S(2)}) collective-permute-start(bf16[32,4096]{1,0:T(8,128)(2,1)S(1)} %get-tuple-element.8), channel_id=1, source_target_pairs={{0,1},{1,0},{2,3},{3,2},{4,5},{5,4},{6,7},{7,6},{8,9},{9,8},{10,11... | collective-permute-start | bytes 786440 | tf_op jit(solution)/shard_map/ppermute | solution.py:283
